TPU v7x, 128 devices: a whole 4x4x4 slice. The times are simulated.
128 devices in a mesh: tm: 8 (over y, core), seq: 16 (over x, z).
Axes of the slice: x: 4, y: 4, z: 4, core: 2. Of those that a mesh axis runs over, the one named last changes fastest.
Arguments:
- queries: bfloat16 [8, 4096, 2048], P('tm', 'seq'), may hold values from -6 to 6
- keys: bfloat16 [8, 4480, 2048], P('tm', 'seq'), may hold values from -6 to 6
- values: bfloat16 [8, 4480, 2048], P('tm', 'seq'), may hold values from -6 to 6
- hidden: bfloat16 [8, 4096, 2432], P('tm', 'seq'), may hold values from -0.119628906 to 0.119628906
- w_proj: bfloat16 [2048, 2432], replicated, may hold values from -0.125 to 0.125
- w_final: bfloat16 [2432, 64], replicated, may hold values from -0.125 to 0.125
- gate_base: float32 [2432], replicated, may hold values from -6 to 6
- gate_slope: float32 [2432], replicated, may hold values from -6 to 6
- start_latent: float32 [4096, 64], P('seq'), may hold values from -6 to 6
- window_steps: int32 [9], replicated, may hold values from 0 to 16, as said below
Outputs:
- velocity: float32 [8, 4096, 64], P('tm', 'seq')
- latents: float32 [8, 4096, 64], P('tm', 'seq')
Inputs may be any that keep to these rules, and one draw needn't show every extreme that they name: window_steps[0] is 0, the last entry is 16, and each entry exceeds the one before by 1 to 3.
All inputs are finite; a program needn't handle non-finite values.
Results may differ from a plain program's by a relative error of at most 0.0059.
Values may be sent and summed in bfloat16 or wider, within the bound.
No kernel may reach another device: no remote copies, remote signals or barrier semaphores. Data moves between devices by JAX's collectives and lax.ppermute only.
A program may use at most 192 MiB of HBM per device.

v0:
```python
import jax
import jax.numpy as jnp
from jax import lax
from jax.sharding import PartitionSpec as P

HEADS = 32
HEAD_DIM = 64
HD = 2048


def entering(value, axis, combine, identity):
    peers, mine = (lax.axis_size(axis), lax.axis_index(axis))
    everything = lax.all_gather(value.astype(jnp.bfloat16), axis)
    start = jnp.broadcast_to(jnp.asarray(identity, value.dtype), value.shape)

    def lap(k, before):
        reached = k < mine
        new = combine(before, everything[k].astype(value.dtype))
        return jnp.where(reached, new, before)

    return lax.fori_loop(0, peers, lap, start)


def head_norm(tensor_in):
    count = tensor_in.shape[0]
    values_f = tensor_in.astype(jnp.float32).reshape(count, HEADS, HEAD_DIM)
    scaled = values_f * lax.rsqrt(jnp.mean(values_f * values_f, axis=-1, keepdims=True) + 1e-06)
    return scaled.astype(jnp.bfloat16)


def sigma_of(index_val, total_steps):
    frac = 1.0 - index_val.astype(jnp.float32) / total_steps
    return 3.0 * frac / (1.0 + 2.0 * frac)


def split_heads(flat_rows):
    return flat_rows.reshape(flat_rows.shape[0], -1, HEAD_DIM).transpose(1, 0, 2)


def head_terms(operands):
    query_head, key_head, value_head = operands
    scores = jnp.dot(query_head, key_head.T, preferred_element_type=jnp.float32) * 0.125
    weights = jnp.exp(scores)
    totals = jnp.sum(weights, axis=1)
    summed = jnp.dot(weights.astype(jnp.bfloat16), value_head, preferred_element_type=jnp.float32)
    return (summed, totals)


def add_drift(earlier, later):
    return earlier + later


def per_device(
    queries,
    keys,
    values,
    hidden,
    w_proj,
    w_final,
    gate_base,
    gate_slope,
    start_latent,
    window_steps,
):
    time_slot = lax.axis_index("tm")
    total_steps = 2 * lax.axis_size("tm")
    sigma_now = sigma_of(window_steps[time_slot], total_steps)
    step_size = sigma_of(window_steps[time_slot + 1], total_steps) - sigma_now
    query_rows = queries[0].shape[0]
    query_flat = head_norm(queries[0]).reshape(query_rows, HD)
    key_flat = head_norm(keys[0]).reshape(keys[0].shape[0], HD)
    value_flat = values[0]
    query_heads = split_heads(query_flat)
    key_piece = lax.all_gather(key_flat, "seq", axis=0, tiled=True)
    value_piece = lax.all_gather(value_flat, "seq", axis=0, tiled=True)
    summed, totals = lax.map(
        head_terms, (query_heads, split_heads(key_piece), split_heads(value_piece))
    )
    summed, totals = (summed, totals)
    attended = (summed / totals[:, :, None]).transpose(1, 0, 2).reshape(query_rows, HD)
    attended = attended.astype(jnp.bfloat16)
    projected = jnp.dot(attended, w_proj, preferred_element_type=jnp.float32)
    gated = hidden[0].astype(jnp.float32) + (gate_base + sigma_now * gate_slope) * projected
    normed = (gated * lax.rsqrt(jnp.mean(gated * gated, axis=-1, keepdims=True) + 1e-06)).astype(
        jnp.bfloat16
    )
    velocity = jnp.dot(normed, w_final, preferred_element_type=jnp.float32)
    drift = step_size * velocity
    earlier = entering(drift, "tm", add_drift, jnp.zeros_like(drift))
    latents = start_latent + earlier + drift
    return (velocity[None], latents[None])


def solution(mesh):
    placed = (
        P("tm", "seq", None),
        P("tm", "seq", None),
        P("tm", "seq", None),
        P("tm", "seq", None),
        P(),
        P(),
        P(),
        P(),
        P("seq", None),
        P(),
    )
    return jax.shard_map(
        per_device,
        mesh=mesh,
        in_specs=placed,
        out_specs=(P("tm", "seq", None), P("tm", "seq", None)),
        check_vma=False,
    )
```

profile of v0, /device:TPU:0, one launch (start us, length us, event | category | flops | bytes accessed | tf_op | source)
XLA Modules:
  0.0 460.0 jit_solution(4255130291157947061)
XLA Ops:
  10.9 2.2 reduce_sum.37
  19.1 118.1 %all-gather.5.cloned.1.call-done = bf16[4480,2048]{1,0:T(8,128)(2,1)} async-done(((bf16[280,2048]{1,0:T(8,128)(2,1)}), bf16[4480,2048]{1,0:T(8,128)(2,1)}) %all-gather.5.cloned.1.call-update) | async-done | bytes 18350096 | tf_op jit(solution)/shard_map/all_gather | solution.py:74
  137.1 24.5 %copy.25 = bf16[4480,2048]{0,1:T(8,128)(2,1)} copy(bf16[4480,2048]{1,0:T(8,128)(2,1)} %all-gather.5.cloned.1.call-done) | data formatting | bytes 36700160 | tf_op jit(solution)/shard_map/all_gather | solution.py:74
  161.6 96.8 %all-gather.7.cloned.1.call-done = bf16[1,4480,2048]{2,1,0:T(8,128)(2,1)} async-done(((bf16[1,280,2048]{2,1,0:T(8,128)(2,1)}), bf16[1,4480,2048]{2,1,0:T(8,128)(2,1)}) %all-gather.7.cloned.1.call-update) | async-done | bytes 18350096 | tf_op jit(solution)/shard_map/all_gather | solution.py:75
  258.4 23.8 %copy.26 = bf16[1,4480,2048]{1,2,0:T(8,128)(2,1)} copy(bf16[1,4480,2048]{2,1,0:T(8,128)(2,1)} %all-gather.7.cloned.1.call-done) | data formatting | bytes 36700160 | tf_op jit(solution)/shard_map/all_gather | solution.py:75
  282.3 147.6 %while.26 = (s32[]{:T(128)}, f32[32,256,64]{1,2,0:T(8,128)}, f32[32,256]{1,0:T(8,128)S(1)}, bf16[32,256,64]{1,2,0:T(8,128)(2,1)S(1)}, bf16[32,4480,64]{1,2,0:T(8...) while((s32[]{:T(128)}, f32[32,256,64]{1,2,0:T(8,128)}, f32[32,256]{1,0:T(8,128)S(1)}, ...), condition=%wide.region_4.5_spmd, body=%wide.region_2.4_spmd.sunk | while | flops 297041664 | bytes 5837913 | solution.py:76
  284.3 2.5 fusion.38
  288.9 2.5 fusion.38
  293.5 2.5 fusion.38
  298.2 2.5 fusion.38
  300.7 2.1 fusion.37
  302.8 2.5 fusion.38
  307.4 2.5 fusion.38
  312.0 2.5 fusion.38
  316.6 2.5 fusion.38
  321.2 2.5 fusion.38
  323.8 2.1 fusion.37
  325.8 2.5 fusion.38
  330.4 2.5 fusion.38
  335.0 2.5 fusion.38
  337.6 2.1 fusion.37
  339.6 2.5 fusion.38
  342.2 2.1 fusion.37
  344.3 2.5 fusion.38
  346.8 2.1 fusion.37
  348.9 2.5 fusion.38
  353.5 2.5 fusion.38
  358.1 2.5 fusion.38
  362.7 2.5 fusion.38
  365.3 2.1 fusion.37
  367.3 2.5 fusion.38
  371.9 2.5 fusion.38
  376.5 2.5 fusion.38
  381.2 2.5 fusion.38
  385.8 2.5 fusion.38
  390.4 2.5 fusion.38
  395.0 2.5 fusion.38
  397.5 2.1 fusion.37
  399.6 2.5 fusion.38
  404.2 2.5 fusion.38
  408.8 2.5 fusion.38
  413.4 2.5 fusion.38
  418.1 2.5 fusion.38
  420.6 2.1 fusion.37
  422.7 2.5 fusion.38
  427.3 2.5 fusion.38
  431.8 5.9 %multiply_reduce_fusion = (f32[256]{0:T(256)S(1)}, f32[256,2432]{1,0:T(8,128)S(1)}) fusion(bf16[256,2048]{0,1:T(8,128)(2,1)S(1)} %bitcast.78, bf16[2048,2432]{1,0:T(8,128)(2,1)} %param.18, f32[2432]{0:T(1024)S(1)} %multiply_add_fusion, bf16[1,256,2432]{2,1,0:T(8,128)(2,1)S(1)} %copy-done.1), kind=kOutput, calls=%fused_computation.24 | convolution fusion | flops 2553249536 | bytes 14756352 | tf_op jit(solution)/shard_map/dot_general | solution.py:82
  438.4 13.2 %all-gather.1 = bf16[2048,64]{0,1:T(8,128)(2,1)S(1)} all-gather(bf16[256,64]{0,1:T(8,128)(2,1)S(1)} %get-tuple-element.182), channel_id=3, replica_groups=mesh['tm'=8,'seq'=16] {'tm'}, dimensions={0}, use_global_device_ids=true | all-gather | bytes 294912 | tf_op jit(solution)/shard_map/all_gather | solution.py:13
  (105 shorter events, 62.6 us)
Async XLA Ops:
  7.2 430.6 %copy-start = (bf16[2432,64]{0,1:T(8,128)(2,1)S(1)}, bf16[2432,64]{0,1:T(8,128)(2,1)}, u32[]{:S(2)}) copy-start(bf16[2432,64]{0,1:T(8,128)(2,1)} %param.19) | copy-start | bytes 933892
  7.2 129.9 %all-gather.5.cloned.1.call-start = ((), (), s32[]{:S(2)}) async-start(), calls=%async_computation | async-start | bytes 19496960 | tf_op jit(solution)/shard_map/all_gather | solution.py:74
  13.4 2.3 copy-start.7
  15.0 2.9 copy-start.2
  15.0 3.8 copy-start.5
  15.0 3.8 copy-start.6
  15.0 243.4 %all-gather.7.cloned.1.call-start = ((), (), s32[]{:S(2)}) async-start(), calls=%async_computation.1 | async-start | bytes 19496960 | tf_op jit(solution)/shard_map/all_gather | solution.py:75
  429.8 2.0 copy-start.1
  437.8 14.7 %copy-start.4 = (f32[256,64]{0,1:T(8,128)S(1)}, f32[256,64]{0,1:T(8,128)}, u32[]{:S(2)}) copy-start(f32[256,64]{0,1:T(8,128)} %param.22) | copy-start | bytes 196612
  438.4 14.7 %copy-start.3 = (f32[256,64]{0,1:T(8,128)}, f32[256,64]{0,1:T(8,128)S(1)}, u32[]{:S(2)}) copy-start(f32[256,64]{0,1:T(8,128)S(1)} %get-tuple-element.183) | copy-start | bytes 196612
Sparse Core Ops, SparseCore 0:
  15.1 121.9 all-gather.4
  139.3 119.0 all-gather.6
where the time goes:
time: 466 us; the launch traced here: 460 us
  waiting for transfers between devices  216 us (46%)
  matrix products  153 us (33%)
  local copies, waits for them, and re-layouts  54.1 us (12%)
  between operations  15.7 us (3%)
  blocking collectives  13.2 us (3%)
  other arithmetic  7.8 us (2%)
    all_gather x1, waiting for transfers between devices, per_device(): key_piece = lax.all_gather(key_flat, 'seq', axis=0, tiled=True)  118 us
    all_gather x1, waiting for transfers between devices, per_device(): value_piece = lax.all_gather(value_flat, 'seq', axis=0, tiled=True)  96.8 us
    dot_general x32, matrix products, head_terms(): jnp.dot(weights.astype(jnp.bfloat16), value_head, preferred_element_type=...  80.5 us
    dot_general x32, matrix products, head_terms(): jnp.dot(query_head, key_head.T, preferred_element_type=jnp.float32) * 0.125  65.8 us
    all_gather x1, local copies, waits for them, and re-layouts, per_device(): key_piece = lax.all_gather(key_flat, 'seq', axis=0, tiled=True)  24.5 us
    all_gather x1, local copies, waits for them, and re-layouts, per_device(): value_piece = lax.all_gather(value_flat, 'seq', axis=0, tiled=True)  23.8 us
    all_gather x1, blocking collectives, entering(): everything = lax.all_gather(value.astype(jnp.bfloat16), axis)  13.2 us
  transfers between devices with their start and end apart: 2, of which 2 were waited for; matrix products, arithmetic and copies ran while one was open for 6% of the time, Pallas kernels for 0%

commit v1 on v0

v1 whole, which is shorter than its diff:
```python
import functools

import jax
import jax.numpy as jnp
from jax import lax
from jax.experimental import pallas as pl
from jax.experimental.pallas import tpu as pltpu
from jax.sharding import PartitionSpec as P

HEADS = 32
HEAD_DIM = 64
HD = 2048
D = 2432
LAT = 64
PAIR = 128
RING = 4
BOTH = ("tm", "seq")
NT = (((1,), (1,)), ((), ()))
SCALE = 0.125 * 1.4426950408889634
KEY_CUTS = ((0, 144), (144, 280))
PIECES = ((0, 128), (128, 256))
QROWS = 256
TILE = 512
BLOCK_Q = 1024
VROWS = 128
MIB = 2**20


def ring_perm(first, shift):
    pairs = []
    for slot in range(8):
        for place in range(16):
            x, z = divmod(place, RING)
            if (slot % 2 == 0) == first:
                x2, z2 = (x + shift) % RING, z
            else:
                x2, z2 = x, (z + shift) % RING
            pairs.append((slot * 16 + place, slot * 16 + x2 * RING + z2))
    return pairs


def send(value, first, shift):
    return lax.ppermute(value, BOTH, ring_perm(first, shift % RING))


def head_norm(block):
    wide = block.astype(jnp.float32)
    square = wide * wide
    high = square.astype(jnp.bfloat16)
    low = (square - high.astype(jnp.float32)).astype(jnp.bfloat16)
    row = lax.broadcasted_iota(jnp.int32, (PAIR, PAIR), 0)
    col = lax.broadcasted_iota(jnp.int32, (PAIR, PAIR), 1)
    same = ((row < HEAD_DIM) == (col < HEAD_DIM)).astype(jnp.bfloat16)
    total = jnp.dot(high, same, preferred_element_type=jnp.float32)
    total = total + jnp.dot(low, same, preferred_element_type=jnp.float32)
    return (wide * lax.rsqrt(total * (1.0 / HEAD_DIM) + 1e-06)).astype(jnp.bfloat16)


def padded(rows):
    return -(-rows // 16) * 16


def pack_kernel(nq, cut, place_ref, *refs):
    if nq:
        q_ref, k_ref, v_ref = refs[:3]
        outs = refs[3:]
    else:
        k_ref, v_ref = refs[:2]
        outs = refs[2:]
    k0, k1 = cut
    nk = k1 - k0
    kp = nq
    vp = kp + padded(nk)
    for d in range(RING):
        group = lax.rem(place_ref[0] + d, RING)
        for j in range(RING):
            lanes = pl.ds(pl.multiple_of(group * (RING * PAIR) + j * PAIR, PAIR), PAIR)
            out = outs[d]
            if nq:
                out[j, 0:nq] = head_norm(q_ref[:, lanes])
            out[j, kp : kp + nk] = head_norm(k_ref[k0:k1, lanes])
            out[j, vp : vp + nk] = v_ref[k0:k1, lanes]
            if vp > kp + nk:
                out[j, kp + nk : vp] = jnp.zeros((vp - kp - nk, PAIR), jnp.bfloat16)


def pack(place, queries, keys, values, nq, cut):
    nk = cut[1] - cut[0]
    rows = nq + padded(nk) + nk
    operands = ([queries] if nq else []) + [keys, values]
    vmem = pl.BlockSpec(memory_space=pltpu.VMEM)
    return pl.pallas_call(
        functools.partial(pack_kernel, nq, cut),
        in_specs=[pl.BlockSpec(memory_space=pltpu.SMEM)] + [vmem] * len(operands),
        out_specs=[vmem] * RING,
        out_shape=[jax.ShapeDtypeStruct((RING, rows, PAIR), jnp.bfloat16)] * RING,
        compiler_params=pltpu.CompilerParams(vmem_limit_bytes=16 * MIB),
        cost_estimate=pl.CostEstimate(flops=2 * 2 * rows * HD * PAIR, bytes_accessed=4 * rows * HD, transcendentals=0),
        name="pack",
    )(place, *operands)


def regroup(parts, index):
    return [
        jnp.stack([lax.dynamic_index_in_dim(part, lax.rem(index + e, RING), 0, keepdims=False) for part in parts])
        for e in range(RING)
    ]


def exchange(parts, second):
    landed = [parts[0]] + [send(parts[d], True, d) for d in range(1, RING)]
    staged = regroup(landed, second)
    return [staged[0]] + [send(staged[e], False, e) for e in range(1, RING)]


def give_back(blocks):
    landed = [blocks[0]] + [send(blocks[e], False, -e) for e in range(1, RING)]
    staged = [jnp.stack([block[d] for block in landed]) for d in range(RING)]
    return [staged[0]] + [send(staged[d], True, -d) for d in range(1, RING)]


def cuts_of(total, step):
    return [(start, min(step, total - start)) for start in range(0, total, step)]


def attend_kernel(nk, kp, rows, first, last, *refs):
    q_refs, refs = refs[:RING], refs[RING:]
    if first:
        kv_refs = q_refs
    else:
        kv_refs, refs = refs[:RING], refs[RING:]
        acc_in, refs = refs[0], refs[1:]
    if last:
        out_refs, refs = refs[:RING], refs[RING:]
    else:
        acc_out, refs = refs[0], refs[1:]
    q_all, k_all, low_t, high_t = refs
    vp = kp + padded(nk)
    r0, r1 = rows
    nr = r1 - r0
    total = RING * RING * nk
    row = lax.broadcasted_iota(jnp.int32, (PAIR, PAIR), 0)
    col = lax.broadcasted_iota(jnp.int32, (PAIR, PAIR), 1)
    eye = (row == col).astype(jnp.bfloat16)
    for e in range(RING):
        for d in range(RING):
            slot = e * RING + d
            for p0, p1 in PIECES:
                if r0 <= p0 and p1 <= r1:
                    base = RING * RING * (p0 - r0) + slot * (p1 - p0)
                    q_all[base : base + p1 - p0] = q_refs[e][d, p0:p1]
            k_all[slot * nk : (slot + 1) * nk] = kv_refs[e][d, kp : kp + nk]
    ones = jnp.ones((VROWS - HEAD_DIM, total), jnp.bfloat16)
    low_t[HEAD_DIM:, :] = ones
    high_t[HEAD_DIM:, :] = ones
    for e in range(RING):
        joined = jnp.concatenate([kv_refs[e][d, vp : vp + nk] for d in range(RING)], axis=0)
        turned = lax.dot_general(eye, joined, NT, preferred_element_type=jnp.float32).astype(jnp.bfloat16)
        low_t[0:HEAD_DIM, e * RING * nk : (e + 1) * RING * nk] = turned[:HEAD_DIM]
        high_t[0:HEAD_DIM, e * RING * nk : (e + 1) * RING * nk] = turned[HEAD_DIM:]
    values_t = (low_t, high_t)
    work = [(h, start, size) for start, size in cuts_of(total, TILE) for h in range(2)]

    @pl.loop(0, RING * RING * nr // BLOCK_Q)
    def _(block):
        q0 = pl.multiple_of(block * BLOCK_Q, BLOCK_Q)
        q = q_all[pl.ds(q0, BLOCK_Q), :]
        lane = lax.broadcasted_iota(jnp.int32, q.shape, 1)
        zero = jnp.zeros_like(q)
        halves = (jnp.where(lane < HEAD_DIM, q, zero), jnp.where(lane < HEAD_DIM, zero, q))
        sums = [jnp.zeros((VROWS, BLOCK_Q), jnp.float32) for _ in range(2)]

        def score(item):
            h, start, size = item
            return lax.dot_general(k_all[start : start + size, :], halves[h], NT, preferred_element_type=jnp.float32)

        ahead = score(work[0])
        for i, (h, start, size) in enumerate(work):
            now = ahead
            if i + 1 < len(work):
                ahead = score(work[i + 1])
            weights = jnp.exp2(now * SCALE).astype(jnp.bfloat16)
            sums[h] = sums[h] + jnp.dot(
                values_t[h][:, start : start + size], weights, preferred_element_type=jnp.float32
            )
        kept = HEAD_DIM + 8
        if not first:
            qa = pl.multiple_of(RING * RING * r0 + block * BLOCK_Q, BLOCK_Q)
            sums = [sums[h][:kept] + acc_in[h, :, pl.ds(qa, BLOCK_Q)] for h in range(2)]
        if not last:
            for h in range(2):
                acc_out[h, :, pl.ds(q0, BLOCK_Q)] = sums[h][:kept]
        else:
            done = jnp.concatenate([s[:HEAD_DIM] / s[HEAD_DIM : HEAD_DIM + 1] for s in sums], axis=0)
            q_all[pl.ds(q0, BLOCK_Q), :] = done.T.astype(jnp.bfloat16)

    if last:
        for e in range(RING):
            for d in range(RING):
                slot = e * RING + d
                out_refs[e][d] = q_all[slot * nr : (slot + 1) * nr]


def attend(q_parts, kv_parts, acc, nk, kp, rows, last):
    first = acc is None
    nr = rows[1] - rows[0]
    nq = RING * RING * nr
    total = RING * RING * nk
    operands = list(q_parts) + ([] if first else list(kv_parts) + [acc])
    vmem = pl.BlockSpec(memory_space=pltpu.VMEM)
    if last:
        out_shape = [jax.ShapeDtypeStruct((RING, nr, PAIR), jnp.bfloat16)] * RING
    else:
        out_shape = [jax.ShapeDtypeStruct((2, HEAD_DIM + 8, nq), jnp.float32)]
    return pl.pallas_call(
        functools.partial(attend_kernel, nk, kp, rows, first, last),
        in_specs=[vmem] * len(operands),
        out_specs=[vmem] * len(out_shape),
        out_shape=out_shape,
        scratch_shapes=[
            pltpu.VMEM((nq, PAIR), jnp.bfloat16),
            pltpu.VMEM((total, PAIR), jnp.bfloat16),
            pltpu.VMEM((VROWS, total), jnp.bfloat16),
            pltpu.VMEM((VROWS, total), jnp.bfloat16),
        ],
        compiler_params=pltpu.CompilerParams(vmem_limit_bytes=32 * MIB),
        cost_estimate=pl.CostEstimate(
            flops=2 * 2 * 4 * nq * total * PAIR, bytes_accessed=2 * MIB, transcendentals=2 * nq * total
        ),
        name="attend",
    )(*operands)


def project_kernel(rows, place_ref, level_ref, *refs):
    parts, refs = refs[:RING], refs[RING:]
    hidden_ref, w_proj_ref, w_final_ref, base_ref, slope_ref, out_ref, joined, gated = refs
    r0, r1 = rows
    for d in range(RING):
        for e in range(RING):
            pair = lax.rem(place_ref[0] + d, RING) * RING + lax.rem(place_ref[1] + e, RING)
            joined[:, pl.ds(pl.multiple_of(pair * PAIR, PAIR), PAIR)] = parts[d][e]
    squares = jnp.zeros((r1 - r0, 1), jnp.float32)
    for start, size in cuts_of(D, 512):
        cols = slice(start, start + size)
        projected = jnp.dot(joined[...], w_proj_ref[:, cols], preferred_element_type=jnp.float32)
        gate = base_ref[:, cols] + level_ref[0] * slope_ref[:, cols]
        value = hidden_ref[r0:r1, cols].astype(jnp.float32) + gate * projected
        gated[:, cols] = value
        squares = squares + jnp.sum(value * value, axis=1, keepdims=True)
    normed = (gated[...] * lax.rsqrt(squares * (1.0 / D) + 1e-06)).astype(jnp.bfloat16)
    out_ref[...] = jnp.dot(normed, w_final_ref[...], preferred_element_type=jnp.float32)


def project(place, level, parts, hidden, w_proj, w_final, base, slope, rows):
    nr = rows[1] - rows[0]
    vmem = pl.BlockSpec(memory_space=pltpu.VMEM)
    smem = pl.BlockSpec(memory_space=pltpu.SMEM)
    return pl.pallas_call(
        functools.partial(project_kernel, rows),
        in_specs=[smem, smem] + [vmem] * (RING + 5),
        out_specs=vmem,
        out_shape=jax.ShapeDtypeStruct((nr, LAT), jnp.float32),
        scratch_shapes=[pltpu.VMEM((nr, HD), jnp.bfloat16), pltpu.VMEM((nr, D), jnp.float32)],
        compiler_params=pltpu.CompilerParams(vmem_limit_bytes=32 * MIB),
        cost_estimate=pl.CostEstimate(flops=2 * nr * HD * D, bytes_accessed=12 * MIB, transcendentals=0),
        name="project",
    )(place, level, *parts, hidden, w_proj, w_final, base, slope)


def sigma_of(index_val, total_steps):
    frac = 1.0 - index_val.astype(jnp.float32) / total_steps
    return 3.0 * frac / (1.0 + 2.0 * frac)


def running_sum(drift, slots):
    shift = 1
    while shift < slots:
        drift = drift + lax.ppermute(drift, "tm", [(i, i + shift) for i in range(slots - shift)])
        shift *= 2
    return drift


def per_device(
    queries, keys, values, hidden, w_proj, w_final, gate_base, gate_slope, start_latent, window_steps
):
    slots = lax.axis_size("tm")
    slot = lax.axis_index("tm")
    seat = lax.axis_index("seq")
    x, z = seat // RING, lax.rem(seat, RING)
    even = lax.rem(slot, 2) == 0
    first, second = jnp.where(even, x, z), jnp.where(even, z, x)
    place = jnp.stack([first, second]).astype(jnp.int32)
    sigma_now = sigma_of(window_steps[slot], 2 * slots)
    step_size = sigma_of(window_steps[slot + 1], 2 * slots) - sigma_now
    level = sigma_now.reshape(1)

    received = []
    for number, cut in enumerate(KEY_CUTS):
        parts = pack(place, queries[0], keys[0], values[0], QROWS if number == 0 else 0, cut)
        received.append(exchange(parts, second))
    q_parts = received[0]
    acc = None
    outs = []
    for number, cut in enumerate(KEY_CUTS):
        nk = cut[1] - cut[0]
        kp = QROWS if number == 0 else 0
        if number < len(KEY_CUTS) - 1:
            (acc,) = attend(q_parts, received[number], acc, nk, kp, (0, QROWS), False)
        else:
            outs = [attend(q_parts, received[number], acc, nk, kp, rows, True) for rows in PIECES]
    velocities, latents = [], []
    for rows, blocks in zip(PIECES, outs):
        back = give_back(blocks)
        velocity = project(
            place, level, back, hidden[0], w_proj, w_final, gate_base[None], gate_slope[None], rows
        )
        velocities.append(velocity)
        latents.append(start_latent[rows[0] : rows[1]] + running_sum(step_size * velocity, slots))
    return (jnp.concatenate(velocities)[None], jnp.concatenate(latents)[None])


def solution(mesh):
    placed = (
        P("tm", "seq", None),
        P("tm", "seq", None),
        P("tm", "seq", None),
        P("tm", "seq", None),
        P(),
        P(),
        P(),
        P(),
        P("seq", None),
        P(),
    )
    return jax.shard_map(
        per_device,
        mesh=mesh,
        in_specs=placed,
        out_specs=(P("tm", "seq", None), P("tm", "seq", None)),
        check_vma=False,
    )
```

time: 466 us -> 143 us (0.31); the launches traced: 460 us -> 142 us
  waiting for transfers between devices: 216 us -> 25.6 us
  matrix products: 153 us -> 0 us
  starting transfers between devices: 0.08 us -> 52.8 us
  Pallas kernels: 0 us -> 41.6 us
  local copies, waits for them, and re-layouts: 54.1 us -> 18.4 us
  blocking collectives: 13.2 us -> 0 us
  between operations: 15.7 us -> 2.63 us
  other arithmetic: 7.8 us -> 0.8 us
    all_gather x2 -> x0, waiting for transfers between devices: 215 us -> none  [the longest x1 118 us: per_device(): key_piece = lax.all_gather(key_flat, 'seq', axis=0, tiled=True)]
    dot_general x66 -> x0, matrix products: 153 us -> none  [the longest x32 80.5 us: head_terms(): jnp.dot(weights.astype(jnp.bfloat16), value_head, preferred_element_type=...]
    ppermute x0 -> x30, starting transfers between devices: none -> 52.8 us  [the longest x24 35.3 us: send(): return lax.ppermute(value, BOTH, ring_perm(first, shift % RING))]
    all_gather x2 -> x0, local copies, waits for them, and re-layouts: 48.3 us -> none  [the longest x1 24.5 us: per_device(): key_piece = lax.all_gather(key_flat, 'seq', axis=0, tiled=True)]
    pallas_call x0 -> x7, Pallas kernels: none -> 41.6 us  [the longest x3 33.1 us: attend(): pl.pallas_call(functools.partial(attend_kernel, nk, kp, rows, first, last...]
    ppermute x0 -> x30, waiting for transfers between devices: none -> 25.6 us  [the longest x24 23.7 us: send(): return lax.ppermute(value, BOTH, ring_perm(first, shift % RING))]
    all_gather x1 -> x0, blocking collectives: 13.2 us -> none  [entering(): everything = lax.all_gather(value.astype(jnp.bfloat16), axis)]
    dynamic_slice x1 -> x9, local copies, waits for them, and re-layouts: 0.67 us -> 7.5 us  [the longest x8 6.91 us: regroup(): lax.dynamic_index_in_dim(part, lax.rem(index + e, RING), 0, keepdims=False)]
  transfers between devices with their start and end apart: 2 -> 30, of which waited for: 2 -> 8; matrix products, arithmetic and copies ran while one was open for 6% -> 10% of each run, Pallas kernels for 0% -> 22%
where the time goes in v1:
time: 143 us; the launch traced here: 142 us
  starting transfers between devices  52.8 us (37%)
  Pallas kernels  41.6 us (29%)
  waiting for transfers between devices  25.6 us (18%)
  local copies, waits for them, and re-layouts  18.4 us (13%)
  between operations  2.63 us (2%)
    ppermute x24, starting transfers between devices, send(): return lax.ppermute(value, BOTH, ring_perm(first, shift % RING))  35.3 us
    pallas_call x3, Pallas kernels, attend(): pl.pallas_call(functools.partial(attend_kernel, nk, kp, rows, first, last...  33.1 us
    ppermute x24, waiting for transfers between devices, send(): return lax.ppermute(value, BOTH, ring_perm(first, shift % RING))  23.7 us
    ppermute x6, starting transfers between devices, running_sum(): lax.ppermute(drift, 'tm', [(i, i + shift) for i in range(slots - shift)])  17.4 us
    unnamed x45, local copies, waits for them, and re-layouts  8.74 us
    dynamic_slice x8, local copies, waits for them, and re-layouts, regroup(): lax.dynamic_index_in_dim(part, lax.rem(index + e, RING), 0, keepdims=False)  6.91 us
    pallas_call x2, Pallas kernels, project(): pl.pallas_call(functools.partial(project_kernel, rows), in_specs=[smem, s...  5.18 us
    pallas_call x2, Pallas kernels, pack(): pl.pallas_call(functools.partial(pack_kernel, nq, cut), in_specs=[pl.Bloc...  3.3 us
  transfers between devices with their start and end apart: 30, of which 8 were waited for; matrix products, arithmetic and copies ran while one was open for 10% of the time, Pallas kernels for 22%

profile of v1, /device:TPU:0, one launch (start us, length us, event | category | flops | bytes accessed | tf_op | source)
XLA Modules:
  0.0 141.8 jit_solution(18342609595698340193)
XLA Ops:
  0.7 1.3 copy-done.1
  2.0 1.3 copy-done.3
  3.2 1.2 copy-done.5
  4.5 2.0 %pack.2 = (bf16[4,544,128]{2,1,0:T(8,128)(2,1)S(1)}, bf16[4,544,128]{2,1,0:T(8,128)(2,1)S(1)}, bf16[4,544,128]{2,1,0:T(8,128)(2,1)S(1)}, bf16[4,544,128]{2,1,0:T(8,128)(2,1)S(1)}) custom-call(s32[2]{0:T(128)S(1)} %pad_add_fusion.place_ref, bf16[256,2048]{1,0:T(8,128)(2,1)S(1)} %bitcast.19, bf16[280,2048]{1,0:T(8,128)(2,1)S(1)} %bitcast.15, ...), custom_call_target="tpu_custom_call" | custom-call | flops 570425344 | bytes 4456448 | tf_op jit(solution)/shard_map/pack/pallas_call | solution.py:92
  6.5 2.9 %collective-permute-start.2 = (bf16[4,544,128]{2,1,0:T(8,128)(2,1)S(1)}, bf16[4,544,128]{2,1,0:T(8,128)(2,1)}, u32[]{:S(2)}, u32[]{:S(2)}) collective-permute-start(bf16[4,544,128]{2,1,0:T(8,128)(2,1)S(1)} %get-tuple-element.21), channel_id=1, source_target_pairs={{0,12},{1,13},{2,14},{3,15},{4,0},{5,1},{6,2},{7,3},{8,4},{9,5},{1... | collective-permute-start | bytes 1671176 | tf_op jit(solution)/shard_map/ppermute | solution.py:43
  10.2 1.3 pack.3
  11.5 1.1 collective-permute-start.8
  12.7 1.9 %collective-permute-start.7 = (bf16[4,280,128]{2,1,0:T(8,128)(2,1)S(1)}, bf16[4,280,128]{2,1,0:T(8,128)(2,1)}, u32[]{:S(2)}, u32[]{:S(2)}) collective-permute-start(bf16[4,280,128]{2,1,0:T(8,128)(2,1)S(1)} %get-tuple-element.24), channel_id=1, source_target_pairs={{0,8},{1,9},{2,10},{3,11},{4,12},{5,13},{6,14},{7,15},{8,0},{9,1},... | collective-permute-start | bytes 860168 | tf_op jit(solution)/shard_map/ppermute | solution.py:43
  14.6 1.2 collective-permute-start.6
  19.7 1.3 copy.12.refs_6_
  22.4 1.5 %copy.19 = f32[128,64]{1,0:T(8,128)} copy(f32[128,64]{0,1:T(8,128)} %get-tuple-element.101) | data formatting | bytes 65536
  24.7 3.8 %collective-permute-done.8 = bf16[4,280,128]{2,1,0:T(8,128)(2,1)} collective-permute-done((bf16[4,280,128]{2,1,0:T(8,128)(2,1)S(1)}, bf16[4,280,128]{2,1,0:T(8,128)(2,1)}, u32[]{:S(2)}, u32[]{:S(2)}) %collective-permute-start.8) | collective-permute-done | bytes 286752 | tf_op jit(solution)/shard_map/ppermute | solution.py:43
  28.5 1.0 constant_dynamic-slice_fusion
  29.6 1.0 constant_dynamic-slice_fusion.1
  30.6 1.0 constant_dynamic-slice_fusion.2
  31.6 1.2 constant_dynamic-slice_fusion.16
  32.8 1.2 constant_dynamic-slice_fusion.17
  34.0 5.8 %collective-permute-done = bf16[4,544,128]{2,1,0:T(8,128)(2,1)S(1)} collective-permute-done((bf16[4,544,128]{2,1,0:T(8,128)(2,1)S(1)}, bf16[4,544,128]{2,1,0:T(8,128)(2,1)S(1)}, u32[]{:S(2)}, u32[]{:S(2)}) %collective-permute-start) | collective-permute-done | bytes 557088 | tf_op jit(solution)/shard_map/ppermute | solution.py:43
  40.0 2.0 %collective-permute-start.3 = (bf16[4,544,128]{2,1,0:T(8,128)(2,1)S(1)}, bf16[4,544,128]{2,1,0:T(8,128)(2,1)S(1)}, u32[]{:S(2)}, u32[]{:S(2)}) collective-permute-start(bf16[4,544,128]{2,1,0:T(8,128)(2,1)S(1)} %pad_maximum_fusion.1), channel_id=1, source_target_pairs={{0,1},{1,2},{2,3},{3,0},{4,5},{5,6},{6,7},{7,4},{8,9},{9,10},{10,1... | collective-permute-start | bytes 1671176 | tf_op jit(solution)/shard_map/ppermute | solution.py:43
  42.1 3.7 %collective-permute-start.4 = (bf16[4,544,128]{2,1,0:T(8,128)(2,1)S(1)}, bf16[4,544,128]{2,1,0:T(8,128)(2,1)S(1)}, u32[]{:S(2)}, u32[]{:S(2)}) collective-permute-start(bf16[4,544,128]{2,1,0:T(8,128)(2,1)S(1)} %pad_maximum_fusion.2), channel_id=1, source_target_pairs={{0,2},{1,3},{2,0},{3,1},{4,6},{5,7},{6,4},{7,5},{8,10},{9,11},{10,... | collective-permute-start | bytes 1671176 | tf_op jit(solution)/shard_map/ppermute | solution.py:43
  45.8 1.1 collective-permute-start.5
  46.9 1.1 collective-permute-start.9
  48.8 2.8 %collective-permute-done.3.refs_1_ = bf16[4,544,128]{2,1,0:T(8,128)(2,1)S(1)} collective-permute-done((bf16[4,544,128]{2,1,0:T(8,128)(2,1)S(1)}, bf16[4,544,128]{2,1,0:T(8,128)(2,1)S(1)}, u32[]{:S(2)}, u32[]{:S(2)}) %collective-permute-start.3) | collective-permute-done | bytes 557088 | tf_op jit(solution)/shard_map/ppermute | solution.py:43
  51.6 2.0 %collective-permute-start.11 = (bf16[4,280,128]{2,1,0:T(8,128)(2,1)S(1)}, bf16[4,280,128]{2,1,0:T(8,128)(2,1)S(1)}, u32[]{:S(2)}, u32[]{:S(2)}) collective-permute-start(bf16[4,280,128]{2,1,0:T(8,128)(2,1)S(1)} %pad_maximum_fusion.7), channel_id=1, source_target_pairs={{0,3},{1,0},{2,1},{3,2},{4,7},{5,4},{6,5},{7,6},{8,11},{9,8},{10,9... | collective-permute-start | bytes 860168 | tf_op jit(solution)/shard_map/ppermute | solution.py:43
  53.6 5.5 %collective-permute-done.4.refs_2_ = bf16[4,544,128]{2,1,0:T(8,128)(2,1)S(1)} collective-permute-done((bf16[4,544,128]{2,1,0:T(8,128)(2,1)S(1)}, bf16[4,544,128]{2,1,0:T(8,128)(2,1)S(1)}, u32[]{:S(2)}, u32[]{:S(2)}) %collective-permute-start.4) | collective-permute-done | bytes 557088 | tf_op jit(solution)/shard_map/ppermute | solution.py:43
  59.1 16.4 %attend.3.refs_8_ = f32[2,72,4096]{2,1,0:T(8,128)S(1)} custom-call(bf16[4,544,128]{2,1,0:T(8,128)(2,1)S(1)} %pad_maximum_fusion.refs_0_, bf16[4,544,128]{2,1,0:T(8,128)(2,1)S(1)} %collective-permute-done.3.refs_1_, bf16[4,544,128]{2,1,0:T(8,128)(2,1)S(1)} %collective-permute-done.4.refs_2_, bf16[4,544,128]{2,1,0:T(8,128)(2,1)S(1)} %collective-permute-done.5.refs_3_), custom_call_target="tpu_custom_call" | custom-call | flops 19327352832 | bytes 2097152 | tf_op jit(solution)/shard_map/attend/pallas_call | solution.py:215
  75.6 8.4 %attend.5 = (bf16[4,128,128]{2,1,0:T(8,128)(2,1)S(1)}, bf16[4,128,128]{2,1,0:T(8,128)(2,1)S(1)}, bf16[4,128,128]{2,1,0:T(8,128)(2,1)S(1)}, bf16[4,128,128]{2,1,0:T(8,128)(2,1)S(1)}) custom-call(bf16[4,544,128]{2,1,0:T(8,128)(2,1)S(1)} %pad_maximum_fusion.refs_0_, bf16[4,544,128]{2,1,0:T(8,128)(2,1)S(1)} %collective-permute-done.3.refs_1_, ...), custom_call_target="tpu_custom_call" | custom-call | flops 9126805504 | bytes 2097152 | tf_op jit(solution)/shard_map/attend/pallas_call | solution.py:215
  83.9 1.7 %collective-permute-start.20 = (bf16[4,128,128]{2,1,0:T(8,128)(2,1)S(1)}, bf16[4,128,128]{2,1,0:T(8,128)(2,1)S(1)}, u32[]{:S(2)}, u32[]{:S(2)}) collective-permute-start(bf16[4,128,128]{2,1,0:T(8,128)(2,1)S(1)} %get-tuple-element.33), channel_id=1, source_target_pairs={{0,1},{1,2},{2,3},{3,0},{4,5},{5,6},{6,7},{7,4},{8,9},{9,10},{10,1... | collective-permute-start | bytes 393224 | tf_op jit(solution)/shard_map/ppermute | solution.py:43
  85.7 1.9 %collective-permute-start.19 = (bf16[4,128,128]{2,1,0:T(8,128)(2,1)S(1)}, bf16[4,128,128]{2,1,0:T(8,128)(2,1)S(1)}, u32[]{:S(2)}, u32[]{:S(2)}) collective-permute-start(bf16[4,128,128]{2,1,0:T(8,128)(2,1)S(1)} %get-tuple-element.32), channel_id=1, source_target_pairs={{0,2},{1,3},{2,0},{3,1},{4,6},{5,7},{6,4},{7,5},{8,10},{9,11},{10,... | collective-permute-start | bytes 393224 | tf_op jit(solution)/shard_map/ppermute | solution.py:43
  87.6 1.6 %collective-permute-start.18 = (bf16[4,128,128]{2,1,0:T(8,128)(2,1)S(1)}, bf16[4,128,128]{2,1,0:T(8,128)(2,1)S(1)}, u32[]{:S(2)}, u32[]{:S(2)}) collective-permute-start(bf16[4,128,128]{2,1,0:T(8,128)(2,1)S(1)} %get-tuple-element.31), channel_id=1, source_target_pairs={{0,3},{1,0},{2,1},{3,2},{4,7},{5,4},{6,5},{7,6},{8,11},{9,8},{10,9... | collective-permute-start | bytes 393224 | tf_op jit(solution)/shard_map/ppermute | solution.py:43
  89.3 8.4 %attend.4 = (bf16[4,128,128]{2,1,0:T(8,128)(2,1)S(1)}, bf16[4,128,128]{2,1,0:T(8,128)(2,1)S(1)}, bf16[4,128,128]{2,1,0:T(8,128)(2,1)S(1)}, bf16[4,128,128]{2,1,0:T(8,128)(2,1)S(1)}) custom-call(bf16[4,544,128]{2,1,0:T(8,128)(2,1)S(1)} %pad_maximum_fusion.refs_0_, bf16[4,544,128]{2,1,0:T(8,128)(2,1)S(1)} %collective-permute-done.3.refs_1_, ...), custom_call_target="tpu_custom_call" | custom-call | flops 9126805504 | bytes 2097152 | tf_op jit(solution)/shard_map/attend/pallas_call | solution.py:215
  98.2 1.6 %collective-permute-start.13 = (bf16[4,128,128]{2,1,0:T(8,128)(2,1)S(1)}, bf16[4,128,128]{2,1,0:T(8,128)(2,1)S(1)}, u32[]{:S(2)}, u32[]{:S(2)}) collective-permute-start(bf16[4,128,128]{2,1,0:T(8,128)(2,1)S(1)} %get-tuple-element.28), channel_id=1, source_target_pairs={{0,2},{1,3},{2,0},{3,1},{4,6},{5,7},{6,4},{7,5},{8,10},{9,11},{10,... | collective-permute-start | bytes 393224 | tf_op jit(solution)/shard_map/ppermute | solution.py:43
  99.8 1.6 %collective-permute-start.12 = (bf16[4,128,128]{2,1,0:T(8,128)(2,1)S(1)}, bf16[4,128,128]{2,1,0:T(8,128)(2,1)S(1)}, u32[]{:S(2)}, u32[]{:S(2)}) collective-permute-start(bf16[4,128,128]{2,1,0:T(8,128)(2,1)S(1)} %get-tuple-element.27), channel_id=1, source_target_pairs={{0,3},{1,0},{2,1},{3,2},{4,7},{5,4},{6,5},{7,6},{8,11},{9,8},{10,9... | collective-permute-start | bytes 393224 | tf_op jit(solution)/shard_map/ppermute | solution.py:43
  101.5 2.1 %collective-permute-start.21 = (bf16[4,128,128]{2,1,0:T(8,128)(2,1)S(1)}, bf16[4,128,128]{2,1,0:T(8,128)(2,1)S(1)}, u32[]{:S(2)}, u32[]{:S(2)}) collective-permute-start(bf16[4,128,128]{2,1,0:T(8,128)(2,1)S(1)} %pad_maximum_fusion.13), channel_id=1, source_target_pairs={{0,12},{1,13},{2,14},{3,15},{4,0},{5,1},{6,2},{7,3},{8,4},{9,5},{1... | collective-permute-start | bytes 393224 | tf_op jit(solution)/shard_map/ppermute | solution.py:43
  103.8 3.7 %collective-permute-done.14 = bf16[4,128,128]{2,1,0:T(8,128)(2,1)S(1)} collective-permute-done((bf16[4,128,128]{2,1,0:T(8,128)(2,1)S(1)}, bf16[4,128,128]{2,1,0:T(8,128)(2,1)S(1)}, u32[]{:S(2)}, u32[]{:S(2)}) %collective-permute-start.14) | collective-permute-done | bytes 131104 | tf_op jit(solution)/shard_map/ppermute | solution.py:43
  107.5 1.1 collective-permute-done.12
  108.7 2.8 %collective-permute-start.15 = (bf16[4,128,128]{2,1,0:T(8,128)(2,1)S(1)}, bf16[4,128,128]{2,1,0:T(8,128)(2,1)S(1)}, u32[]{:S(2)}, u32[]{:S(2)}) collective-permute-start(bf16[4,128,128]{2,1,0:T(8,128)(2,1)S(1)} %pad_maximum_fusion.9), channel_id=1, source_target_pairs={{0,12},{1,13},{2,14},{3,15},{4,0},{5,1},{6,2},{7,3},{8,4},{9,5},{1... | collective-permute-start | bytes 393224 | tf_op jit(solution)/shard_map/ppermute | solution.py:43
  111.5 1.6 %collective-permute-start.16 = (bf16[4,128,128]{2,1,0:T(8,128)(2,1)S(1)}, bf16[4,128,128]{2,1,0:T(8,128)(2,1)S(1)}, u32[]{:S(2)}, u32[]{:S(2)}) collective-permute-start(bf16[4,128,128]{2,1,0:T(8,128)(2,1)S(1)} %pad_maximum_fusion.10), channel_id=1, source_target_pairs={{0,8},{1,9},{2,10},{3,11},{4,12},{5,13},{6,14},{7,15},{8,0},{9,1},... | collective-permute-start | bytes 393224 | tf_op jit(solution)/shard_map/ppermute | solution.py:43
  113.2 1.5 %collective-permute-start.17 = (bf16[4,128,128]{2,1,0:T(8,128)(2,1)S(1)}, bf16[4,128,128]{2,1,0:T(8,128)(2,1)S(1)}, u32[]{:S(2)}, u32[]{:S(2)}) collective-permute-start(bf16[4,128,128]{2,1,0:T(8,128)(2,1)S(1)} %pad_maximum_fusion.11), channel_id=1, source_target_pairs={{0,4},{1,5},{2,6},{3,7},{4,8},{5,9},{6,10},{7,11},{8,12},{9,13},{1... | collective-permute-start | bytes 393224 | tf_op jit(solution)/shard_map/ppermute | solution.py:43
  114.7 2.6 %project.3 = f32[128,64]{1,0:T(8,128)S(1)} custom-call(s32[2]{0:T(128)S(1)} %pad_add_fusion.place_ref, f32[1]{0:T(128)S(6)} %div.27.level_ref, bf16[4,128,128]{2,1,0:T(8,128)(2,1)S(1)} %pad_maximum_fusion.12.refs_0_, bf16[4,128,128]{2,1,0:T(8,128)(2,1)S(1)} %collective-permute-done.21.refs_1_, bf16[4,128,128]{2,1,0:T(8,128)(2,1)S(1)} %collective-permute-done.22.refs_2_, ...), custom_call_target="tpu_custom_call" | custom-call | flops 1275068416 | bytes 12582912 | tf_op jit(solution)/shard_map/project/pallas_call | solution.py:258
  117.3 1.3 collective-permute-start.27
  119.5 2.6 %project.2 = f32[128,64]{1,0:T(8,128)S(1)} custom-call(s32[2]{0:T(128)S(1)} %pad_add_fusion.place_ref, f32[1]{0:T(128)S(6)} %div.27.level_ref, bf16[4,128,128]{2,1,0:T(8,128)(2,1)S(1)} %pad_maximum_fusion.8.refs_0_, bf16[4,128,128]{2,1,0:T(8,128)(2,1)S(1)} %collective-permute-done.15.refs_1_, bf16[4,128,128]{2,1,0:T(8,128)(2,1)S(1)} %collective-permute-done.16.refs_2_, ...), custom_call_target="tpu_custom_call" | custom-call | flops 1275068416 | bytes 12582912 | tf_op jit(solution)/shard_map/project/pallas_call | solution.py:258
  122.1 3.5 %collective-permute-start.24 = (f32[128,64]{1,0:T(8,128)S(1)}, f32[128,64]{1,0:T(8,128)S(1)}, u32[]{:S(2)}, u32[]{:S(2)}) collective-permute-start(f32[128,64]{1,0:T(8,128)S(1)} %broadcast_multiply_fusion.1), channel_id=1, source_target_pairs={{0,16},{16,32},{32,48},{48,64},{64,80},{80,96},{96,112},{1,17},{17... | collective-permute-start | bytes 98312 | tf_op jit(solution)/shard_map/ppermute | solution.py:278
  125.6 3.5 %collective-permute-start.28 = (f32[128,64]{1,0:T(8,128)S(1)}, f32[128,64]{1,0:T(8,128)S(1)}, u32[]{:S(2)}, u32[]{:S(2)}) collective-permute-start(f32[128,64]{1,0:T(8,128)S(1)} %fusion.11), channel_id=1, source_target_pairs={{0,32},{16,48},{32,64},{48,80},{64,96},{80,112},{1,33},{17,49},{33... | collective-permute-start | bytes 98312 | tf_op jit(solution)/shard_map/ppermute | solution.py:278
  129.2 3.2 %collective-permute-start.25 = (f32[128,64]{1,0:T(8,128)S(1)}, f32[128,64]{1,0:T(8,128)S(1)}, u32[]{:S(2)}, u32[]{:S(2)}) collective-permute-start(f32[128,64]{1,0:T(8,128)S(1)} %fusion.10), channel_id=1, source_target_pairs={{0,32},{16,48},{32,64},{48,80},{64,96},{80,112},{1,33},{17,49},{33... | collective-permute-start | bytes 98312 | tf_op jit(solution)/shard_map/ppermute | solution.py:278
  132.4 4.2 %collective-permute-start.29 = (f32[128,64]{1,0:T(8,128)S(1)}, f32[128,64]{1,0:T(8,128)S(1)}, u32[]{:S(2)}, u32[]{:S(2)}) collective-permute-start(f32[128,64]{1,0:T(8,128)S(1)} %add.131), channel_id=1, source_target_pairs={{0,64},{16,80},{32,96},{48,112},{1,65},{17,81},{33,97},{49,113},{2... | collective-permute-start | bytes 98312 | tf_op jit(solution)/shard_map/ppermute | solution.py:278
  137.4 1.7 %collective-permute-start.26 = (f32[128,64]{1,0:T(8,128)S(1)}, f32[128,64]{1,0:T(8,128)S(1)}, u32[]{:S(2)}, u32[]{:S(2)}) collective-permute-start(f32[128,64]{1,0:T(8,128)S(1)} %add.127), channel_id=1, source_target_pairs={{0,64},{16,80},{32,96},{48,112},{1,65},{17,81},{33,97},{49,113},{2... | collective-permute-start | bytes 98312 | tf_op jit(solution)/shard_map/ppermute | solution.py:278
  139.2 1.8 %collective-permute-done.26 = f32[128,64]{1,0:T(8,128)S(1)} collective-permute-done((f32[128,64]{1,0:T(8,128)S(1)}, f32[128,64]{1,0:T(8,128)S(1)}, u32[]{:S(2)}, u32[]{:S(2)}) %collective-permute-start.26) | collective-permute-done | bytes 32800 | tf_op jit(solution)/shard_map/ppermute | solution.py:278
  (112 shorter events, 10.1 us)
Async XLA Ops:
  0.7 1.3 copy-start.1
  4.5 5.7 %copy-start.2 = (bf16[1,280,2048]{2,1,0:T(8,128)(2,1)S(1)}, bf16[1,280,2048]{2,1,0:T(8,128)(2,1)}, u32[]{:S(2)}) copy-start(bf16[1,280,2048]{2,1,0:T(8,128)(2,1)} %param.11) | copy-start | bytes 3440644
  4.5 5.7 %copy-start.4 = (bf16[1,280,2048]{2,1,0:T(8,128)(2,1)S(1)}, bf16[1,280,2048]{2,1,0:T(8,128)(2,1)}, u32[]{:S(2)}) copy-start(bf16[1,280,2048]{2,1,0:T(8,128)(2,1)} %param.12) | copy-start | bytes 3440644
  6.4 9.3 %copy-start.15 = (f32[256,64]{0,1:T(8,128)S(1)}, f32[256,64]{0,1:T(8,128)}, u32[]{:S(2)}) copy-start(f32[256,64]{0,1:T(8,128)} %param.18) | copy-start | bytes 196612
  6.5 25.2 %collective-permute-start.2 = (bf16[4,544,128]{2,1,0:T(8,128)(2,1)S(1)}, bf16[4,544,128]{2,1,0:T(8,128)(2,1)}, u32[]{:S(2)}, u32[]{:S(2)}) collective-permute-start(bf16[4,544,128]{2,1,0:T(8,128)(2,1)S(1)} %get-tuple-element.21), channel_id=1, source_target_pairs={{0,12},{1,13},{2,14},{3,15},{4,0},{5,1},{6,2},{7,3},{8,4},{9,5},{1... | collective-permute-start | bytes 1671176 | tf_op jit(solution)/shard_map/ppermute | solution.py:43
  9.4 23.4 %collective-permute-start.1 = (bf16[4,544,128]{2,1,0:T(8,128)(2,1)S(1)}, bf16[4,544,128]{2,1,0:T(8,128)(2,1)}, u32[]{:S(2)}, u32[]{:S(2)}) collective-permute-start(bf16[4,544,128]{2,1,0:T(8,128)(2,1)S(1)} %get-tuple-element.20), channel_id=1, source_target_pairs={{0,8},{1,9},{2,10},{3,11},{4,12},{5,13},{6,14},{7,15},{8,0},{9,1},... | collective-permute-start | bytes 1671176 | tf_op jit(solution)/shard_map/ppermute | solution.py:43
  11.5 6.3 %copy-start.16 = (s32[9]{0:T(128)S(1)}, s32[9]{0:T(128)}, u32[]{:S(2)}) copy-start(s32[9]{0:T(128)} %param.19) | copy-start | bytes 112
  11.5 17.0 %collective-permute-start.8 = (bf16[4,280,128]{2,1,0:T(8,128)(2,1)S(1)}, bf16[4,280,128]{2,1,0:T(8,128)(2,1)}, u32[]{:S(2)}, u32[]{:S(2)}) collective-permute-start(bf16[4,280,128]{2,1,0:T(8,128)(2,1)S(1)} %get-tuple-element.25), channel_id=1, source_target_pairs={{0,12},{1,13},{2,14},{3,15},{4,0},{5,1},{6,2},{7,3},{8,4},{9,5},{1... | collective-permute-start | bytes 860168 | tf_op jit(solution)/shard_map/ppermute | solution.py:43
  12.7 16.9 %collective-permute-start.7 = (bf16[4,280,128]{2,1,0:T(8,128)(2,1)S(1)}, bf16[4,280,128]{2,1,0:T(8,128)(2,1)}, u32[]{:S(2)}, u32[]{:S(2)}) collective-permute-start(bf16[4,280,128]{2,1,0:T(8,128)(2,1)S(1)} %get-tuple-element.24), channel_id=1, source_target_pairs={{0,8},{1,9},{2,10},{3,11},{4,12},{5,13},{6,14},{7,15},{8,0},{9,1},... | collective-permute-start | bytes 860168 | tf_op jit(solution)/shard_map/ppermute | solution.py:43
  14.6 16.0 %collective-permute-start.6 = (bf16[4,280,128]{2,1,0:T(8,128)(2,1)S(1)}, bf16[4,280,128]{2,1,0:T(8,128)(2,1)}, u32[]{:S(2)}, u32[]{:S(2)}) collective-permute-start(bf16[4,280,128]{2,1,0:T(8,128)(2,1)S(1)} %get-tuple-element.23), channel_id=1, source_target_pairs={{0,4},{1,5},{2,6},{3,7},{4,8},{5,9},{6,10},{7,11},{8,12},{9,13},{1... | collective-permute-start | bytes 860168 | tf_op jit(solution)/shard_map/ppermute | solution.py:43
  28.5 11.3 %collective-permute-start = (bf16[4,544,128]{2,1,0:T(8,128)(2,1)S(1)}, bf16[4,544,128]{2,1,0:T(8,128)(2,1)S(1)}, u32[]{:S(2)}, u32[]{:S(2)}) collective-permute-start(bf16[4,544,128]{2,1,0:T(8,128)(2,1)S(1)} %get-tuple-element.19), channel_id=1, source_target_pairs={{0,4},{1,5},{2,6},{3,7},{4,8},{5,9},{6,10},{7,11},{8,12},{9,13},{1... | collective-permute-start | bytes 1671176 | tf_op jit(solution)/shard_map/ppermute | solution.py:43
  32.8 7.1 %copy-start.8 = (bf16[1,544,128]{2,1,0:T(8,128)(2,1)S(1)}, bf16[1,544,128]{2,1,0:T(8,128)(2,1)}, u32[]{:S(2)}) copy-start(bf16[1,544,128]{2,1,0:T(8,128)(2,1)} %get-tuple-element.38) | copy-start | bytes 417796
  34.0 8.0 %copy-start.7 = (bf16[1,544,128]{2,1,0:T(8,128)(2,1)S(1)}, bf16[1,544,128]{2,1,0:T(8,128)(2,1)}, u32[]{:S(2)}) copy-start(bf16[1,544,128]{2,1,0:T(8,128)(2,1)} %get-tuple-element.37) | copy-start | bytes 417796
  39.9 5.8 %copy-start.6 = (bf16[1,544,128]{2,1,0:T(8,128)(2,1)S(1)}, bf16[1,544,128]{2,1,0:T(8,128)(2,1)}, u32[]{:S(2)}) copy-start(bf16[1,544,128]{2,1,0:T(8,128)(2,1)} %get-tuple-element.36) | copy-start | bytes 417796
  40.0 6.9 %copy-start.12 = (bf16[1,280,128]{2,1,0:T(8,128)(2,1)S(1)}, bf16[1,280,128]{2,1,0:T(8,128)(2,1)}, u32[]{:S(2)}) copy-start(bf16[1,280,128]{2,1,0:T(8,128)(2,1)} %get-tuple-element.54) | copy-start | bytes 215044
  40.0 11.6 %collective-permute-start.3 = (bf16[4,544,128]{2,1,0:T(8,128)(2,1)S(1)}, bf16[4,544,128]{2,1,0:T(8,128)(2,1)S(1)}, u32[]{:S(2)}, u32[]{:S(2)}) collective-permute-start(bf16[4,544,128]{2,1,0:T(8,128)(2,1)S(1)} %pad_maximum_fusion.1), channel_id=1, source_target_pairs={{0,1},{1,2},{2,3},{3,0},{4,5},{5,6},{6,7},{7,4},{8,9},{9,10},{10,1... | collective-permute-start | bytes 1671176 | tf_op jit(solution)/shard_map/ppermute | solution.py:43
  42.0 6.0 %copy-start.11 = (bf16[1,280,128]{2,1,0:T(8,128)(2,1)S(1)}, bf16[1,280,128]{2,1,0:T(8,128)(2,1)}, u32[]{:S(2)}) copy-start(bf16[1,280,128]{2,1,0:T(8,128)(2,1)} %get-tuple-element.53) | copy-start | bytes 215044
  42.1 6.6 %copy-start.10 = (bf16[1,280,128]{2,1,0:T(8,128)(2,1)S(1)}, bf16[1,280,128]{2,1,0:T(8,128)(2,1)}, u32[]{:S(2)}) copy-start(bf16[1,280,128]{2,1,0:T(8,128)(2,1)} %get-tuple-element.55) | copy-start | bytes 215044
  42.1 17.1 %collective-permute-start.4 = (bf16[4,544,128]{2,1,0:T(8,128)(2,1)S(1)}, bf16[4,544,128]{2,1,0:T(8,128)(2,1)S(1)}, u32[]{:S(2)}, u32[]{:S(2)}) collective-permute-start(bf16[4,544,128]{2,1,0:T(8,128)(2,1)S(1)} %pad_maximum_fusion.2), channel_id=1, source_target_pairs={{0,2},{1,3},{2,0},{3,1},{4,6},{5,7},{6,4},{7,5},{8,10},{9,11},{10,... | collective-permute-start | bytes 1671176 | tf_op jit(solution)/shard_map/ppermute | solution.py:43
  45.7 2.9 %copy-start.9 = (bf16[1,280,128]{2,1,0:T(8,128)(2,1)S(1)}, bf16[1,280,128]{2,1,0:T(8,128)(2,1)}, u32[]{:S(2)}) copy-start(bf16[1,280,128]{2,1,0:T(8,128)(2,1)} %get-tuple-element.52) | copy-start | bytes 215044
  45.8 13.3 %collective-permute-start.5 = (bf16[4,544,128]{2,1,0:T(8,128)(2,1)S(1)}, bf16[4,544,128]{2,1,0:T(8,128)(2,1)S(1)}, u32[]{:S(2)}, u32[]{:S(2)}) collective-permute-start(bf16[4,544,128]{2,1,0:T(8,128)(2,1)S(1)} %pad_maximum_fusion.3), channel_id=1, source_target_pairs={{0,3},{1,0},{2,1},{3,2},{4,7},{5,4},{6,5},{7,6},{8,11},{9,8},{10,9... | collective-permute-start | bytes 1671176 | tf_op jit(solution)/shard_map/ppermute | solution.py:43
  46.9 28.6 %collective-permute-start.9 = (bf16[4,280,128]{2,1,0:T(8,128)(2,1)S(1)}, bf16[4,280,128]{2,1,0:T(8,128)(2,1)S(1)}, u32[]{:S(2)}, u32[]{:S(2)}) collective-permute-start(bf16[4,280,128]{2,1,0:T(8,128)(2,1)S(1)} %pad_maximum_fusion.5), channel_id=1, source_target_pairs={{0,1},{1,2},{2,3},{3,0},{4,5},{5,6},{6,7},{7,4},{8,9},{9,10},{10,1... | collective-permute-start | bytes 860168 | tf_op jit(solution)/shard_map/ppermute | solution.py:43
  48.1 27.5 %collective-permute-start.10 = (bf16[4,280,128]{2,1,0:T(8,128)(2,1)S(1)}, bf16[4,280,128]{2,1,0:T(8,128)(2,1)S(1)}, u32[]{:S(2)}, u32[]{:S(2)}) collective-permute-start(bf16[4,280,128]{2,1,0:T(8,128)(2,1)S(1)} %pad_maximum_fusion.6), channel_id=1, source_target_pairs={{0,2},{1,3},{2,0},{3,1},{4,6},{5,7},{6,4},{7,5},{8,10},{9,11},{10,... | collective-permute-start | bytes 860168 | tf_op jit(solution)/shard_map/ppermute | solution.py:43
  51.6 23.9 %collective-permute-start.11 = (bf16[4,280,128]{2,1,0:T(8,128)(2,1)S(1)}, bf16[4,280,128]{2,1,0:T(8,128)(2,1)S(1)}, u32[]{:S(2)}, u32[]{:S(2)}) collective-permute-start(bf16[4,280,128]{2,1,0:T(8,128)(2,1)S(1)} %pad_maximum_fusion.7), channel_id=1, source_target_pairs={{0,3},{1,0},{2,1},{3,2},{4,7},{5,4},{6,5},{7,6},{8,11},{9,8},{10,9... | collective-permute-start | bytes 860168 | tf_op jit(solution)/shard_map/ppermute | solution.py:43
  83.9 15.8 %collective-permute-start.20 = (bf16[4,128,128]{2,1,0:T(8,128)(2,1)S(1)}, bf16[4,128,128]{2,1,0:T(8,128)(2,1)S(1)}, u32[]{:S(2)}, u32[]{:S(2)}) collective-permute-start(bf16[4,128,128]{2,1,0:T(8,128)(2,1)S(1)} %get-tuple-element.33), channel_id=1, source_target_pairs={{0,1},{1,2},{2,3},{3,0},{4,5},{5,6},{6,7},{7,4},{8,9},{9,10},{10,1... | collective-permute-start | bytes 393224 | tf_op jit(solution)/shard_map/ppermute | solution.py:43
  85.7 15.7 %collective-permute-start.19 = (bf16[4,128,128]{2,1,0:T(8,128)(2,1)S(1)}, bf16[4,128,128]{2,1,0:T(8,128)(2,1)S(1)}, u32[]{:S(2)}, u32[]{:S(2)}) collective-permute-start(bf16[4,128,128]{2,1,0:T(8,128)(2,1)S(1)} %get-tuple-element.32), channel_id=1, source_target_pairs={{0,2},{1,3},{2,0},{3,1},{4,6},{5,7},{6,4},{7,5},{8,10},{9,11},{10,... | collective-permute-start | bytes 393224 | tf_op jit(solution)/shard_map/ppermute | solution.py:43
  87.6 13.8 %collective-permute-start.18 = (bf16[4,128,128]{2,1,0:T(8,128)(2,1)S(1)}, bf16[4,128,128]{2,1,0:T(8,128)(2,1)S(1)}, u32[]{:S(2)}, u32[]{:S(2)}) collective-permute-start(bf16[4,128,128]{2,1,0:T(8,128)(2,1)S(1)} %get-tuple-element.31), channel_id=1, source_target_pairs={{0,3},{1,0},{2,1},{3,2},{4,7},{5,4},{6,5},{7,6},{8,11},{9,8},{10,9... | collective-permute-start | bytes 393224 | tf_op jit(solution)/shard_map/ppermute | solution.py:43
  89.2 25.4 %slice-start = ((s8[9961472]{0:T(1024)(128)(4,1)}), s8[4194304]{0:T(1024)(128)(4,1)S(1)}, s32[]{:S(2)}) async-start(s8[9961472]{0:T(1024)(128)(4,1)} %bitcast.11), calls=%async_computation | async-start | bytes 8388608
  89.3 25.4 %slice-start.1 = ((s8[9961472]{0:T(1024)(128)(4,1)}), s8[4194304]{0:T(1024)(128)(4,1)S(1)}, s32[]{:S(2)}) async-start(s8[9961472]{0:T(1024)(128)(4,1)} %bitcast.11), calls=%async_computation.1 | async-start | bytes 8388608
  89.3 25.4 %slice-start.2 = ((s8[9961472]{0:T(1024)(128)(4,1)}), s8[1572864]{0:T(1024)(128)(4,1)S(1)}, s32[]{:S(2)}) async-start(s8[9961472]{0:T(1024)(128)(4,1)} %bitcast.11), calls=%async_computation.2 | async-start | bytes 3145728
  97.7 9.8 %collective-permute-start.14 = (bf16[4,128,128]{2,1,0:T(8,128)(2,1)S(1)}, bf16[4,128,128]{2,1,0:T(8,128)(2,1)S(1)}, u32[]{:S(2)}, u32[]{:S(2)}) collective-permute-start(bf16[4,128,128]{2,1,0:T(8,128)(2,1)S(1)} %get-tuple-element.29), channel_id=1, source_target_pairs={{0,1},{1,2},{2,3},{3,0},{4,5},{5,6},{6,7},{7,4},{8,9},{9,10},{10,1... | collective-permute-start | bytes 393224 | tf_op jit(solution)/shard_map/ppermute | solution.py:43
  98.2 9.3 %collective-permute-start.13 = (bf16[4,128,128]{2,1,0:T(8,128)(2,1)S(1)}, bf16[4,128,128]{2,1,0:T(8,128)(2,1)S(1)}, u32[]{:S(2)}, u32[]{:S(2)}) collective-permute-start(bf16[4,128,128]{2,1,0:T(8,128)(2,1)S(1)} %get-tuple-element.28), channel_id=1, source_target_pairs={{0,2},{1,3},{2,0},{3,1},{4,6},{5,7},{6,4},{7,5},{8,10},{9,11},{10,... | collective-permute-start | bytes 393224 | tf_op jit(solution)/shard_map/ppermute | solution.py:43
  99.8 8.9 %collective-permute-start.12 = (bf16[4,128,128]{2,1,0:T(8,128)(2,1)S(1)}, bf16[4,128,128]{2,1,0:T(8,128)(2,1)S(1)}, u32[]{:S(2)}, u32[]{:S(2)}) collective-permute-start(bf16[4,128,128]{2,1,0:T(8,128)(2,1)S(1)} %get-tuple-element.27), channel_id=1, source_target_pairs={{0,3},{1,0},{2,1},{3,2},{4,7},{5,4},{6,5},{7,6},{8,11},{9,8},{10,9... | collective-permute-start | bytes 393224 | tf_op jit(solution)/shard_map/ppermute | solution.py:43
  101.5 11.6 %collective-permute-start.21 = (bf16[4,128,128]{2,1,0:T(8,128)(2,1)S(1)}, bf16[4,128,128]{2,1,0:T(8,128)(2,1)S(1)}, u32[]{:S(2)}, u32[]{:S(2)}) collective-permute-start(bf16[4,128,128]{2,1,0:T(8,128)(2,1)S(1)} %pad_maximum_fusion.13), channel_id=1, source_target_pairs={{0,12},{1,13},{2,14},{3,15},{4,0},{5,1},{6,2},{7,3},{8,4},{9,5},{1... | collective-permute-start | bytes 393224 | tf_op jit(solution)/shard_map/ppermute | solution.py:43
  103.6 11.0 %copy-start = (bf16[1,256,2432]{2,1,0:T(8,128)(2,1)S(1)}, bf16[1,256,2432]{2,1,0:T(8,128)(2,1)}, u32[]{:S(2)}) copy-start(bf16[1,256,2432]{2,1,0:T(8,128)(2,1)} %param.13) | copy-start | bytes 3735556
  103.7 11.0 %collective-permute-start.22 = (bf16[4,128,128]{2,1,0:T(8,128)(2,1)S(1)}, bf16[4,128,128]{2,1,0:T(8,128)(2,1)S(1)}, u32[]{:S(2)}, u32[]{:S(2)}) collective-permute-start(bf16[4,128,128]{2,1,0:T(8,128)(2,1)S(1)} %pad_maximum_fusion.14), channel_id=1, source_target_pairs={{0,8},{1,9},{2,10},{3,11},{4,12},{5,13},{6,14},{7,15},{8,0},{9,1},... | collective-permute-start | bytes 393224 | tf_op jit(solution)/shard_map/ppermute | solution.py:43
  107.5 7.2 %collective-permute-start.23 = (bf16[4,128,128]{2,1,0:T(8,128)(2,1)S(1)}, bf16[4,128,128]{2,1,0:T(8,128)(2,1)S(1)}, u32[]{:S(2)}, u32[]{:S(2)}) collective-permute-start(bf16[4,128,128]{2,1,0:T(8,128)(2,1)S(1)} %pad_maximum_fusion.15), channel_id=1, source_target_pairs={{0,4},{1,5},{2,6},{3,7},{4,8},{5,9},{6,10},{7,11},{8,12},{9,13},{1... | collective-permute-start | bytes 393224 | tf_op jit(solution)/shard_map/ppermute | solution.py:43
  108.7 9.9 %collective-permute-start.15 = (bf16[4,128,128]{2,1,0:T(8,128)(2,1)S(1)}, bf16[4,128,128]{2,1,0:T(8,128)(2,1)S(1)}, u32[]{:S(2)}, u32[]{:S(2)}) collective-permute-start(bf16[4,128,128]{2,1,0:T(8,128)(2,1)S(1)} %pad_maximum_fusion.9), channel_id=1, source_target_pairs={{0,12},{1,13},{2,14},{3,15},{4,0},{5,1},{6,2},{7,3},{8,4},{9,5},{1... | collective-permute-start | bytes 393224 | tf_op jit(solution)/shard_map/ppermute | solution.py:43
  111.5 7.1 %collective-permute-start.16 = (bf16[4,128,128]{2,1,0:T(8,128)(2,1)S(1)}, bf16[4,128,128]{2,1,0:T(8,128)(2,1)S(1)}, u32[]{:S(2)}, u32[]{:S(2)}) collective-permute-start(bf16[4,128,128]{2,1,0:T(8,128)(2,1)S(1)} %pad_maximum_fusion.10), channel_id=1, source_target_pairs={{0,8},{1,9},{2,10},{3,11},{4,12},{5,13},{6,14},{7,15},{8,0},{9,1},... | collective-permute-start | bytes 393224 | tf_op jit(solution)/shard_map/ppermute | solution.py:43
  113.2 6.3 %collective-permute-start.17 = (bf16[4,128,128]{2,1,0:T(8,128)(2,1)S(1)}, bf16[4,128,128]{2,1,0:T(8,128)(2,1)S(1)}, u32[]{:S(2)}, u32[]{:S(2)}) collective-permute-start(bf16[4,128,128]{2,1,0:T(8,128)(2,1)S(1)} %pad_maximum_fusion.11), channel_id=1, source_target_pairs={{0,4},{1,5},{2,6},{3,7},{4,8},{5,9},{6,10},{7,11},{8,12},{9,13},{1... | collective-permute-start | bytes 393224 | tf_op jit(solution)/shard_map/ppermute | solution.py:43
  117.3 8.3 %collective-permute-start.27 = (f32[128,64]{1,0:T(8,128)S(1)}, f32[128,64]{1,0:T(8,128)S(1)}, u32[]{:S(2)}, u32[]{:S(2)}) collective-permute-start(f32[128,64]{1,0:T(8,128)S(1)} %broadcast_multiply_fusion), channel_id=1, source_target_pairs={{0,16},{16,32},{32,48},{48,64},{64,80},{80,96},{96,112},{1,17},{17... | collective-permute-start | bytes 98312 | tf_op jit(solution)/shard_map/ppermute | solution.py:278
  122.1 17.1 %copy-start.14 = (f32[128,64]{1,0:T(8,128)S(1)}, f32[128,64]{1,0:T(8,128)}, u32[]{:S(2)}) copy-start(f32[128,64]{1,0:T(8,128)} %copy.19) | copy-start | bytes 98308
  122.1 18.9 %copy-start.13 = (f32[128,64]{1,0:T(8,128)S(1)}, f32[128,64]{1,0:T(8,128)}, u32[]{:S(2)}) copy-start(f32[128,64]{1,0:T(8,128)} %copy.18) | copy-start | bytes 98308
  122.1 7.1 %collective-permute-start.24 = (f32[128,64]{1,0:T(8,128)S(1)}, f32[128,64]{1,0:T(8,128)S(1)}, u32[]{:S(2)}, u32[]{:S(2)}) collective-permute-start(f32[128,64]{1,0:T(8,128)S(1)} %broadcast_multiply_fusion.1), channel_id=1, source_target_pairs={{0,16},{16,32},{32,48},{48,64},{64,80},{80,96},{96,112},{1,17},{17... | collective-permute-start | bytes 98312 | tf_op jit(solution)/shard_map/ppermute | solution.py:278
  125.6 6.7 %collective-permute-start.28 = (f32[128,64]{1,0:T(8,128)S(1)}, f32[128,64]{1,0:T(8,128)S(1)}, u32[]{:S(2)}, u32[]{:S(2)}) collective-permute-start(f32[128,64]{1,0:T(8,128)S(1)} %fusion.11), channel_id=1, source_target_pairs={{0,32},{16,48},{32,64},{48,80},{64,96},{80,112},{1,33},{17,49},{33... | collective-permute-start | bytes 98312 | tf_op jit(solution)/shard_map/ppermute | solution.py:278
  129.2 8.2 %collective-permute-start.25 = (f32[128,64]{1,0:T(8,128)S(1)}, f32[128,64]{1,0:T(8,128)S(1)}, u32[]{:S(2)}, u32[]{:S(2)}) collective-permute-start(f32[128,64]{1,0:T(8,128)S(1)} %fusion.10), channel_id=1, source_target_pairs={{0,32},{16,48},{32,64},{48,80},{64,96},{80,112},{1,33},{17,49},{33... | collective-permute-start | bytes 98312 | tf_op jit(solution)/shard_map/ppermute | solution.py:278
  132.4 6.7 %collective-permute-start.29 = (f32[128,64]{1,0:T(8,128)S(1)}, f32[128,64]{1,0:T(8,128)S(1)}, u32[]{:S(2)}, u32[]{:S(2)}) collective-permute-start(f32[128,64]{1,0:T(8,128)S(1)} %add.131), channel_id=1, source_target_pairs={{0,64},{16,80},{32,96},{48,112},{1,65},{17,81},{33,97},{49,113},{2... | collective-permute-start | bytes 98312 | tf_op jit(solution)/shard_map/ppermute | solution.py:278
  137.4 3.6 %collective-permute-start.26 = (f32[128,64]{1,0:T(8,128)S(1)}, f32[128,64]{1,0:T(8,128)S(1)}, u32[]{:S(2)}, u32[]{:S(2)}) collective-permute-start(f32[128,64]{1,0:T(8,128)S(1)} %add.127), channel_id=1, source_target_pairs={{0,64},{16,80},{32,96},{48,112},{1,65},{17,81},{33,97},{49,113},{2... | collective-permute-start | bytes 98312 | tf_op jit(solution)/shard_map/ppermute | solution.py:278
  (2 other events, 2.5 us)

commit v2 on v1

--- a/solution.py
+++ b/solution.py
@@ -17,9 +17,9 @@
 BOTH = ("tm", "seq")
 NT = (((1,), (1,)), ((), ()))
 SCALE = 0.125 * 1.4426950408889634
-KEY_CUTS = ((0, 144), (144, 280))
-PIECES = ((0, 128), (128, 256))
+KEY_CUTS = ((0, 96), (96, 280))
 QROWS = 256
+KROWS = 280
 TILE = 512
 BLOCK_Q = 1024
 VROWS = 128
@@ -60,56 +60,73 @@
     return -(-rows // 16) * 16
 
 
-def pack_kernel(nq, cut, place_ref, *refs):
-    if nq:
-        q_ref, k_ref, v_ref = refs[:3]
-        outs = refs[3:]
-    else:
-        k_ref, v_ref = refs[:2]
-        outs = refs[2:]
-    k0, k1 = cut
-    nk = k1 - k0
-    kp = nq
-    vp = kp + padded(nk)
-    for d in range(RING):
+def layout():
+    at, places = QROWS, []
+    for k0, k1 in KEY_CUTS:
+        places.append((at, at + padded(k1 - k0)))
+        at += 2 * padded(k1 - k0)
+    return places, at
+
+
+def pack_kernel(place_ref, q_hbm, k_hbm, v_hbm, *refs):
+    outs, (q_buf, k_buf, v_buf, sems) = refs[:RING], refs[RING:]
+    places, _ = layout()
+    order = (1, 3, 2, 0)
+    copies = {}
+    for d in order:
         group = lax.rem(place_ref[0] + d, RING)
-        for j in range(RING):
-            lanes = pl.ds(pl.multiple_of(group * (RING * PAIR) + j * PAIR, PAIR), PAIR)
-            out = outs[d]
-            if nq:
-                out[j, 0:nq] = head_norm(q_ref[:, lanes])
-            out[j, kp : kp + nk] = head_norm(k_ref[k0:k1, lanes])
-            out[j, vp : vp + nk] = v_ref[k0:k1, lanes]
-            if vp > kp + nk:
-                out[j, kp + nk : vp] = jnp.zeros((vp - kp - nk, PAIR), jnp.bfloat16)
-
-
-def pack(place, queries, keys, values, nq, cut):
-    nk = cut[1] - cut[0]
-    rows = nq + padded(nk) + nk
-    operands = ([queries] if nq else []) + [keys, values]
+        lanes = pl.ds(pl.multiple_of(group * (RING * PAIR), RING * PAIR), RING * PAIR)
+        copies[d] = [
+            pltpu.make_async_copy(source.at[:, lanes], target.at[d], sems.at[d, n])
+            for n, (source, target) in enumerate(((q_hbm, q_buf), (k_hbm, k_buf), (v_hbm, v_buf)))
+        ]
+        for copy in copies[d]:
+            copy.start()
+    for d in order:
+        for copy in copies[d]:
+            copy.wait()
+        out = outs[d]
+        for e in range(RING):
+            pair = lax.rem(place_ref[1] + e, RING)
+            lanes = pl.ds(pl.multiple_of(pair * PAIR, PAIR), PAIR)
+            out[e, 0:QROWS] = head_norm(q_buf[d, :, lanes])
+            keys = head_norm(k_buf[d, :, lanes])
+            for (k0, k1), (kp, vp) in zip(KEY_CUTS, places):
+                out[e, kp : kp + k1 - k0] = keys[k0:k1]
+                out[e, vp : vp + k1 - k0] = v_buf[d, k0:k1, lanes]
+                gap = padded(k1 - k0) - (k1 - k0)
+                if gap:
+                    out[e, vp - gap : vp] = jnp.zeros((gap, PAIR), jnp.bfloat16)
+                    out[e, vp + k1 - k0 : vp + k1 - k0 + gap] = jnp.zeros((gap, PAIR), jnp.bfloat16)
+
+
+def pack(place, queries, keys, values):
+    _, rows = layout()
     vmem = pl.BlockSpec(memory_space=pltpu.VMEM)
+    wide = RING * PAIR
     return pl.pallas_call(
-        functools.partial(pack_kernel, nq, cut),
-        in_specs=[pl.BlockSpec(memory_space=pltpu.SMEM)] + [vmem] * len(operands),
+        pack_kernel,
+        in_specs=[pl.BlockSpec(memory_space=pltpu.SMEM)] + [pl.BlockSpec(memory_space=pl.ANY)] * 3,
         out_specs=[vmem] * RING,
         out_shape=[jax.ShapeDtypeStruct((RING, rows, PAIR), jnp.bfloat16)] * RING,
-        compiler_params=pltpu.CompilerParams(vmem_limit_bytes=16 * MIB),
+        scratch_shapes=[
+            pltpu.VMEM((RING, QROWS, wide), jnp.bfloat16),
+            pltpu.VMEM((RING, KROWS, wide), jnp.bfloat16),
+            pltpu.VMEM((RING, KROWS, wide), jnp.bfloat16),
+            pltpu.SemaphoreType.DMA((RING, 3)),
+        ],
+        compiler_params=pltpu.CompilerParams(vmem_limit_bytes=24 * MIB),
         cost_estimate=pl.CostEstimate(flops=2 * 2 * rows * HD * PAIR, bytes_accessed=4 * rows * HD, transcendentals=0),
         name="pack",
-    )(place, *operands)
-
-
-def regroup(parts, index):
-    return [
-        jnp.stack([lax.dynamic_index_in_dim(part, lax.rem(index + e, RING), 0, keepdims=False) for part in parts])
-        for e in range(RING)
-    ]
-
-
-def exchange(parts, second):
-    landed = [parts[0]] + [send(parts[d], True, d) for d in range(1, RING)]
-    staged = regroup(landed, second)
+    )(place, queries, keys, values)
+
+
+def first_hop(parts):
+    return [parts[0]] + [send(parts[d], True, d) for d in range(1, RING)]
+
+
+def second_hop(landed, start, stop):
+    staged = [jnp.stack([part[e, start:stop] for part in landed]) for e in range(RING)]
     return [staged[0]] + [send(staged[e], False, e) for e in range(1, RING)]
 
 
@@ -123,7 +140,7 @@
     return [(start, min(step, total - start)) for start in range(0, total, step)]
 
 
-def attend_kernel(nk, kp, rows, first, last, *refs):
+def attend_kernel(nk, kp, vp, first, last, *refs):
     q_refs, refs = refs[:RING], refs[RING:]
     if first:
         kv_refs = q_refs
@@ -135,9 +152,7 @@
     else:
         acc_out, refs = refs[0], refs[1:]
     q_all, k_all, low_t, high_t = refs
-    vp = kp + padded(nk)
-    r0, r1 = rows
-    nr = r1 - r0
+    nr = QROWS
     total = RING * RING * nk
     row = lax.broadcasted_iota(jnp.int32, (PAIR, PAIR), 0)
     col = lax.broadcasted_iota(jnp.int32, (PAIR, PAIR), 1)
@@ -145,10 +160,7 @@
     for e in range(RING):
         for d in range(RING):
             slot = e * RING + d
-            for p0, p1 in PIECES:
-                if r0 <= p0 and p1 <= r1:
-                    base = RING * RING * (p0 - r0) + slot * (p1 - p0)
-                    q_all[base : base + p1 - p0] = q_refs[e][d, p0:p1]
+            q_all[slot * nr : (slot + 1) * nr] = q_refs[e][d, 0:nr]
             k_all[slot * nk : (slot + 1) * nk] = kv_refs[e][d, kp : kp + nk]
     ones = jnp.ones((VROWS - HEAD_DIM, total), jnp.bfloat16)
     low_t[HEAD_DIM:, :] = ones
@@ -185,8 +197,7 @@
             )
         kept = HEAD_DIM + 8
         if not first:
-            qa = pl.multiple_of(RING * RING * r0 + block * BLOCK_Q, BLOCK_Q)
-            sums = [sums[h][:kept] + acc_in[h, :, pl.ds(qa, BLOCK_Q)] for h in range(2)]
+            sums = [sums[h][:kept] + acc_in[h, :, pl.ds(q0, BLOCK_Q)] for h in range(2)]
         if not last:
             for h in range(2):
                 acc_out[h, :, pl.ds(q0, BLOCK_Q)] = sums[h][:kept]
@@ -201,9 +212,9 @@
                 out_refs[e][d] = q_all[slot * nr : (slot + 1) * nr]
 
 
-def attend(q_parts, kv_parts, acc, nk, kp, rows, last):
+def attend(q_parts, kv_parts, acc, nk, kp, vp, last):
     first = acc is None
-    nr = rows[1] - rows[0]
+    nr = QROWS
     nq = RING * RING * nr
     total = RING * RING * nk
     operands = list(q_parts) + ([] if first else list(kv_parts) + [acc])
@@ -213,7 +224,7 @@
     else:
         out_shape = [jax.ShapeDtypeStruct((2, HEAD_DIM + 8, nq), jnp.float32)]
     return pl.pallas_call(
-        functools.partial(attend_kernel, nk, kp, rows, first, last),
+        functools.partial(attend_kernel, nk, kp, vp, first, last),
         in_specs=[vmem] * len(operands),
         out_specs=[vmem] * len(out_shape),
         out_shape=out_shape,
@@ -231,35 +242,40 @@
     )(*operands)
 
 
-def project_kernel(rows, place_ref, level_ref, *refs):
+def project_kernel(place_ref, level_ref, *refs):
     parts, refs = refs[:RING], refs[RING:]
-    hidden_ref, w_proj_ref, w_final_ref, base_ref, slope_ref, out_ref, joined, gated = refs
-    r0, r1 = rows
+    hidden_ref, w_proj_ref, w_final_ref, base_ref, slope_ref, out_ref, drift_ref, joined, gated = refs
     for d in range(RING):
         for e in range(RING):
             pair = lax.rem(place_ref[0] + d, RING) * RING + lax.rem(place_ref[1] + e, RING)
             joined[:, pl.ds(pl.multiple_of(pair * PAIR, PAIR), PAIR)] = parts[d][e]
-    squares = jnp.zeros((r1 - r0, 1), jnp.float32)
+    squares = jnp.zeros((QROWS, 1), jnp.float32)
     for start, size in cuts_of(D, 512):
         cols = slice(start, start + size)
         projected = jnp.dot(joined[...], w_proj_ref[:, cols], preferred_element_type=jnp.float32)
         gate = base_ref[:, cols] + level_ref[0] * slope_ref[:, cols]
-        value = hidden_ref[r0:r1, cols].astype(jnp.float32) + gate * projected
+        value = hidden_ref[:, cols].astype(jnp.float32) + gate * projected
         gated[:, cols] = value
         squares = squares + jnp.sum(value * value, axis=1, keepdims=True)
     normed = (gated[...] * lax.rsqrt(squares * (1.0 / D) + 1e-06)).astype(jnp.bfloat16)
-    out_ref[...] = jnp.dot(normed, w_final_ref[...], preferred_element_type=jnp.float32)
-
-
-def project(place, level, parts, hidden, w_proj, w_final, base, slope, rows):
-    nr = rows[1] - rows[0]
+    velocity = jnp.dot(normed, w_final_ref[...], preferred_element_type=jnp.float32)
+    out_ref[...] = velocity
+    half = QROWS // 2
+    drift_ref[...] = jnp.concatenate([velocity[:half], velocity[half:]], axis=1) * level_ref[1]
+
+
+def project(place, level, parts, hidden, w_proj, w_final, base, slope):
+    nr = QROWS
     vmem = pl.BlockSpec(memory_space=pltpu.VMEM)
     smem = pl.BlockSpec(memory_space=pltpu.SMEM)
     return pl.pallas_call(
-        functools.partial(project_kernel, rows),
+        project_kernel,
         in_specs=[smem, smem] + [vmem] * (RING + 5),
-        out_specs=vmem,
-        out_shape=jax.ShapeDtypeStruct((nr, LAT), jnp.float32),
+        out_specs=[vmem, vmem],
+        out_shape=[
+            jax.ShapeDtypeStruct((nr, LAT), jnp.float32),
+            jax.ShapeDtypeStruct((nr // 2, 2 * LAT), jnp.float32),
+        ],
         scratch_shapes=[pltpu.VMEM((nr, HD), jnp.bfloat16), pltpu.VMEM((nr, D), jnp.float32)],
         compiler_params=pltpu.CompilerParams(vmem_limit_bytes=32 * MIB),
         cost_estimate=pl.CostEstimate(flops=2 * nr * HD * D, bytes_accessed=12 * MIB, transcendentals=0),
@@ -275,7 +291,9 @@
 def running_sum(drift, slots):
     shift = 1
     while shift < slots:
-        drift = drift + lax.ppermute(drift, "tm", [(i, i + shift) for i in range(slots - shift)])
+        drift = drift + lax.ppermute(drift.astype(jnp.bfloat16), "tm", [(i, i + shift) for i in range(slots - shift)]).astype(
+            jnp.float32
+        )
         shift *= 2
     return drift
 
@@ -292,31 +310,25 @@
     place = jnp.stack([first, second]).astype(jnp.int32)
     sigma_now = sigma_of(window_steps[slot], 2 * slots)
     step_size = sigma_of(window_steps[slot + 1], 2 * slots) - sigma_now
-    level = sigma_now.reshape(1)
-
-    received = []
-    for number, cut in enumerate(KEY_CUTS):
-        parts = pack(place, queries[0], keys[0], values[0], QROWS if number == 0 else 0, cut)
-        received.append(exchange(parts, second))
-    q_parts = received[0]
+    level = jnp.stack([sigma_now, step_size])
+
+    places, end = layout()
+    starts = [0] + [kp for kp, _ in places[1:]] + [end]
+    landed = first_hop(pack(place, queries[0], keys[0], values[0]))
+    received = [second_hop(landed, start, stop) for start, stop in zip(starts, starts[1:])]
     acc = None
-    outs = []
-    for number, cut in enumerate(KEY_CUTS):
-        nk = cut[1] - cut[0]
-        kp = QROWS if number == 0 else 0
-        if number < len(KEY_CUTS) - 1:
-            (acc,) = attend(q_parts, received[number], acc, nk, kp, (0, QROWS), False)
-        else:
-            outs = [attend(q_parts, received[number], acc, nk, kp, rows, True) for rows in PIECES]
-    velocities, latents = [], []
-    for rows, blocks in zip(PIECES, outs):
-        back = give_back(blocks)
-        velocity = project(
-            place, level, back, hidden[0], w_proj, w_final, gate_base[None], gate_slope[None], rows
-        )
-        velocities.append(velocity)
-        latents.append(start_latent[rows[0] : rows[1]] + running_sum(step_size * velocity, slots))
-    return (jnp.concatenate(velocities)[None], jnp.concatenate(latents)[None])
+    for number, ((k0, k1), (kp, vp)) in enumerate(zip(KEY_CUTS, places)):
+        start = starts[number]
+        last = number == len(KEY_CUTS) - 1
+        got = attend(received[0], received[number], acc, k1 - k0, kp - start, vp - start, last)
+        acc = None if last else got[0]
+    velocity, drift = project(
+        place, level, give_back(got), hidden[0], w_proj, w_final, gate_base[None], gate_slope[None]
+    )
+    drift = running_sum(drift, slots)
+    half = QROWS // 2
+    latents = start_latent + jnp.concatenate([drift[:, :LAT], drift[:, LAT:]], axis=0)
+    return (velocity[None], latents[None])
 
 
 def solution(mesh):

time: 143 us -> 137 us (0.958); the launches traced: 142 us -> 134 us
  waiting for transfers between devices: 25.6 us -> 43.5 us
  starting transfers between devices: 52.8 us -> 36 us
  local copies, waits for them, and re-layouts: 18.4 us -> 10.5 us
  Pallas kernels: 41.6 us -> 39.6 us
    ppermute x24 -> x15, waiting for transfers between devices: 23.7 us -> 40.3 us  [send(): return lax.ppermute(value, BOTH, ring_perm(first, shift % RING))]
    ppermute x24 -> x15, starting transfers between devices: 35.3 us -> 22.3 us  [send(): return lax.ppermute(value, BOTH, ring_perm(first, shift % RING))]
    dynamic_slice x9 -> x1, local copies, waits for them, and re-layouts: 7.5 us -> 0.59 us  [per_device(): sigma_now = sigma_of(window_steps[slot], 2 * slots)]
    ppermute x6 -> x3, starting transfers between devices: 17.4 us -> 13.7 us  [running_sum(): lax.ppermute(drift.astype(jnp.bfloat16), 'tm', [(i, i + shift) for i in r...]
    pallas_call x7 -> x4, Pallas kernels: 41.6 us -> 39.6 us  [the longest x2 32.2 us: attend(): pl.pallas_call(functools.partial(attend_kernel, nk, kp, vp, first, last),...]
    ppermute x6 -> x3, waiting for transfers between devices: 1.86 us -> 3.17 us  [running_sum(): lax.ppermute(drift.astype(jnp.bfloat16), 'tm', [(i, i + shift) for i in r...]
    unnamed x45 -> x24, local copies, waits for them, and re-layouts: 8.74 us -> 9.46 us
  transfers between devices with their start and end apart: 30 -> 18, of which waited for: 8 -> 13; matrix products, arithmetic and copies ran while one was open for 10% -> 3% of each run, Pallas kernels for 22% -> 8%
where the time goes in v2:
time: 137 us; the launch traced here: 134 us
  waiting for transfers between devices  43.5 us (32%)
  Pallas kernels  39.6 us (29%)
  starting transfers between devices  36 us (26%)
  local copies, waits for them, and re-layouts  10.5 us (8%)
  between operations  2.4 us (2%)
  other arithmetic  2.22 us (2%)
    ppermute x15, waiting for transfers between devices, send(): return lax.ppermute(value, BOTH, ring_perm(first, shift % RING))  40.3 us
    pallas_call x2, Pallas kernels, attend(): pl.pallas_call(functools.partial(attend_kernel, nk, kp, vp, first, last),...  32.2 us
    ppermute x15, starting transfers between devices, send(): return lax.ppermute(value, BOTH, ring_perm(first, shift % RING))  22.3 us
    ppermute x3, starting transfers between devices, running_sum(): lax.ppermute(drift.astype(jnp.bfloat16), 'tm', [(i, i + shift) for i in r...  13.7 us
    unnamed x24, local copies, waits for them, and re-layouts  9.46 us
    pallas_call x1, Pallas kernels, project(): pl.pallas_call(project_kernel, in_specs=[smem, smem] + [vmem] * (RING + 5...  4.42 us
    ppermute x3, waiting for transfers between devices, running_sum(): lax.ppermute(drift.astype(jnp.bfloat16), 'tm', [(i, i + shift) for i in r...  3.17 us
    pallas_call x1, Pallas kernels, pack(): pl.pallas_call(pack_kernel, in_specs=[pl.BlockSpec(memory_space=pltpu.SME...  2.98 us
  transfers between devices with their start and end apart: 18, of which 13 were waited for; matrix products, arithmetic and copies ran while one was open for 3% of the time, Pallas kernels for 8%

profile of v2, /device:TPU:0, one launch (start us, length us, event | category | flops | bytes accessed | tf_op | source)
XLA Modules:
  0.0 134.2 jit_solution(11935676653139298115)
XLA Ops:
  0.7 0.1 pad_add_fusion.place_ref
  0.7 1.3 copy-done.2
  2.0 1.3 copy-done.3
  3.2 1.2 copy-done.4
  4.5 3.0 %pack.1 = (bf16[4,832,128]{2,1,0:T(8,128)(2,1)S(1)}, bf16[4,832,128]{2,1,0:T(8,128)(2,1)S(1)}, bf16[4,832,128]{2,1,0:T(8,128)(2,1)S(1)}, bf16[4,832,128]{2,1,0:T(8,128)(2,1)S(1)}) custom-call(s32[2]{0:T(128)S(1)} %pad_add_fusion.place_ref, bf16[256,2048]{1,0:T(8,128)(2,1)S(1)} %bitcast.12, bf16[280,2048]{1,0:T(8,128)(2,1)S(1)} %bitcast.10, ...), custom_call_target="tpu_custom_call" | custom-call | flops 872415232 | bytes 6815744 | tf_op jit(solution)/shard_map/pack/pallas_call | solution.py:107
  7.5 2.9 %collective-permute-start.2 = (bf16[4,832,128]{2,1,0:T(8,128)(2,1)S(1)}, bf16[4,832,128]{2,1,0:T(8,128)(2,1)S(1)}, u32[]{:S(2)}, u32[]{:S(2)}) collective-permute-start(bf16[4,832,128]{2,1,0:T(8,128)(2,1)S(1)} %get-tuple-element.15), channel_id=1, source_target_pairs={{0,12},{1,13},{2,14},{3,15},{4,0},{5,1},{6,2},{7,3},{8,4},{9,5},{1... | collective-permute-start | bytes 2555912 | tf_op jit(solution)/shard_map/ppermute | solution.py:43
  10.4 0.8 collective-permute-start.1
  11.2 0.9 collective-permute-start
  12.1 17.6 %collective-permute-done.2 = bf16[4,832,128]{2,1,0:T(8,128)(2,1)S(1)} collective-permute-done((bf16[4,832,128]{2,1,0:T(8,128)(2,1)S(1)}, bf16[4,832,128]{2,1,0:T(8,128)(2,1)S(1)}, u32[]{:S(2)}, u32[]{:S(2)}) %collective-permute-start.2) | collective-permute-done | bytes 852000 | tf_op jit(solution)/shard_map/ppermute | solution.py:43
  29.8 3.9 %collective-permute-done = bf16[4,832,128]{2,1,0:T(8,128)(2,1)S(1)} collective-permute-done((bf16[4,832,128]{2,1,0:T(8,128)(2,1)S(1)}, bf16[4,832,128]{2,1,0:T(8,128)(2,1)S(1)}, u32[]{:S(2)}, u32[]{:S(2)}) %collective-permute-start) | collective-permute-done | bytes 852000 | tf_op jit(solution)/shard_map/ppermute | solution.py:43
  33.8 2.0 %collective-permute-start.3 = (bf16[4,448,128]{2,1,0:T(8,128)(2,1)S(1)}, bf16[4,448,128]{2,1,0:T(8,128)(2,1)S(1)}, u32[]{:S(2)}, u32[]{:S(2)}) collective-permute-start(bf16[4,448,128]{2,1,0:T(8,128)(2,1)S(1)} %pad_maximum_fusion.1), channel_id=1, source_target_pairs={{0,1},{1,2},{2,3},{3,0},{4,5},{5,6},{6,7},{7,4},{8,9},{9,10},{10,1... | collective-permute-start | bytes 1376264 | tf_op jit(solution)/shard_map/ppermute | solution.py:43
  35.8 3.7 %collective-permute-start.4 = (bf16[4,448,128]{2,1,0:T(8,128)(2,1)S(1)}, bf16[4,448,128]{2,1,0:T(8,128)(2,1)S(1)}, u32[]{:S(2)}, u32[]{:S(2)}) collective-permute-start(bf16[4,448,128]{2,1,0:T(8,128)(2,1)S(1)} %pad_maximum_fusion.2), channel_id=1, source_target_pairs={{0,2},{1,3},{2,0},{3,1},{4,6},{5,7},{6,4},{7,5},{8,10},{9,11},{10,... | collective-permute-start | bytes 1376264 | tf_op jit(solution)/shard_map/ppermute | solution.py:43
  39.6 1.1 collective-permute-start.5
  40.8 1.1 collective-permute-start.6
  42.0 0.5 collective-permute-start.7
  42.7 1.7 %collective-permute-done.3.refs_1_ = bf16[4,448,128]{2,1,0:T(8,128)(2,1)S(1)} collective-permute-done((bf16[4,448,128]{2,1,0:T(8,128)(2,1)S(1)}, bf16[4,448,128]{2,1,0:T(8,128)(2,1)S(1)}, u32[]{:S(2)}, u32[]{:S(2)}) %collective-permute-start.3) | collective-permute-done | bytes 458784 | tf_op jit(solution)/shard_map/ppermute | solution.py:43
  44.4 2.0 %collective-permute-start.8 = (bf16[4,384,128]{2,1,0:T(8,128)(2,1)S(1)}, bf16[4,384,128]{2,1,0:T(8,128)(2,1)S(1)}, u32[]{:S(2)}, u32[]{:S(2)}) collective-permute-start(bf16[4,384,128]{2,1,0:T(8,128)(2,1)S(1)} %pad_maximum_fusion.7), channel_id=1, source_target_pairs={{0,3},{1,0},{2,1},{3,2},{4,7},{5,4},{6,5},{7,6},{8,11},{9,8},{10,9... | collective-permute-start | bytes 1179656 | tf_op jit(solution)/shard_map/ppermute | solution.py:43
  46.4 4.5 %collective-permute-done.4.refs_2_ = bf16[4,448,128]{2,1,0:T(8,128)(2,1)S(1)} collective-permute-done((bf16[4,448,128]{2,1,0:T(8,128)(2,1)S(1)}, bf16[4,448,128]{2,1,0:T(8,128)(2,1)S(1)}, u32[]{:S(2)}, u32[]{:S(2)}) %collective-permute-start.4) | collective-permute-done | bytes 458784 | tf_op jit(solution)/shard_map/ppermute | solution.py:43
  50.8 11.0 %attend.2.refs_8_ = f32[2,72,4096]{2,1,0:T(8,128)S(1)} custom-call(bf16[4,448,128]{2,1,0:T(8,128)(2,1)S(1)} %pad_maximum_fusion.refs_0_, bf16[4,448,128]{2,1,0:T(8,128)(2,1)S(1)} %collective-permute-done.3.refs_1_, bf16[4,448,128]{2,1,0:T(8,128)(2,1)S(1)} %collective-permute-done.4.refs_2_, bf16[4,448,128]{2,1,0:T(8,128)(2,1)S(1)} %collective-permute-done.5.refs_3_), custom_call_target="tpu_custom_call" | custom-call | flops 12884901888 | bytes 2097152 | tf_op jit(solution)/shard_map/attend/pallas_call | solution.py:226
  61.9 21.2 %attend.3 = (bf16[4,256,128]{2,1,0:T(8,128)(2,1)S(1)}, bf16[4,256,128]{2,1,0:T(8,128)(2,1)S(1)}, bf16[4,256,128]{2,1,0:T(8,128)(2,1)S(1)}, bf16[4,256,128]{2,1,0:T(8,128)(2,1)S(1)}) custom-call(bf16[4,448,128]{2,1,0:T(8,128)(2,1)S(1)} %pad_maximum_fusion.refs_0_, bf16[4,448,128]{2,1,0:T(8,128)(2,1)S(1)} %collective-permute-done.3.refs_1_, ...), custom_call_target="tpu_custom_call" | custom-call | flops 24696061952 | bytes 2097152 | tf_op jit(solution)/shard_map/attend/pallas_call | solution.py:226
  83.1 1.7 %collective-permute-start.11 = (bf16[4,256,128]{2,1,0:T(8,128)(2,1)S(1)}, bf16[4,256,128]{2,1,0:T(8,128)(2,1)S(1)}, u32[]{:S(2)}, u32[]{:S(2)}) collective-permute-start(bf16[4,256,128]{2,1,0:T(8,128)(2,1)S(1)} %get-tuple-element.19), channel_id=1, source_target_pairs={{0,1},{1,2},{2,3},{3,0},{4,5},{5,6},{6,7},{7,4},{8,9},{9,10},{10,1... | collective-permute-start | bytes 786440 | tf_op jit(solution)/shard_map/ppermute | solution.py:43
  84.8 2.0 %collective-permute-start.10 = (bf16[4,256,128]{2,1,0:T(8,128)(2,1)S(1)}, bf16[4,256,128]{2,1,0:T(8,128)(2,1)S(1)}, u32[]{:S(2)}, u32[]{:S(2)}) collective-permute-start(bf16[4,256,128]{2,1,0:T(8,128)(2,1)S(1)} %get-tuple-element.18), channel_id=1, source_target_pairs={{0,2},{1,3},{2,0},{3,1},{4,6},{5,7},{6,4},{7,5},{8,10},{9,11},{10,... | collective-permute-start | bytes 786440 | tf_op jit(solution)/shard_map/ppermute | solution.py:43
  86.7 1.6 %collective-permute-start.9 = (bf16[4,256,128]{2,1,0:T(8,128)(2,1)S(1)}, bf16[4,256,128]{2,1,0:T(8,128)(2,1)S(1)}, u32[]{:S(2)}, u32[]{:S(2)}) collective-permute-start(bf16[4,256,128]{2,1,0:T(8,128)(2,1)S(1)} %get-tuple-element.17), channel_id=1, source_target_pairs={{0,3},{1,0},{2,1},{3,2},{4,7},{5,4},{6,5},{7,6},{8,11},{9,8},{10,9... | collective-permute-start | bytes 786440 | tf_op jit(solution)/shard_map/ppermute | solution.py:43
  88.4 2.4 %collective-permute-done.11 = bf16[4,256,128]{2,1,0:T(8,128)(2,1)S(1)} collective-permute-done((bf16[4,256,128]{2,1,0:T(8,128)(2,1)S(1)}, bf16[4,256,128]{2,1,0:T(8,128)(2,1)S(1)}, u32[]{:S(2)}, u32[]{:S(2)}) %collective-permute-start.11) | collective-permute-done | bytes 262176 | tf_op jit(solution)/shard_map/ppermute | solution.py:43
  90.8 3.1 %collective-permute-done.10 = bf16[4,256,128]{2,1,0:T(8,128)(2,1)S(1)} collective-permute-done((bf16[4,256,128]{2,1,0:T(8,128)(2,1)S(1)}, bf16[4,256,128]{2,1,0:T(8,128)(2,1)S(1)}, u32[]{:S(2)}, u32[]{:S(2)}) %collective-permute-start.10) | collective-permute-done | bytes 262176 | tf_op jit(solution)/shard_map/ppermute | solution.py:43
  93.9 1.6 %collective-permute-done.9 = bf16[4,256,128]{2,1,0:T(8,128)(2,1)S(1)} collective-permute-done((bf16[4,256,128]{2,1,0:T(8,128)(2,1)S(1)}, bf16[4,256,128]{2,1,0:T(8,128)(2,1)S(1)}, u32[]{:S(2)}, u32[]{:S(2)}) %collective-permute-start.9) | collective-permute-done | bytes 262176 | tf_op jit(solution)/shard_map/ppermute | solution.py:43
  95.7 0.7 pad_maximum_fusion.10
  96.4 0.3 collective-permute-start.13
  96.7 0.7 pad_maximum_fusion.11
  97.5 1.7 %collective-permute-start.14 = (bf16[4,256,128]{2,1,0:T(8,128)(2,1)}, bf16[4,256,128]{2,1,0:T(8,128)(2,1)S(1)}, u32[]{:S(2)}, u32[]{:S(2)}) collective-permute-start(bf16[4,256,128]{2,1,0:T(8,128)(2,1)} %pad_maximum_fusion.11), channel_id=1, source_target_pairs={{0,4},{1,5},{2,6},{3,7},{4,8},{5,9},{6,10},{7,11},{8,12},{9,13},{1... | collective-permute-start | bytes 786440 | tf_op jit(solution)/shard_map/ppermute | solution.py:43
  99.2 0.6 fusion.16
  101.1 0.3 copy.12.refs_6_
  101.5 0.1 pad_maximum_fusion.12.level_ref
  101.7 0.4 collective-permute-done.12.refs_1_
  102.0 2.6 %collective-permute-done.13.refs_2_ = bf16[4,256,128]{2,1,0:T(8,128)(2,1)S(1)} collective-permute-done((bf16[4,256,128]{2,1,0:T(8,128)(2,1)}, bf16[4,256,128]{2,1,0:T(8,128)(2,1)S(1)}, u32[]{:S(2)}, u32[]{:S(2)}) %collective-permute-start.13) | collective-permute-done | bytes 262176 | tf_op jit(solution)/shard_map/ppermute | solution.py:43
  104.6 2.7 %collective-permute-done.14.refs_3_ = bf16[4,256,128]{2,1,0:T(8,128)(2,1)S(1)} collective-permute-done((bf16[4,256,128]{2,1,0:T(8,128)(2,1)}, bf16[4,256,128]{2,1,0:T(8,128)(2,1)S(1)}, u32[]{:S(2)}, u32[]{:S(2)}) %collective-permute-start.14) | collective-permute-done | bytes 262176 | tf_op jit(solution)/shard_map/ppermute | solution.py:43
  107.3 3.8 %copy-done = bf16[2048,2432]{1,0:T(8,128)(2,1)S(1)} copy-done((bf16[2048,2432]{1,0:T(8,128)(2,1)S(1)}, bf16[2048,2432]{1,0:T(8,128)(2,1)}, u32[]{:S(2)}) %copy-start) | copy-done | bytes 9961496
  111.1 4.4 %project.1 = (f32[256,64]{1,0:T(8,128)S(1)}, f32[128,128]{1,0:T(8,128)S(1)}) custom-call(s32[2]{0:T(128)S(1)} %pad_add_fusion.place_ref, f32[2]{0:T(128)S(1)} %pad_maximum_fusion.12.level_ref, bf16[4,256,128]{2,1,0:T(8,128)(2,1)S(1)} %pad_maximum_fusion.8.refs_0_, bf16[4,256,128]{2,1,0:T(8,128)(2,1)S(1)} %collective-permute-done.12.refs_1_, ...), custom_call_target="tpu_custom_call" | custom-call | flops 2550136832 | bytes 12582912 | tf_op jit(solution)/shard_map/project/pallas_call | solution.py:271
  115.6 1.3 collective-permute-start.15
  116.9 0.8 collective-permute-done.15
  117.7 6.6 %collective-permute-start.16 = (bf16[128,128]{1,0:T(8,128)(2,1)S(1)}, bf16[128,128]{1,0:T(8,128)(2,1)S(1)}, u32[]{:S(2)}, u32[]{:S(2)}) collective-permute-start(bf16[128,128]{1,0:T(8,128)(2,1)S(1)} %fusion.1), channel_id=1, source_target_pairs={{0,32},{16,48},{32,64},{48,80},{64,96},{80,112},{1,33},{17,49},{33... | collective-permute-start | bytes 98312 | tf_op jit(solution)/shard_map/ppermute | solution.py:294
  124.3 1.6 %collective-permute-done.16 = bf16[128,128]{1,0:T(8,128)(2,1)S(1)} collective-permute-done((bf16[128,128]{1,0:T(8,128)(2,1)S(1)}, bf16[128,128]{1,0:T(8,128)(2,1)S(1)}, u32[]{:S(2)}, u32[]{:S(2)}) %collective-permute-start.16) | collective-permute-done | bytes 32800 | tf_op jit(solution)/shard_map/ppermute | solution.py:294
  125.9 5.8 %collective-permute-start.17 = (bf16[128,128]{1,0:T(8,128)(2,1)S(1)}, bf16[128,128]{1,0:T(8,128)(2,1)S(1)}, u32[]{:S(2)}, u32[]{:S(2)}) collective-permute-start(bf16[128,128]{1,0:T(8,128)(2,1)S(1)} %fusion.2), channel_id=1, source_target_pairs={{0,64},{16,80},{32,96},{48,112},{1,65},{17,81},{33,97},{49,113},{2... | collective-permute-start | bytes 98312 | tf_op jit(solution)/shard_map/ppermute | solution.py:294
  131.8 0.1 copy.13
  131.8 0.7 copy.14
  132.6 0.8 collective-permute-done.17
  133.3 0.1 fusion.15
  133.5 0.7 copy.15
  (51 shorter events, 1.0 us)
Async XLA Ops:
  0.7 1.3 copy-start.2
  2.0 1.3 copy-start.3
  3.2 1.2 copy-start.4
  7.5 22.2 %collective-permute-start.2 = (bf16[4,832,128]{2,1,0:T(8,128)(2,1)S(1)}, bf16[4,832,128]{2,1,0:T(8,128)(2,1)S(1)}, u32[]{:S(2)}, u32[]{:S(2)}) collective-permute-start(bf16[4,832,128]{2,1,0:T(8,128)(2,1)S(1)} %get-tuple-element.15), channel_id=1, source_target_pairs={{0,12},{1,13},{2,14},{3,15},{4,0},{5,1},{6,2},{7,3},{8,4},{9,5},{1... | collective-permute-start | bytes 2555912 | tf_op jit(solution)/shard_map/ppermute | solution.py:43
  10.4 19.4 %collective-permute-start.1 = (bf16[4,832,128]{2,1,0:T(8,128)(2,1)S(1)}, bf16[4,832,128]{2,1,0:T(8,128)(2,1)S(1)}, u32[]{:S(2)}, u32[]{:S(2)}) collective-permute-start(bf16[4,832,128]{2,1,0:T(8,128)(2,1)S(1)} %get-tuple-element.14), channel_id=1, source_target_pairs={{0,8},{1,9},{2,10},{3,11},{4,12},{5,13},{6,14},{7,15},{8,0},{9,1},... | collective-permute-start | bytes 2555912 | tf_op jit(solution)/shard_map/ppermute | solution.py:43
  11.2 22.5 %collective-permute-start = (bf16[4,832,128]{2,1,0:T(8,128)(2,1)S(1)}, bf16[4,832,128]{2,1,0:T(8,128)(2,1)S(1)}, u32[]{:S(2)}, u32[]{:S(2)}) collective-permute-start(bf16[4,832,128]{2,1,0:T(8,128)(2,1)S(1)} %get-tuple-element.13), channel_id=1, source_target_pairs={{0,4},{1,5},{2,6},{3,7},{4,8},{5,9},{6,10},{7,11},{8,12},{9,13},{1... | collective-permute-start | bytes 2555912 | tf_op jit(solution)/shard_map/ppermute | solution.py:43
  33.8 10.6 %collective-permute-start.3 = (bf16[4,448,128]{2,1,0:T(8,128)(2,1)S(1)}, bf16[4,448,128]{2,1,0:T(8,128)(2,1)S(1)}, u32[]{:S(2)}, u32[]{:S(2)}) collective-permute-start(bf16[4,448,128]{2,1,0:T(8,128)(2,1)S(1)} %pad_maximum_fusion.1), channel_id=1, source_target_pairs={{0,1},{1,2},{2,3},{3,0},{4,5},{5,6},{6,7},{7,4},{8,9},{9,10},{10,1... | collective-permute-start | bytes 1376264 | tf_op jit(solution)/shard_map/ppermute | solution.py:43
  35.8 15.0 %collective-permute-start.4 = (bf16[4,448,128]{2,1,0:T(8,128)(2,1)S(1)}, bf16[4,448,128]{2,1,0:T(8,128)(2,1)S(1)}, u32[]{:S(2)}, u32[]{:S(2)}) collective-permute-start(bf16[4,448,128]{2,1,0:T(8,128)(2,1)S(1)} %pad_maximum_fusion.2), channel_id=1, source_target_pairs={{0,2},{1,3},{2,0},{3,1},{4,6},{5,7},{6,4},{7,5},{8,10},{9,11},{10,... | collective-permute-start | bytes 1376264 | tf_op jit(solution)/shard_map/ppermute | solution.py:43
  39.6 11.3 %collective-permute-start.5 = (bf16[4,448,128]{2,1,0:T(8,128)(2,1)S(1)}, bf16[4,448,128]{2,1,0:T(8,128)(2,1)S(1)}, u32[]{:S(2)}, u32[]{:S(2)}) collective-permute-start(bf16[4,448,128]{2,1,0:T(8,128)(2,1)S(1)} %pad_maximum_fusion.3), channel_id=1, source_target_pairs={{0,3},{1,0},{2,1},{3,2},{4,7},{5,4},{6,5},{7,6},{8,11},{9,8},{10,9... | collective-permute-start | bytes 1376264 | tf_op jit(solution)/shard_map/ppermute | solution.py:43
  40.8 21.1 %collective-permute-start.6 = (bf16[4,384,128]{2,1,0:T(8,128)(2,1)S(1)}, bf16[4,384,128]{2,1,0:T(8,128)(2,1)S(1)}, u32[]{:S(2)}, u32[]{:S(2)}) collective-permute-start(bf16[4,384,128]{2,1,0:T(8,128)(2,1)S(1)} %pad_maximum_fusion.5), channel_id=1, source_target_pairs={{0,1},{1,2},{2,3},{3,0},{4,5},{5,6},{6,7},{7,4},{8,9},{9,10},{10,1... | collective-permute-start | bytes 1179656 | tf_op jit(solution)/shard_map/ppermute | solution.py:43
  42.0 19.9 %collective-permute-start.7 = (bf16[4,384,128]{2,1,0:T(8,128)(2,1)S(1)}, bf16[4,384,128]{2,1,0:T(8,128)(2,1)S(1)}, u32[]{:S(2)}, u32[]{:S(2)}) collective-permute-start(bf16[4,384,128]{2,1,0:T(8,128)(2,1)S(1)} %pad_maximum_fusion.6), channel_id=1, source_target_pairs={{0,2},{1,3},{2,0},{3,1},{4,6},{5,7},{6,4},{7,5},{8,10},{9,11},{10,... | collective-permute-start | bytes 1179656 | tf_op jit(solution)/shard_map/ppermute | solution.py:43
  44.4 17.5 %collective-permute-start.8 = (bf16[4,384,128]{2,1,0:T(8,128)(2,1)S(1)}, bf16[4,384,128]{2,1,0:T(8,128)(2,1)S(1)}, u32[]{:S(2)}, u32[]{:S(2)}) collective-permute-start(bf16[4,384,128]{2,1,0:T(8,128)(2,1)S(1)} %pad_maximum_fusion.7), channel_id=1, source_target_pairs={{0,3},{1,0},{2,1},{3,2},{4,7},{5,4},{6,5},{7,6},{8,11},{9,8},{10,9... | collective-permute-start | bytes 1179656 | tf_op jit(solution)/shard_map/ppermute | solution.py:43
  83.1 7.7 %collective-permute-start.11 = (bf16[4,256,128]{2,1,0:T(8,128)(2,1)S(1)}, bf16[4,256,128]{2,1,0:T(8,128)(2,1)S(1)}, u32[]{:S(2)}, u32[]{:S(2)}) collective-permute-start(bf16[4,256,128]{2,1,0:T(8,128)(2,1)S(1)} %get-tuple-element.19), channel_id=1, source_target_pairs={{0,1},{1,2},{2,3},{3,0},{4,5},{5,6},{6,7},{7,4},{8,9},{9,10},{10,1... | collective-permute-start | bytes 786440 | tf_op jit(solution)/shard_map/ppermute | solution.py:43
  84.8 9.1 %collective-permute-start.10 = (bf16[4,256,128]{2,1,0:T(8,128)(2,1)S(1)}, bf16[4,256,128]{2,1,0:T(8,128)(2,1)S(1)}, u32[]{:S(2)}, u32[]{:S(2)}) collective-permute-start(bf16[4,256,128]{2,1,0:T(8,128)(2,1)S(1)} %get-tuple-element.18), channel_id=1, source_target_pairs={{0,2},{1,3},{2,0},{3,1},{4,6},{5,7},{6,4},{7,5},{8,10},{9,11},{10,... | collective-permute-start | bytes 786440 | tf_op jit(solution)/shard_map/ppermute | solution.py:43
  86.7 8.7 %collective-permute-start.9 = (bf16[4,256,128]{2,1,0:T(8,128)(2,1)S(1)}, bf16[4,256,128]{2,1,0:T(8,128)(2,1)S(1)}, u32[]{:S(2)}, u32[]{:S(2)}) collective-permute-start(bf16[4,256,128]{2,1,0:T(8,128)(2,1)S(1)} %get-tuple-element.17), channel_id=1, source_target_pairs={{0,3},{1,0},{2,1},{3,2},{4,7},{5,4},{6,5},{7,6},{8,11},{9,8},{10,9... | collective-permute-start | bytes 786440 | tf_op jit(solution)/shard_map/ppermute | solution.py:43
  90.8 8.4 %copy-start.9 = (s32[9]{0:T(128)S(1)}, s32[9]{0:T(128)}, u32[]{:S(2)}) copy-start(s32[9]{0:T(128)} %param.19) | copy-start | bytes 112
  90.8 10.3 %copy-start.5 = (bf16[2432,64]{0,1:T(8,128)(2,1)S(1)}, bf16[2432,64]{0,1:T(8,128)(2,1)}, u32[]{:S(2)}) copy-start(bf16[2432,64]{0,1:T(8,128)(2,1)} %param.15) | copy-start | bytes 933892
  95.5 5.9 %copy-start.7 = (f32[2432]{0:T(1024)S(1)}, f32[2432]{0:T(1024)}, u32[]{:S(2)}) copy-start(f32[2432]{0:T(1024)} %param.16) | copy-start | bytes 29188
  95.5 5.9 %copy-start.8 = (f32[2432]{0:T(1024)S(1)}, f32[2432]{0:T(1024)}, u32[]{:S(2)}) copy-start(f32[2432]{0:T(1024)} %param.17) | copy-start | bytes 29188
  95.6 6.4 %collective-permute-start.12 = (bf16[4,256,128]{2,1,0:T(8,128)(2,1)S(1)}, bf16[4,256,128]{2,1,0:T(8,128)(2,1)S(1)}, u32[]{:S(2)}, u32[]{:S(2)}) collective-permute-start(bf16[4,256,128]{2,1,0:T(8,128)(2,1)S(1)} %pad_maximum_fusion.9), channel_id=1, source_target_pairs={{0,12},{1,13},{2,14},{3,15},{4,0},{5,1},{6,2},{7,3},{8,4},{9,5},{1... | collective-permute-start | bytes 786440 | tf_op jit(solution)/shard_map/ppermute | solution.py:43
  95.7 11.6 %copy-start.1 = (bf16[1,256,2432]{2,1,0:T(8,128)(2,1)S(1)}, bf16[1,256,2432]{2,1,0:T(8,128)(2,1)}, u32[]{:S(2)}) copy-start(bf16[1,256,2432]{2,1,0:T(8,128)(2,1)} %param.13) | copy-start | bytes 3735556
  96.4 8.2 %collective-permute-start.13 = (bf16[4,256,128]{2,1,0:T(8,128)(2,1)}, bf16[4,256,128]{2,1,0:T(8,128)(2,1)S(1)}, u32[]{:S(2)}, u32[]{:S(2)}) collective-permute-start(bf16[4,256,128]{2,1,0:T(8,128)(2,1)} %pad_maximum_fusion.10), channel_id=1, source_target_pairs={{0,8},{1,9},{2,10},{3,11},{4,12},{5,13},{6,14},{7,15},{8,0},{9,1},... | collective-permute-start | bytes 786440 | tf_op jit(solution)/shard_map/ppermute | solution.py:43
  97.5 9.8 %collective-permute-start.14 = (bf16[4,256,128]{2,1,0:T(8,128)(2,1)}, bf16[4,256,128]{2,1,0:T(8,128)(2,1)S(1)}, u32[]{:S(2)}, u32[]{:S(2)}) collective-permute-start(bf16[4,256,128]{2,1,0:T(8,128)(2,1)} %pad_maximum_fusion.11), channel_id=1, source_target_pairs={{0,4},{1,5},{2,6},{3,7},{4,8},{5,9},{6,10},{7,11},{8,12},{9,13},{1... | collective-permute-start | bytes 786440 | tf_op jit(solution)/shard_map/ppermute | solution.py:43
  107.3 3.8 %copy-start = (bf16[2048,2432]{1,0:T(8,128)(2,1)S(1)}, bf16[2048,2432]{1,0:T(8,128)(2,1)}, u32[]{:S(2)}) copy-start(bf16[2048,2432]{1,0:T(8,128)(2,1)} %refs_5_.1) | copy-start | bytes 29884420
  111.1 20.6 %copy-start.6 = (f32[256,64]{0,1:T(8,128)S(1)}, f32[256,64]{0,1:T(8,128)}, u32[]{:S(2)}) copy-start(f32[256,64]{0,1:T(8,128)} %param.18) | copy-start | bytes 196612
  115.6 2.1 %collective-permute-start.15 = (bf16[128,128]{1,0:T(8,128)(2,1)S(1)}, bf16[128,128]{1,0:T(8,128)(2,1)S(1)}, u32[]{:S(2)}, u32[]{:S(2)}) collective-permute-start(bf16[128,128]{1,0:T(8,128)(2,1)S(1)} %convert_element_type.28), channel_id=1, source_target_pairs={{0,16},{16,32},{32,48},{48,64},{64,80},{80,96},{96,112},{1,17},{17... | collective-permute-start | bytes 98312 | tf_op jit(solution)/shard_map/ppermute | solution.py:294
  117.7 8.1 %collective-permute-start.16 = (bf16[128,128]{1,0:T(8,128)(2,1)S(1)}, bf16[128,128]{1,0:T(8,128)(2,1)S(1)}, u32[]{:S(2)}, u32[]{:S(2)}) collective-permute-start(bf16[128,128]{1,0:T(8,128)(2,1)S(1)} %fusion.1), channel_id=1, source_target_pairs={{0,32},{16,48},{32,64},{48,80},{64,96},{80,112},{1,33},{17,49},{33... | collective-permute-start | bytes 98312 | tf_op jit(solution)/shard_map/ppermute | solution.py:294
  125.9 7.4 %collective-permute-start.17 = (bf16[128,128]{1,0:T(8,128)(2,1)S(1)}, bf16[128,128]{1,0:T(8,128)(2,1)S(1)}, u32[]{:S(2)}, u32[]{:S(2)}) collective-permute-start(bf16[128,128]{1,0:T(8,128)(2,1)S(1)} %fusion.2), channel_id=1, source_target_pairs={{0,64},{16,80},{32,96},{48,112},{1,65},{17,81},{33,97},{49,113},{2... | collective-permute-start | bytes 98312 | tf_op jit(solution)/shard_map/ppermute | solution.py:294

commit v3 on v2

--- a/solution.py
+++ b/solution.py
@@ -14,6 +14,7 @@
 LAT = 64
 PAIR = 128
 RING = 4
+SLOTS = 8
 BOTH = ("tm", "seq")
 NT = (((1,), (1,)), ((), ()))
 SCALE = 0.125 * 1.4426950408889634
@@ -106,7 +107,7 @@
     wide = RING * PAIR
     return pl.pallas_call(
         pack_kernel,
-        in_specs=[pl.BlockSpec(memory_space=pltpu.SMEM)] + [pl.BlockSpec(memory_space=pl.ANY)] * 3,
+        in_specs=[pl.BlockSpec(memory_space=pltpu.SMEM)] + [pl.BlockSpec(memory_space=pltpu.HBM)] * 3,
         out_specs=[vmem] * RING,
         out_shape=[jax.ShapeDtypeStruct((RING, rows, PAIR), jnp.bfloat16)] * RING,
         scratch_shapes=[
@@ -130,17 +131,11 @@
     return [staged[0]] + [send(staged[e], False, e) for e in range(1, RING)]
 
 
-def give_back(blocks):
-    landed = [blocks[0]] + [send(blocks[e], False, -e) for e in range(1, RING)]
-    staged = [jnp.stack([block[d] for block in landed]) for d in range(RING)]
-    return [staged[0]] + [send(staged[d], True, -d) for d in range(1, RING)]
-
-
 def cuts_of(total, step):
     return [(start, min(step, total - start)) for start in range(0, total, step)]
 
 
-def attend_kernel(nk, kp, vp, first, last, *refs):
+def attend_kernel(nk, kp, vp, first, last, place_ref, *refs):
     q_refs, refs = refs[:RING], refs[RING:]
     if first:
         kv_refs = q_refs
@@ -148,7 +143,7 @@
         kv_refs, refs = refs[:RING], refs[RING:]
         acc_in, refs = refs[0], refs[1:]
     if last:
-        out_refs, refs = refs[:RING], refs[RING:]
+        out_ref, refs = refs[0], refs[1:]
     else:
         acc_out, refs = refs[0], refs[1:]
     q_all, k_all, low_t, high_t = refs
@@ -209,10 +204,12 @@
         for e in range(RING):
             for d in range(RING):
                 slot = e * RING + d
-                out_refs[e][d] = q_all[slot * nr : (slot + 1) * nr]
-
-
-def attend(q_parts, kv_parts, acc, nk, kp, vp, last):
+                along = lax.rem(place_ref[0] + RING - d, RING)
+                across = lax.rem(place_ref[1] + RING - e, RING)
+                out_ref[along * place_ref[2] + across * place_ref[3]] = q_all[slot * nr : (slot + 1) * nr]
+
+
+def attend(place, q_parts, kv_parts, acc, nk, kp, vp, last):
     first = acc is None
     nr = QROWS
     nq = RING * RING * nr
@@ -220,12 +217,12 @@
     operands = list(q_parts) + ([] if first else list(kv_parts) + [acc])
     vmem = pl.BlockSpec(memory_space=pltpu.VMEM)
     if last:
-        out_shape = [jax.ShapeDtypeStruct((RING, nr, PAIR), jnp.bfloat16)] * RING
+        out_shape = [jax.ShapeDtypeStruct((RING * RING, nr, PAIR), jnp.bfloat16)]
     else:
         out_shape = [jax.ShapeDtypeStruct((2, HEAD_DIM + 8, nq), jnp.float32)]
     return pl.pallas_call(
         functools.partial(attend_kernel, nk, kp, vp, first, last),
-        in_specs=[vmem] * len(operands),
+        in_specs=[pl.BlockSpec(memory_space=pltpu.SMEM)] + [vmem] * len(operands),
         out_specs=[vmem] * len(out_shape),
         out_shape=out_shape,
         scratch_shapes=[
@@ -234,21 +231,20 @@
             pltpu.VMEM((VROWS, total), jnp.bfloat16),
             pltpu.VMEM((VROWS, total), jnp.bfloat16),
         ],
-        compiler_params=pltpu.CompilerParams(vmem_limit_bytes=32 * MIB),
+        compiler_params=pltpu.CompilerParams(vmem_limit_bytes=20 * MIB),
         cost_estimate=pl.CostEstimate(
             flops=2 * 2 * 4 * nq * total * PAIR, bytes_accessed=2 * MIB, transcendentals=2 * nq * total
         ),
         name="attend",
-    )(*operands)
-
-
-def project_kernel(place_ref, level_ref, *refs):
-    parts, refs = refs[:RING], refs[RING:]
-    hidden_ref, w_proj_ref, w_final_ref, base_ref, slope_ref, out_ref, drift_ref, joined, gated = refs
-    for d in range(RING):
-        for e in range(RING):
-            pair = lax.rem(place_ref[0] + d, RING) * RING + lax.rem(place_ref[1] + e, RING)
-            joined[:, pl.ds(pl.multiple_of(pair * PAIR, PAIR), PAIR)] = parts[d][e]
+    )(place, *operands)
+
+
+def project_kernel(place_ref, level_ref, got_ref, hidden_ref, w_proj_ref, w_final_ref, base_ref, slope_ref, *refs):
+    velocity_ref, drift_ref, later_ref, joined, gated = refs
+    for j in range(RING * RING):
+        hi, lo = divmod(j, RING)
+        pair = hi * place_ref[2] + lo * place_ref[3]
+        joined[:, pl.ds(pl.multiple_of(pair * PAIR, PAIR), PAIR)] = got_ref[j]
     squares = jnp.zeros((QROWS, 1), jnp.float32)
     for start, size in cuts_of(D, 512):
         cols = slice(start, start + size)
@@ -258,44 +254,37 @@
         gated[:, cols] = value
         squares = squares + jnp.sum(value * value, axis=1, keepdims=True)
     normed = (gated[...] * lax.rsqrt(squares * (1.0 / D) + 1e-06)).astype(jnp.bfloat16)
-    velocity = jnp.dot(normed, w_final_ref[...], preferred_element_type=jnp.float32)
-    out_ref[...] = velocity
-    half = QROWS // 2
-    drift_ref[...] = jnp.concatenate([velocity[:half], velocity[half:]], axis=1) * level_ref[1]
-
-
-def project(place, level, parts, hidden, w_proj, w_final, base, slope):
-    nr = QROWS
+    velocity = lax.dot_general(w_final_ref[...], normed, NT, preferred_element_type=jnp.float32)
+    velocity_ref[...] = velocity
+    drift = velocity * level_ref[1]
+    drift_ref[...] = drift
+    low = drift.astype(jnp.bfloat16)
+    for k in range(SLOTS):
+        later_ref[k] = jnp.where(place_ref[4] < k, low, jnp.zeros_like(low))
+
+
+def project(place, level, got, hidden, w_proj, w_final, base, slope):
     vmem = pl.BlockSpec(memory_space=pltpu.VMEM)
     smem = pl.BlockSpec(memory_space=pltpu.SMEM)
     return pl.pallas_call(
         project_kernel,
-        in_specs=[smem, smem] + [vmem] * (RING + 5),
-        out_specs=[vmem, vmem],
+        in_specs=[smem, smem] + [vmem] * 6,
+        out_specs=[vmem] * 3,
         out_shape=[
-            jax.ShapeDtypeStruct((nr, LAT), jnp.float32),
-            jax.ShapeDtypeStruct((nr // 2, 2 * LAT), jnp.float32),
+            jax.ShapeDtypeStruct((LAT, QROWS), jnp.float32),
+            jax.ShapeDtypeStruct((LAT, QROWS), jnp.float32),
+            jax.ShapeDtypeStruct((SLOTS, LAT, QROWS), jnp.bfloat16),
         ],
-        scratch_shapes=[pltpu.VMEM((nr, HD), jnp.bfloat16), pltpu.VMEM((nr, D), jnp.float32)],
-        compiler_params=pltpu.CompilerParams(vmem_limit_bytes=32 * MIB),
-        cost_estimate=pl.CostEstimate(flops=2 * nr * HD * D, bytes_accessed=12 * MIB, transcendentals=0),
+        scratch_shapes=[pltpu.VMEM((QROWS, HD), jnp.bfloat16), pltpu.VMEM((QROWS, D), jnp.float32)],
+        compiler_params=pltpu.CompilerParams(vmem_limit_bytes=16 * MIB),
+        cost_estimate=pl.CostEstimate(flops=2 * QROWS * HD * D, bytes_accessed=12 * MIB, transcendentals=0),
         name="project",
-    )(place, level, *parts, hidden, w_proj, w_final, base, slope)
+    )(place, level, got, hidden, w_proj, w_final, base, slope)
 
 
 def sigma_of(index_val, total_steps):
     frac = 1.0 - index_val.astype(jnp.float32) / total_steps
     return 3.0 * frac / (1.0 + 2.0 * frac)
-
-
-def running_sum(drift, slots):
-    shift = 1
-    while shift < slots:
-        drift = drift + lax.ppermute(drift.astype(jnp.bfloat16), "tm", [(i, i + shift) for i in range(slots - shift)]).astype(
-            jnp.float32
-        )
-        shift *= 2
-    return drift
 
 
 def per_device(
@@ -307,7 +296,7 @@
     x, z = seat // RING, lax.rem(seat, RING)
     even = lax.rem(slot, 2) == 0
     first, second = jnp.where(even, x, z), jnp.where(even, z, x)
-    place = jnp.stack([first, second]).astype(jnp.int32)
+    place = jnp.stack([first, second, jnp.where(even, RING, 1), jnp.where(even, 1, RING), slot]).astype(jnp.int32)
     sigma_now = sigma_of(window_steps[slot], 2 * slots)
     step_size = sigma_of(window_steps[slot + 1], 2 * slots) - sigma_now
     level = jnp.stack([sigma_now, step_size])
@@ -320,15 +309,15 @@
     for number, ((k0, k1), (kp, vp)) in enumerate(zip(KEY_CUTS, places)):
         start = starts[number]
         last = number == len(KEY_CUTS) - 1
-        got = attend(received[0], received[number], acc, k1 - k0, kp - start, vp - start, last)
+        got = attend(place, received[0], received[number], acc, k1 - k0, kp - start, vp - start, last)
         acc = None if last else got[0]
-    velocity, drift = project(
-        place, level, give_back(got), hidden[0], w_proj, w_final, gate_base[None], gate_slope[None]
+    got = lax.all_to_all(got[0], "seq", 0, 0, tiled=True)
+    velocity, drift, later = project(
+        place, level, got, hidden[0], w_proj, w_final.T, gate_base[None], gate_slope[None]
     )
-    drift = running_sum(drift, slots)
-    half = QROWS // 2
-    latents = start_latent + jnp.concatenate([drift[:, :LAT], drift[:, LAT:]], axis=0)
-    return (velocity[None], latents[None])
+    earlier = lax.all_to_all(later, "tm", 0, 0, tiled=True).astype(jnp.float32)
+    latents = start_latent.T + drift + jnp.sum(earlier, axis=0)
+    return (velocity.T[None], latents.T[None])
 
 
 def solution(mesh):

time: 137 us -> 127 us (0.927); the launches traced: 134 us -> 127 us
  starting transfers between devices: 36 us -> 19.2 us
  blocking collectives: 0 us -> 11.8 us
  Pallas kernels: 39.6 us -> 42.9 us
  waiting for transfers between devices: 43.5 us -> 40.7 us
  local copies, waits for them, and re-layouts: 10.5 us -> 8.53 us
    ppermute x3 -> x0, starting transfers between devices: 13.7 us -> none  [running_sum(): lax.ppermute(drift.astype(jnp.bfloat16), 'tm', [(i, i + shift) for i in r...]
    all_to_all x0 -> x1, waiting for transfers between devices: none -> 13.1 us  [per_device(): got = lax.all_to_all(got[0], 'seq', 0, 0, tiled=True)]
    ppermute x15 -> x9, waiting for transfers between devices: 40.3 us -> 27.7 us  [send(): return lax.ppermute(value, BOTH, ring_perm(first, shift % RING))]
    all_to_all x0 -> x1, blocking collectives: none -> 11.8 us  [per_device(): earlier = lax.all_to_all(later, 'tm', 0, 0, tiled=True).astype(jnp.float32)]
    ppermute x15 -> x9, starting transfers between devices: 22.3 us -> 14.9 us  [send(): return lax.ppermute(value, BOTH, ring_perm(first, shift % RING))]
    all_to_all x0 -> x1, starting transfers between devices: none -> 4.3 us  [per_device(): got = lax.all_to_all(got[0], 'seq', 0, 0, tiled=True)]
    ppermute x3 -> x0, waiting for transfers between devices: 3.17 us -> none  [running_sum(): lax.ppermute(drift.astype(jnp.bfloat16), 'tm', [(i, i + shift) for i in r...]
    pallas_call x2, Pallas kernels: 32.2 us -> 34.4 us  [attend(): pl.pallas_call(functools.partial(attend_kernel, nk, kp, vp, first, last),...]
  transfers between devices with their start and end apart: 18 -> 10, of which waited for: 13 -> 5; matrix products, arithmetic and copies ran while one was open for 3% -> 1% of each run, Pallas kernels for 8% -> 9%
where the time goes in v3:
time: 127 us
  Pallas kernels  42.9 us (34%)
  waiting for transfers between devices  40.7 us (32%)
  starting transfers between devices  19.2 us (15%)
  blocking collectives  11.8 us (9%)
  local copies, waits for them, and re-layouts  8.53 us (7%)
  between operations  2.28 us (2%)
    pallas_call x2, Pallas kernels, attend(): pl.pallas_call(functools.partial(attend_kernel, nk, kp, vp, first, last),...  34.4 us
    ppermute x9, waiting for transfers between devices, send(): return lax.ppermute(value, BOTH, ring_perm(first, shift % RING))  27.7 us
    ppermute x9, starting transfers between devices, send(): return lax.ppermute(value, BOTH, ring_perm(first, shift % RING))  14.9 us
    all_to_all x1, waiting for transfers between devices, per_device(): got = lax.all_to_all(got[0], 'seq', 0, 0, tiled=True)  13.1 us
    all_to_all x1, blocking collectives, per_device(): earlier = lax.all_to_all(later, 'tm', 0, 0, tiled=True).astype(jnp.float32)  11.8 us
    unnamed x20, local copies, waits for them, and re-layouts  7.6 us
    pallas_call x1, Pallas kernels, project(): pl.pallas_call(project_kernel, in_specs=[smem, smem] + [vmem] * 6, out_sp...  5.5 us
    all_to_all x1, starting transfers between devices, per_device(): got = lax.all_to_all(got[0], 'seq', 0, 0, tiled=True)  4.3 us
  transfers between devices with their start and end apart: 10, of which 5 were waited for; matrix products, arithmetic and copies ran while one was open for 1% of the time, Pallas kernels for 9%

profile of v3, /device:TPU:0, one launch (start us, length us, event | category | flops | bytes accessed | tf_op | source)
XLA Modules:
  0.0 126.7 jit_solution(17190539628581716407)
XLA Ops:
  0.7 0.1 stack.56.place_ref
  0.7 1.3 copy-done.2
  2.0 1.3 copy-done.3
  3.3 1.2 copy-done.4
  4.5 3.0 %pack.1 = (bf16[4,832,128]{2,1,0:T(8,128)(2,1)S(1)}, bf16[4,832,128]{2,1,0:T(8,128)(2,1)S(1)}, bf16[4,832,128]{2,1,0:T(8,128)(2,1)S(1)}, bf16[4,832,128]{2,1,0:T(8,128)(2,1)S(1)}) custom-call(s32[5]{0:T(128)S(1)} %stack.56.place_ref, bf16[256,2048]{1,0:T(8,128)(2,1)S(1)} %bitcast.26, bf16[280,2048]{1,0:T(8,128)(2,1)S(1)} %bitcast.24, ...), custom_call_target="tpu_custom_call" | custom-call | flops 872415232 | bytes 6815744 | tf_op jit(solution)/shard_map/pack/pallas_call | solution.py:108
  7.5 2.9 %collective-permute-start.2 = (bf16[4,832,128]{2,1,0:T(8,128)(2,1)S(1)}, bf16[4,832,128]{2,1,0:T(8,128)(2,1)S(1)}, u32[]{:S(2)}, u32[]{:S(2)}) collective-permute-start(bf16[4,832,128]{2,1,0:T(8,128)(2,1)S(1)} %get-tuple-element.12), channel_id=1, source_target_pairs={{0,12},{1,13},{2,14},{3,15},{4,0},{5,1},{6,2},{7,3},{8,4},{9,5},{1... | collective-permute-start | bytes 2555912 | tf_op jit(solution)/shard_map/ppermute | solution.py:44
  10.4 0.8 collective-permute-start.1
  11.2 0.9 collective-permute-start
  12.1 17.6 %collective-permute-done.2 = bf16[4,832,128]{2,1,0:T(8,128)(2,1)S(1)} collective-permute-done((bf16[4,832,128]{2,1,0:T(8,128)(2,1)S(1)}, bf16[4,832,128]{2,1,0:T(8,128)(2,1)S(1)}, u32[]{:S(2)}, u32[]{:S(2)}) %collective-permute-start.2) | collective-permute-done | bytes 852000 | tf_op jit(solution)/shard_map/ppermute | solution.py:44
  29.8 0.0 collective-permute-done.1
  29.8 3.9 %collective-permute-done = bf16[4,832,128]{2,1,0:T(8,128)(2,1)S(1)} collective-permute-done((bf16[4,832,128]{2,1,0:T(8,128)(2,1)S(1)}, bf16[4,832,128]{2,1,0:T(8,128)(2,1)S(1)}, u32[]{:S(2)}, u32[]{:S(2)}) %collective-permute-start) | collective-permute-done | bytes 852000 | tf_op jit(solution)/shard_map/ppermute | solution.py:44
  33.8 0.1 pad_maximum_fusion.1
  33.8 2.0 %collective-permute-start.3 = (bf16[4,448,128]{2,1,0:T(8,128)(2,1)S(1)}, bf16[4,448,128]{2,1,0:T(8,128)(2,1)S(1)}, u32[]{:S(2)}, u32[]{:S(2)}) collective-permute-start(bf16[4,448,128]{2,1,0:T(8,128)(2,1)S(1)} %pad_maximum_fusion.1), channel_id=1, source_target_pairs={{0,1},{1,2},{2,3},{3,0},{4,5},{5,6},{6,7},{7,4},{8,9},{9,10},{10,1... | collective-permute-start | bytes 1376264 | tf_op jit(solution)/shard_map/ppermute | solution.py:44
  35.8 0.1 pad_maximum_fusion.2
  35.8 3.7 %collective-permute-start.4 = (bf16[4,448,128]{2,1,0:T(8,128)(2,1)S(1)}, bf16[4,448,128]{2,1,0:T(8,128)(2,1)S(1)}, u32[]{:S(2)}, u32[]{:S(2)}) collective-permute-start(bf16[4,448,128]{2,1,0:T(8,128)(2,1)S(1)} %pad_maximum_fusion.2), channel_id=1, source_target_pairs={{0,2},{1,3},{2,0},{3,1},{4,6},{5,7},{6,4},{7,5},{8,10},{9,11},{10,... | collective-permute-start | bytes 1376264 | tf_op jit(solution)/shard_map/ppermute | solution.py:44
  39.5 0.1 pad_maximum_fusion.3
  39.6 1.1 collective-permute-start.5
  40.7 0.1 pad_maximum_fusion.5
  40.8 1.1 collective-permute-start.6
  41.9 0.1 pad_maximum_fusion.6
  42.0 0.5 collective-permute-start.7
  42.5 0.1 pad_maximum_fusion.4.refs_4_
  42.5 0.1 pad_maximum_fusion.7
  42.6 0.1 pad_maximum_fusion.refs_0_
  42.7 1.7 %collective-permute-done.3.refs_1_ = bf16[4,448,128]{2,1,0:T(8,128)(2,1)S(1)} collective-permute-done((bf16[4,448,128]{2,1,0:T(8,128)(2,1)S(1)}, bf16[4,448,128]{2,1,0:T(8,128)(2,1)S(1)}, u32[]{:S(2)}, u32[]{:S(2)}) %collective-permute-start.3) | collective-permute-done | bytes 458784 | tf_op jit(solution)/shard_map/ppermute | solution.py:44
  44.4 2.0 %collective-permute-start.8 = (bf16[4,384,128]{2,1,0:T(8,128)(2,1)S(1)}, bf16[4,384,128]{2,1,0:T(8,128)(2,1)S(1)}, u32[]{:S(2)}, u32[]{:S(2)}) collective-permute-start(bf16[4,384,128]{2,1,0:T(8,128)(2,1)S(1)} %pad_maximum_fusion.7), channel_id=1, source_target_pairs={{0,3},{1,0},{2,1},{3,2},{4,7},{5,4},{6,5},{7,6},{8,11},{9,8},{10,9... | collective-permute-start | bytes 1179656 | tf_op jit(solution)/shard_map/ppermute | solution.py:44
  46.4 4.5 %collective-permute-done.4.refs_2_ = bf16[4,448,128]{2,1,0:T(8,128)(2,1)S(1)} collective-permute-done((bf16[4,448,128]{2,1,0:T(8,128)(2,1)S(1)}, bf16[4,448,128]{2,1,0:T(8,128)(2,1)S(1)}, u32[]{:S(2)}, u32[]{:S(2)}) %collective-permute-start.4) | collective-permute-done | bytes 458784 | tf_op jit(solution)/shard_map/ppermute | solution.py:44
  50.9 0.0 collective-permute-done.5.refs_3_
  50.9 11.6 %attend.2.refs_8_ = f32[2,72,4096]{2,1,0:T(8,128)S(1)} custom-call(s32[5]{0:T(128)S(1)} %stack.56.place_ref, bf16[4,448,128]{2,1,0:T(8,128)(2,1)S(1)} %pad_maximum_fusion.refs_0_, bf16[4,448,128]{2,1,0:T(8,128)(2,1)S(1)} %collective-permute-done.3.refs_1_, bf16[4,448,128]{2,1,0:T(8,128)(2,1)S(1)} %collective-permute-done.4.refs_2_, ...), custom_call_target="tpu_custom_call" | custom-call | flops 12884901888 | bytes 2097152 | tf_op jit(solution)/shard_map/attend/pallas_call | solution.py:223
  62.5 0.0 collective-permute-done.6.refs_5_
  62.5 0.0 collective-permute-done.7.refs_6_
  62.5 0.0 collective-permute-done.8.refs_7_
  62.5 22.8 %attend.3 = bf16[16,256,128]{2,1,0:T(8,128)(2,1)} custom-call(s32[5]{0:T(128)S(1)} %stack.56.place_ref, bf16[4,448,128]{2,1,0:T(8,128)(2,1)S(1)} %pad_maximum_fusion.refs_0_, bf16[4,448,128]{2,1,0:T(8,128)(2,1)S(1)} %collective-permute-done.3.refs_1_, bf16[4,448,128]{2,1,0:T(8,128)(2,1)S(1)} %collective-permute-done.4.refs_2_, ...), custom_call_target="tpu_custom_call" | custom-call | flops 24696061952 | bytes 2097152 | tf_op jit(solution)/shard_map/attend/pallas_call | solution.py:223
  85.3 0.0 copy-start.5
  85.3 4.3 %all-to-all-start = ((bf16[16,256,128]{2,1,0:T(8,128)(2,1)}), bf16[16,256,128]{2,1,0:T(8,128)(2,1)S(1)}, u32[]{:S(2)}, u32[]{:S(2)}) async-start(bf16[16,256,128]{2,1,0:T(8,128)(2,1)} %attend.3), calls=%async_computation | async-start | bytes 2097152 | tf_op jit(solution)/shard_map/all_to_all | solution.py:314
  89.6 0.0 copy-done.9
  89.6 0.6 fusion.10
  91.5 0.0 copy-done.7
  91.6 0.0 copy-done.8
  91.7 0.1 pad_maximum_fusion.8.level_ref
  91.8 13.1 %all-to-all-done.got_ref = bf16[16,256,128]{2,1,0:T(8,128)(2,1)S(1)} async-done(((bf16[16,256,128]{2,1,0:T(8,128)(2,1)}), bf16[16,256,128]{2,1,0:T(8,128)(2,1)S(1)}, u32[]{:S(2)}, u32[]{:S(2)}) %all-to-all-start) | async-done | bytes 1048608 | tf_op jit(solution)/shard_map/all_to_all | solution.py:314
  104.8 0.0 copy-done.1
  104.8 0.0 copy-done.5
  104.8 3.8 %copy-done = bf16[2048,2432]{1,0:T(8,128)(2,1)S(1)} copy-done((bf16[2048,2432]{1,0:T(8,128)(2,1)S(1)}, bf16[2048,2432]{1,0:T(8,128)(2,1)}, u32[]{:S(2)}) %copy-start) | copy-done | bytes 9961496
  108.7 5.5 %project.1 = (f32[64,256]{1,0:T(8,128)}, f32[64,256]{1,0:T(8,128)S(1)}, bf16[8,64,256]{2,1,0:T(8,128)(2,1)S(1)}) custom-call(s32[5]{0:T(128)S(1)} %stack.56.place_ref, f32[2]{0:T(128)S(1)} %pad_maximum_fusion.8.level_ref, bf16[16,256,128]{2,1,0:T(8,128)(2,1)S(1)} %all-to-all-done.got_ref, bf16[256,2432]{1,0:T(8,128)(2,1)S(1)} %bitcast.23, ...), custom_call_target="tpu_custom_call" | custom-call | flops 2550136832 | bytes 12582912 | tf_op jit(solution)/shard_map/project/pallas_call | solution.py:269
  114.2 11.8 %all_to_all.10 = bf16[8,64,256]{2,1,0:T(8,128)(2,1)S(1)} all-to-all(bf16[8,64,256]{2,1,0:T(8,128)(2,1)S(1)} %get-tuple-element.15), channel_id=1, replica_groups=mesh['tm'=8,'seq'=16] {'tm'}, dimensions={0} | all-to-all | bytes 524288 | tf_op jit(solution)/shard_map/all_to_all | solution.py:318
  126.0 0.0 copy-done.6
  126.0 0.6 fusion.1
  (20 shorter events, 0.3 us)
Async XLA Ops:
  0.7 1.3 copy-start.2
  2.0 1.3 copy-start.3
  3.3 1.2 copy-start.4
  7.5 22.3 %collective-permute-start.2 = (bf16[4,832,128]{2,1,0:T(8,128)(2,1)S(1)}, bf16[4,832,128]{2,1,0:T(8,128)(2,1)S(1)}, u32[]{:S(2)}, u32[]{:S(2)}) collective-permute-start(bf16[4,832,128]{2,1,0:T(8,128)(2,1)S(1)} %get-tuple-element.12), channel_id=1, source_target_pairs={{0,12},{1,13},{2,14},{3,15},{4,0},{5,1},{6,2},{7,3},{8,4},{9,5},{1... | collective-permute-start | bytes 2555912 | tf_op jit(solution)/shard_map/ppermute | solution.py:44
  10.4 19.4 %collective-permute-start.1 = (bf16[4,832,128]{2,1,0:T(8,128)(2,1)S(1)}, bf16[4,832,128]{2,1,0:T(8,128)(2,1)S(1)}, u32[]{:S(2)}, u32[]{:S(2)}) collective-permute-start(bf16[4,832,128]{2,1,0:T(8,128)(2,1)S(1)} %get-tuple-element.11), channel_id=1, source_target_pairs={{0,8},{1,9},{2,10},{3,11},{4,12},{5,13},{6,14},{7,15},{8,0},{9,1},... | collective-permute-start | bytes 2555912 | tf_op jit(solution)/shard_map/ppermute | solution.py:44
  11.2 22.5 %collective-permute-start = (bf16[4,832,128]{2,1,0:T(8,128)(2,1)S(1)}, bf16[4,832,128]{2,1,0:T(8,128)(2,1)S(1)}, u32[]{:S(2)}, u32[]{:S(2)}) collective-permute-start(bf16[4,832,128]{2,1,0:T(8,128)(2,1)S(1)} %get-tuple-element.10), channel_id=1, source_target_pairs={{0,4},{1,5},{2,6},{3,7},{4,8},{5,9},{6,10},{7,11},{8,12},{9,13},{1... | collective-permute-start | bytes 2555912 | tf_op jit(solution)/shard_map/ppermute | solution.py:44
  33.8 10.6 %collective-permute-start.3 = (bf16[4,448,128]{2,1,0:T(8,128)(2,1)S(1)}, bf16[4,448,128]{2,1,0:T(8,128)(2,1)S(1)}, u32[]{:S(2)}, u32[]{:S(2)}) collective-permute-start(bf16[4,448,128]{2,1,0:T(8,128)(2,1)S(1)} %pad_maximum_fusion.1), channel_id=1, source_target_pairs={{0,1},{1,2},{2,3},{3,0},{4,5},{5,6},{6,7},{7,4},{8,9},{9,10},{10,1... | collective-permute-start | bytes 1376264 | tf_op jit(solution)/shard_map/ppermute | solution.py:44
  35.8 15.0 %collective-permute-start.4 = (bf16[4,448,128]{2,1,0:T(8,128)(2,1)S(1)}, bf16[4,448,128]{2,1,0:T(8,128)(2,1)S(1)}, u32[]{:S(2)}, u32[]{:S(2)}) collective-permute-start(bf16[4,448,128]{2,1,0:T(8,128)(2,1)S(1)} %pad_maximum_fusion.2), channel_id=1, source_target_pairs={{0,2},{1,3},{2,0},{3,1},{4,6},{5,7},{6,4},{7,5},{8,10},{9,11},{10,... | collective-permute-start | bytes 1376264 | tf_op jit(solution)/shard_map/ppermute | solution.py:44
  39.6 11.3 %collective-permute-start.5 = (bf16[4,448,128]{2,1,0:T(8,128)(2,1)S(1)}, bf16[4,448,128]{2,1,0:T(8,128)(2,1)S(1)}, u32[]{:S(2)}, u32[]{:S(2)}) collective-permute-start(bf16[4,448,128]{2,1,0:T(8,128)(2,1)S(1)} %pad_maximum_fusion.3), channel_id=1, source_target_pairs={{0,3},{1,0},{2,1},{3,2},{4,7},{5,4},{6,5},{7,6},{8,11},{9,8},{10,9... | collective-permute-start | bytes 1376264 | tf_op jit(solution)/shard_map/ppermute | solution.py:44
  40.8 21.7 %collective-permute-start.6 = (bf16[4,384,128]{2,1,0:T(8,128)(2,1)S(1)}, bf16[4,384,128]{2,1,0:T(8,128)(2,1)S(1)}, u32[]{:S(2)}, u32[]{:S(2)}) collective-permute-start(bf16[4,384,128]{2,1,0:T(8,128)(2,1)S(1)} %pad_maximum_fusion.5), channel_id=1, source_target_pairs={{0,1},{1,2},{2,3},{3,0},{4,5},{5,6},{6,7},{7,4},{8,9},{9,10},{10,1... | collective-permute-start | bytes 1179656 | tf_op jit(solution)/shard_map/ppermute | solution.py:44
  42.0 20.5 %collective-permute-start.7 = (bf16[4,384,128]{2,1,0:T(8,128)(2,1)S(1)}, bf16[4,384,128]{2,1,0:T(8,128)(2,1)S(1)}, u32[]{:S(2)}, u32[]{:S(2)}) collective-permute-start(bf16[4,384,128]{2,1,0:T(8,128)(2,1)S(1)} %pad_maximum_fusion.6), channel_id=1, source_target_pairs={{0,2},{1,3},{2,0},{3,1},{4,6},{5,7},{6,4},{7,5},{8,10},{9,11},{10,... | collective-permute-start | bytes 1179656 | tf_op jit(solution)/shard_map/ppermute | solution.py:44
  44.4 18.1 %collective-permute-start.8 = (bf16[4,384,128]{2,1,0:T(8,128)(2,1)S(1)}, bf16[4,384,128]{2,1,0:T(8,128)(2,1)S(1)}, u32[]{:S(2)}, u32[]{:S(2)}) collective-permute-start(bf16[4,384,128]{2,1,0:T(8,128)(2,1)S(1)} %pad_maximum_fusion.7), channel_id=1, source_target_pairs={{0,3},{1,0},{2,1},{3,2},{4,7},{5,4},{6,5},{7,6},{8,11},{9,8},{10,9... | collective-permute-start | bytes 1179656 | tf_op jit(solution)/shard_map/ppermute | solution.py:44
  85.3 4.3 %copy-start.9 = (s32[9]{0:T(128)S(1)}, s32[9]{0:T(128)}, u32[]{:S(2)}) copy-start(s32[9]{0:T(128)} %param.19) | copy-start | bytes 112
  85.3 6.2 %copy-start.7 = (f32[2432]{0:T(1024)S(1)}, f32[2432]{0:T(1024)}, u32[]{:S(2)}) copy-start(f32[2432]{0:T(1024)} %param.16) | copy-start | bytes 29188
  85.3 6.3 %copy-start.8 = (f32[2432]{0:T(1024)S(1)}, f32[2432]{0:T(1024)}, u32[]{:S(2)}) copy-start(f32[2432]{0:T(1024)} %param.17) | copy-start | bytes 29188
  85.3 19.5 %copy-start.1 = (bf16[1,256,2432]{2,1,0:T(8,128)(2,1)S(1)}, bf16[1,256,2432]{2,1,0:T(8,128)(2,1)}, u32[]{:S(2)}) copy-start(bf16[1,256,2432]{2,1,0:T(8,128)(2,1)} %param.13) | copy-start | bytes 3735556
  85.3 19.5 %copy-start.5 = (bf16[2432,64]{0,1:T(8,128)(2,1)S(1)}, bf16[2432,64]{0,1:T(8,128)(2,1)}, u32[]{:S(2)}) copy-start(bf16[2432,64]{0,1:T(8,128)(2,1)} %param.15) | copy-start | bytes 933892
  85.3 19.5 %all-to-all-start = ((bf16[16,256,128]{2,1,0:T(8,128)(2,1)}), bf16[16,256,128]{2,1,0:T(8,128)(2,1)S(1)}, u32[]{:S(2)}, u32[]{:S(2)}) async-start(bf16[16,256,128]{2,1,0:T(8,128)(2,1)} %attend.3), calls=%async_computation | async-start | bytes 2097152 | tf_op jit(solution)/shard_map/all_to_all | solution.py:314
  104.8 3.8 %copy-start = (bf16[2048,2432]{1,0:T(8,128)(2,1)S(1)}, bf16[2048,2432]{1,0:T(8,128)(2,1)}, u32[]{:S(2)}) copy-start(bf16[2048,2432]{1,0:T(8,128)(2,1)} %w_proj_ref.1) | copy-start | bytes 29884420
  108.7 17.3 %copy-start.6 = (f32[256,64]{0,1:T(8,128)S(1)}, f32[256,64]{0,1:T(8,128)}, u32[]{:S(2)}) copy-start(f32[256,64]{0,1:T(8,128)} %param.18) | copy-start | bytes 196612

commit v4 on v3

--- a/solution.py
+++ b/solution.py
@@ -116,7 +116,7 @@
             pltpu.VMEM((RING, KROWS, wide), jnp.bfloat16),
             pltpu.SemaphoreType.DMA((RING, 3)),
         ],
-        compiler_params=pltpu.CompilerParams(vmem_limit_bytes=24 * MIB),
+        compiler_params=pltpu.CompilerParams(vmem_limit_bytes=59 * MIB),
         cost_estimate=pl.CostEstimate(flops=2 * 2 * rows * HD * PAIR, bytes_accessed=4 * rows * HD, transcendentals=0),
         name="pack",
     )(place, queries, keys, values)
@@ -231,7 +231,7 @@
             pltpu.VMEM((VROWS, total), jnp.bfloat16),
             pltpu.VMEM((VROWS, total), jnp.bfloat16),
         ],
-        compiler_params=pltpu.CompilerParams(vmem_limit_bytes=20 * MIB),
+        compiler_params=pltpu.CompilerParams(vmem_limit_bytes=32 * MIB),
         cost_estimate=pl.CostEstimate(
             flops=2 * 2 * 4 * nq * total * PAIR, bytes_accessed=2 * MIB, transcendentals=2 * nq * total
         ),
@@ -311,10 +311,11 @@
         last = number == len(KEY_CUTS) - 1
         got = attend(place, received[0], received[number], acc, k1 - k0, kp - start, vp - start, last)
         acc = None if last else got[0]
-    got = lax.all_to_all(got[0], "seq", 0, 0, tiled=True)
-    velocity, drift, later = project(
-        place, level, got, hidden[0], w_proj, w_final.T, gate_base[None], gate_slope[None]
+    got, *operands = lax.optimization_barrier(
+        (got[0], level, hidden[0], w_proj, w_final.T, gate_base[None], gate_slope[None])
     )
+    got = lax.all_to_all(got, "seq", 0, 0, tiled=True)
+    velocity, drift, later = project(place, operands[0], got, *operands[1:])
     earlier = lax.all_to_all(later, "tm", 0, 0, tiled=True).astype(jnp.float32)
     latents = start_latent.T + drift + jnp.sum(earlier, axis=0)
     return (velocity.T[None], latents.T[None])

time: 127 us -> 122 us (0.961)
  blocking collectives: 11.8 us -> 30.9 us
  waiting for transfers between devices: 40.7 us -> 23.6 us
  local copies, waits for them, and re-layouts: 8.53 us -> 3.66 us
  starting transfers between devices: 19.2 us -> 15 us
  Pallas kernels: 42.9 us -> 44.5 us
    all_to_all x0 -> x1, blocking collectives: none -> 19.1 us  [per_device(): got = lax.all_to_all(got, 'seq', 0, 0, tiled=True)]
    all_to_all x1 -> x0, waiting for transfers between devices: 13.1 us -> none  [per_device(): got = lax.all_to_all(got[0], 'seq', 0, 0, tiled=True)]
    unnamed x20, local copies, waits for them, and re-layouts: 7.6 us -> 0.05 us
    all_to_all x1 -> x0, starting transfers between devices: 4.3 us -> none  [per_device(): got = lax.all_to_all(got[0], 'seq', 0, 0, tiled=True)]
    ppermute x9, waiting for transfers between devices: 27.7 us -> 23.6 us  [send(): return lax.ppermute(value, BOTH, ring_perm(first, shift % RING))]
    pallas_call x1, Pallas kernels: 2.98 us -> 5.49 us  [pack(): pl.pallas_call(pack_kernel, in_specs=[pl.BlockSpec(memory_space=pltpu.SME...]
    slice x8, local copies, waits for them, and re-layouts: 0.24 us -> 2.33 us  [second_hop(): part[e, start:stop]]
  transfers between devices with their start and end apart: 10 -> 9, of which waited for: 5 -> 4; matrix products, arithmetic and copies ran while one was open for 1% -> 3% of each run, Pallas kernels for 9% -> 10%
where the time goes in v4:
time: 122 us; the launch traced here: 121 us
  Pallas kernels  44.5 us (36%)
  blocking collectives  30.9 us (25%)
  waiting for transfers between devices  23.6 us (19%)
  starting transfers between devices  15 us (12%)
  local copies, waits for them, and re-layouts  3.66 us (3%)
  between operations  2.33 us (2%)
    pallas_call x2, Pallas kernels, attend(): pl.pallas_call(functools.partial(attend_kernel, nk, kp, vp, first, last),...  33.4 us
    ppermute x9, waiting for transfers between devices, send(): return lax.ppermute(value, BOTH, ring_perm(first, shift % RING))  23.6 us
    all_to_all x1, blocking collectives, per_device(): got = lax.all_to_all(got, 'seq', 0, 0, tiled=True)  19.1 us
    ppermute x9, starting transfers between devices, send(): return lax.ppermute(value, BOTH, ring_perm(first, shift % RING))  15 us
    all_to_all x1, blocking collectives, per_device(): earlier = lax.all_to_all(later, 'tm', 0, 0, tiled=True).astype(jnp.float32)  11.8 us
    pallas_call x1, Pallas kernels, project(): pl.pallas_call(project_kernel, in_specs=[smem, smem] + [vmem] * 6, out_sp...  5.55 us
    pallas_call x1, Pallas kernels, pack(): pl.pallas_call(pack_kernel, in_specs=[pl.BlockSpec(memory_space=pltpu.SME...  5.49 us
  transfers between devices with their start and end apart: 9, of which 4 were waited for; matrix products, arithmetic and copies ran while one was open for 3% of the time, Pallas kernels for 10%

profile of v4, /device:TPU:0, one launch (start us, length us, event | category | flops | bytes accessed | tf_op | source)
XLA Modules:
  0.0 121.2 jit_solution(1720211302859196262)
XLA Ops:
  0.7 0.7 stack.56.place_ref
  1.3 5.5 %pack.1 = (bf16[4,832,128]{2,1,0:T(8,128)(2,1)}, bf16[4,832,128]{2,1,0:T(8,128)(2,1)}, bf16[4,832,128]{2,1,0:T(8,128)(2,1)}, bf16[4,832,128]{2,1,0:T(8,128)(2,1)}) custom-call(s32[5]{0:T(128)} %stack.56.place_ref, bf16[256,2048]{1,0:T(8,128)(2,1)} %bitcast.29, bf16[280,2048]{1,0:T(8,128)(2,1)} %bitcast.27, bf16[280,2048]{1,0:T(8,128)(2,1)} %bitcast.28), custom_call_target="tpu_custom_call" | custom-call | flops 872415232 | bytes 6815744 | tf_op jit(solution)/shard_map/pack/pallas_call | solution.py:108
  6.8 2.9 %collective-permute-start.2 = (bf16[4,832,128]{2,1,0:T(8,128)(2,1)}, bf16[4,832,128]{2,1,0:T(8,128)(2,1)S(1)}, u32[]{:S(2)}, u32[]{:S(2)}) collective-permute-start(bf16[4,832,128]{2,1,0:T(8,128)(2,1)} %get-tuple-element.19), channel_id=1, source_target_pairs={{0,12},{1,13},{2,14},{3,15},{4,0},{5,1},{6,2},{7,3},{8,4},{9,5},{1... | collective-permute-start | bytes 2555912 | tf_op jit(solution)/shard_map/ppermute | solution.py:44
  9.7 0.8 collective-permute-start.1
  10.6 0.9 collective-permute-start
  11.4 1.1 fusion.2
  12.5 0.0 copy-done.6
  12.5 0.6 fusion.10
  14.4 0.0 copy-done.4
  14.4 0.0 copy-done.5
  14.6 0.1 pad_maximum_fusion.8.level_ref
  14.6 1.1 fusion.6
  15.7 13.7 %collective-permute-done.2 = bf16[4,832,128]{2,1,0:T(8,128)(2,1)S(1)} collective-permute-done((bf16[4,832,128]{2,1,0:T(8,128)(2,1)}, bf16[4,832,128]{2,1,0:T(8,128)(2,1)S(1)}, u32[]{:S(2)}, u32[]{:S(2)}) %collective-permute-start.2) | collective-permute-done | bytes 852000 | tf_op jit(solution)/shard_map/ppermute | solution.py:44
  29.4 0.0 collective-permute-done.1
  29.5 3.8 %collective-permute-done = bf16[4,832,128]{2,1,0:T(8,128)(2,1)S(1)} collective-permute-done((bf16[4,832,128]{2,1,0:T(8,128)(2,1)}, bf16[4,832,128]{2,1,0:T(8,128)(2,1)S(1)}, u32[]{:S(2)}, u32[]{:S(2)}) %collective-permute-start) | collective-permute-done | bytes 852000 | tf_op jit(solution)/shard_map/ppermute | solution.py:44
  33.3 0.1 pad_maximum_fusion.1
  33.4 2.0 %collective-permute-start.3 = (bf16[4,448,128]{2,1,0:T(8,128)(2,1)S(1)}, bf16[4,448,128]{2,1,0:T(8,128)(2,1)S(1)}, u32[]{:S(2)}, u32[]{:S(2)}) collective-permute-start(bf16[4,448,128]{2,1,0:T(8,128)(2,1)S(1)} %pad_maximum_fusion.1), channel_id=1, source_target_pairs={{0,1},{1,2},{2,3},{3,0},{4,5},{5,6},{6,7},{7,4},{8,9},{9,10},{10,1... | collective-permute-start | bytes 1376264 | tf_op jit(solution)/shard_map/ppermute | solution.py:44
  35.4 0.1 pad_maximum_fusion.2
  35.4 3.7 %collective-permute-start.4 = (bf16[4,448,128]{2,1,0:T(8,128)(2,1)S(1)}, bf16[4,448,128]{2,1,0:T(8,128)(2,1)S(1)}, u32[]{:S(2)}, u32[]{:S(2)}) collective-permute-start(bf16[4,448,128]{2,1,0:T(8,128)(2,1)S(1)} %pad_maximum_fusion.2), channel_id=1, source_target_pairs={{0,2},{1,3},{2,0},{3,1},{4,6},{5,7},{6,4},{7,5},{8,10},{9,11},{10,... | collective-permute-start | bytes 1376264 | tf_op jit(solution)/shard_map/ppermute | solution.py:44
  39.1 0.1 pad_maximum_fusion.3
  39.2 1.1 collective-permute-start.5
  40.3 0.1 pad_maximum_fusion.5
  40.4 1.1 collective-permute-start.6
  41.5 0.1 pad_maximum_fusion.6
  41.5 0.5 collective-permute-start.7
  42.1 0.1 pad_maximum_fusion.4.refs_4_
  42.1 0.1 pad_maximum_fusion.7
  42.2 0.1 pad_maximum_fusion.refs_0_
  42.3 1.7 %collective-permute-done.3.refs_1_ = bf16[4,448,128]{2,1,0:T(8,128)(2,1)S(1)} collective-permute-done((bf16[4,448,128]{2,1,0:T(8,128)(2,1)S(1)}, bf16[4,448,128]{2,1,0:T(8,128)(2,1)S(1)}, u32[]{:S(2)}, u32[]{:S(2)}) %collective-permute-start.3) | collective-permute-done | bytes 458784 | tf_op jit(solution)/shard_map/ppermute | solution.py:44
  43.9 2.0 %collective-permute-start.8 = (bf16[4,384,128]{2,1,0:T(8,128)(2,1)S(1)}, bf16[4,384,128]{2,1,0:T(8,128)(2,1)S(1)}, u32[]{:S(2)}, u32[]{:S(2)}) collective-permute-start(bf16[4,384,128]{2,1,0:T(8,128)(2,1)S(1)} %pad_maximum_fusion.7), channel_id=1, source_target_pairs={{0,3},{1,0},{2,1},{3,2},{4,7},{5,4},{6,5},{7,6},{8,11},{9,8},{10,9... | collective-permute-start | bytes 1179656 | tf_op jit(solution)/shard_map/ppermute | solution.py:44
  46.0 4.5 %collective-permute-done.4.refs_2_ = bf16[4,448,128]{2,1,0:T(8,128)(2,1)S(1)} collective-permute-done((bf16[4,448,128]{2,1,0:T(8,128)(2,1)S(1)}, bf16[4,448,128]{2,1,0:T(8,128)(2,1)S(1)}, u32[]{:S(2)}, u32[]{:S(2)}) %collective-permute-start.4) | collective-permute-done | bytes 458784 | tf_op jit(solution)/shard_map/ppermute | solution.py:44
  50.4 0.0 collective-permute-done.5.refs_3_
  50.4 0.0 copy-done.2
  50.4 0.0 slice-start.1
  50.4 11.6 %attend.2.refs_8_ = f32[2,72,4096]{2,1,0:T(8,128)S(1)} custom-call(s32[5]{0:T(128)S(1)} %copy-done.2, bf16[4,448,128]{2,1,0:T(8,128)(2,1)S(1)} %pad_maximum_fusion.refs_0_, bf16[4,448,128]{2,1,0:T(8,128)(2,1)S(1)} %collective-permute-done.3.refs_1_, bf16[4,448,128]{2,1,0:T(8,128)(2,1)S(1)} %collective-permute-done.4.refs_2_, ...), custom_call_target="tpu_custom_call" | custom-call | flops 12884901888 | bytes 2097152 | tf_op jit(solution)/shard_map/attend/pallas_call | solution.py:223
  62.1 0.0 slice-start.2
  62.1 0.0 collective-permute-done.6.refs_5_
  62.1 0.0 collective-permute-done.7.refs_6_
  62.1 0.0 collective-permute-done.8.refs_7_
  62.1 21.8 %attend.3 = bf16[16,256,128]{2,1,0:T(8,128)(2,1)S(1)} custom-call(s32[5]{0:T(128)S(1)} %copy-done.2, bf16[4,448,128]{2,1,0:T(8,128)(2,1)S(1)} %pad_maximum_fusion.refs_0_, bf16[4,448,128]{2,1,0:T(8,128)(2,1)S(1)} %collective-permute-done.3.refs_1_, bf16[4,448,128]{2,1,0:T(8,128)(2,1)S(1)} %collective-permute-done.4.refs_2_, ...), custom_call_target="tpu_custom_call" | custom-call | flops 24696061952 | bytes 2097152 | tf_op jit(solution)/shard_map/attend/pallas_call | solution.py:223
  83.9 0.0 copy-start
  83.9 0.0 copy-start.1
  84.0 19.1 %all_to_all.10.got_ref = bf16[16,256,128]{2,1,0:T(8,128)(2,1)S(1)} all-to-all(bf16[16,256,128]{2,1,0:T(8,128)(2,1)S(1)} %attend.3), channel_id=1, replica_groups=mesh['tm'=8,'seq'=16] {'seq'}, dimensions={0} | all-to-all | bytes 2097152 | tf_op jit(solution)/shard_map/all_to_all | solution.py:317
  103.1 0.0 slice-done.1
  103.1 0.0 copy-start.3
  103.1 5.6 %project.1 = (f32[64,256]{1,0:T(8,128)}, f32[64,256]{1,0:T(8,128)S(1)}, bf16[8,64,256]{2,1,0:T(8,128)(2,1)S(1)}) custom-call(s32[5]{0:T(128)S(1)} %copy-done.2, f32[2]{0:T(128)S(1)} %pad_maximum_fusion.8.level_ref, bf16[16,256,128]{2,1,0:T(8,128)(2,1)S(1)} %all_to_all.10.got_ref, bf16[256,2432]{1,0:T(8,128)(2,1)S(1)} %bitcast.25, ...), custom_call_target="tpu_custom_call" | custom-call | flops 2550136832 | bytes 12582912 | tf_op jit(solution)/shard_map/project/pallas_call | solution.py:269
  108.7 11.8 %all_to_all.11 = bf16[8,64,256]{2,1,0:T(8,128)(2,1)S(1)} all-to-all(bf16[8,64,256]{2,1,0:T(8,128)(2,1)S(1)} %get-tuple-element.29), channel_id=1, replica_groups=mesh['tm'=8,'seq'=16] {'tm'}, dimensions={0} | all-to-all | bytes 524288 | tf_op jit(solution)/shard_map/all_to_all | solution.py:319
  120.5 0.6 fusion.1
  (20 shorter events, 0.3 us)
Async XLA Ops:
  1.3 11.2 %copy-start.6 = (s32[9]{0:T(128)S(1)}, s32[9]{0:T(128)}, u32[]{:S(2)}) copy-start(s32[9]{0:T(128)} %param.19) | copy-start | bytes 112
  1.3 13.1 %copy-start.4 = (f32[2432]{0:T(1024)S(1)}, f32[2432]{0:T(1024)}, u32[]{:S(2)}) copy-start(f32[2432]{0:T(1024)} %param.16) | copy-start | bytes 29188
  1.3 13.1 %copy-start.5 = (f32[2432]{0:T(1024)S(1)}, f32[2432]{0:T(1024)}, u32[]{:S(2)}) copy-start(f32[2432]{0:T(1024)} %param.17) | copy-start | bytes 29188
  6.8 22.6 %collective-permute-start.2 = (bf16[4,832,128]{2,1,0:T(8,128)(2,1)}, bf16[4,832,128]{2,1,0:T(8,128)(2,1)S(1)}, u32[]{:S(2)}, u32[]{:S(2)}) collective-permute-start(bf16[4,832,128]{2,1,0:T(8,128)(2,1)} %get-tuple-element.19), channel_id=1, source_target_pairs={{0,12},{1,13},{2,14},{3,15},{4,0},{5,1},{6,2},{7,3},{8,4},{9,5},{1... | collective-permute-start | bytes 2555912 | tf_op jit(solution)/shard_map/ppermute | solution.py:44
  9.7 19.7 %collective-permute-start.1 = (bf16[4,832,128]{2,1,0:T(8,128)(2,1)}, bf16[4,832,128]{2,1,0:T(8,128)(2,1)S(1)}, u32[]{:S(2)}, u32[]{:S(2)}) collective-permute-start(bf16[4,832,128]{2,1,0:T(8,128)(2,1)} %get-tuple-element.18), channel_id=1, source_target_pairs={{0,8},{1,9},{2,10},{3,11},{4,12},{5,13},{6,14},{7,15},{8,0},{9,1},... | collective-permute-start | bytes 2555912 | tf_op jit(solution)/shard_map/ppermute | solution.py:44
  10.6 22.7 %collective-permute-start = (bf16[4,832,128]{2,1,0:T(8,128)(2,1)}, bf16[4,832,128]{2,1,0:T(8,128)(2,1)S(1)}, u32[]{:S(2)}, u32[]{:S(2)}) collective-permute-start(bf16[4,832,128]{2,1,0:T(8,128)(2,1)} %get-tuple-element.17), channel_id=1, source_target_pairs={{0,4},{1,5},{2,6},{3,7},{4,8},{5,9},{6,10},{7,11},{8,12},{9,13},{1... | collective-permute-start | bytes 2555912 | tf_op jit(solution)/shard_map/ppermute | solution.py:44
  33.4 10.6 %collective-permute-start.3 = (bf16[4,448,128]{2,1,0:T(8,128)(2,1)S(1)}, bf16[4,448,128]{2,1,0:T(8,128)(2,1)S(1)}, u32[]{:S(2)}, u32[]{:S(2)}) collective-permute-start(bf16[4,448,128]{2,1,0:T(8,128)(2,1)S(1)} %pad_maximum_fusion.1), channel_id=1, source_target_pairs={{0,1},{1,2},{2,3},{3,0},{4,5},{5,6},{6,7},{7,4},{8,9},{9,10},{10,1... | collective-permute-start | bytes 1376264 | tf_op jit(solution)/shard_map/ppermute | solution.py:44
  35.4 15.0 %collective-permute-start.4 = (bf16[4,448,128]{2,1,0:T(8,128)(2,1)S(1)}, bf16[4,448,128]{2,1,0:T(8,128)(2,1)S(1)}, u32[]{:S(2)}, u32[]{:S(2)}) collective-permute-start(bf16[4,448,128]{2,1,0:T(8,128)(2,1)S(1)} %pad_maximum_fusion.2), channel_id=1, source_target_pairs={{0,2},{1,3},{2,0},{3,1},{4,6},{5,7},{6,4},{7,5},{8,10},{9,11},{10,... | collective-permute-start | bytes 1376264 | tf_op jit(solution)/shard_map/ppermute | solution.py:44
  39.2 11.3 %collective-permute-start.5 = (bf16[4,448,128]{2,1,0:T(8,128)(2,1)S(1)}, bf16[4,448,128]{2,1,0:T(8,128)(2,1)S(1)}, u32[]{:S(2)}, u32[]{:S(2)}) collective-permute-start(bf16[4,448,128]{2,1,0:T(8,128)(2,1)S(1)} %pad_maximum_fusion.3), channel_id=1, source_target_pairs={{0,3},{1,0},{2,1},{3,2},{4,7},{5,4},{6,5},{7,6},{8,11},{9,8},{10,9... | collective-permute-start | bytes 1376264 | tf_op jit(solution)/shard_map/ppermute | solution.py:44
  40.4 21.7 %collective-permute-start.6 = (bf16[4,384,128]{2,1,0:T(8,128)(2,1)S(1)}, bf16[4,384,128]{2,1,0:T(8,128)(2,1)S(1)}, u32[]{:S(2)}, u32[]{:S(2)}) collective-permute-start(bf16[4,384,128]{2,1,0:T(8,128)(2,1)S(1)} %pad_maximum_fusion.5), channel_id=1, source_target_pairs={{0,1},{1,2},{2,3},{3,0},{4,5},{5,6},{6,7},{7,4},{8,9},{9,10},{10,1... | collective-permute-start | bytes 1179656 | tf_op jit(solution)/shard_map/ppermute | solution.py:44
  41.5 20.6 %collective-permute-start.7 = (bf16[4,384,128]{2,1,0:T(8,128)(2,1)S(1)}, bf16[4,384,128]{2,1,0:T(8,128)(2,1)S(1)}, u32[]{:S(2)}, u32[]{:S(2)}) collective-permute-start(bf16[4,384,128]{2,1,0:T(8,128)(2,1)S(1)} %pad_maximum_fusion.6), channel_id=1, source_target_pairs={{0,2},{1,3},{2,0},{3,1},{4,6},{5,7},{6,4},{7,5},{8,10},{9,11},{10,... | collective-permute-start | bytes 1179656 | tf_op jit(solution)/shard_map/ppermute | solution.py:44
  42.1 8.4 %copy-start.2 = (s32[5]{0:T(128)S(1)}, s32[5]{0:T(128)}, u32[]{:S(2)}) copy-start(s32[5]{0:T(128)} %stack.56.place_ref) | copy-start | bytes 64
  43.9 18.2 %collective-permute-start.8 = (bf16[4,384,128]{2,1,0:T(8,128)(2,1)S(1)}, bf16[4,384,128]{2,1,0:T(8,128)(2,1)S(1)}, u32[]{:S(2)}, u32[]{:S(2)}) collective-permute-start(bf16[4,384,128]{2,1,0:T(8,128)(2,1)S(1)} %pad_maximum_fusion.7), channel_id=1, source_target_pairs={{0,3},{1,0},{2,1},{3,2},{4,7},{5,4},{6,5},{7,6},{8,11},{9,8},{10,9... | collective-permute-start | bytes 1179656 | tf_op jit(solution)/shard_map/ppermute | solution.py:44
  50.4 52.7 %slice-start = ((s8[9961472]{0:T(1024)(128)(4,1)}), s8[4194304]{0:T(1024)(128)(4,1)S(1)}, s32[]{:S(2)}) async-start(s8[9961472]{0:T(1024)(128)(4,1)} %bitcast.23), calls=%async_computation.2 | async-start | bytes 8388608
  50.4 52.7 %slice-start.1 = ((s8[9961472]{0:T(1024)(128)(4,1)}), s8[4194304]{0:T(1024)(128)(4,1)S(1)}, s32[]{:S(2)}) async-start(s8[9961472]{0:T(1024)(128)(4,1)} %bitcast.23), calls=%async_computation.3 | async-start | bytes 8388608
  62.1 41.0 %slice-start.2 = ((s8[9961472]{0:T(1024)(128)(4,1)}), s8[1572864]{0:T(1024)(128)(4,1)S(1)}, s32[]{:S(2)}) async-start(s8[9961472]{0:T(1024)(128)(4,1)} %bitcast.23), calls=%async_computation.4 | async-start | bytes 3145728
  83.9 19.2 %copy-start = (bf16[1,256,2432]{2,1,0:T(8,128)(2,1)S(1)}, bf16[1,256,2432]{2,1,0:T(8,128)(2,1)}, u32[]{:S(2)}) copy-start(bf16[1,256,2432]{2,1,0:T(8,128)(2,1)} %param.13) | copy-start | bytes 3735556
  83.9 19.2 %copy-start.1 = (bf16[2432,64]{0,1:T(8,128)(2,1)S(1)}, bf16[2432,64]{0,1:T(8,128)(2,1)}, u32[]{:S(2)}) copy-start(bf16[2432,64]{0,1:T(8,128)(2,1)} %param.15) | copy-start | bytes 933892
  103.1 17.4 %copy-start.3 = (f32[256,64]{0,1:T(8,128)S(1)}, f32[256,64]{0,1:T(8,128)}, u32[]{:S(2)}) copy-start(f32[256,64]{0,1:T(8,128)} %param.18) | copy-start | bytes 196612

commit v5 on v4

--- a/solution.py
+++ b/solution.py
@@ -22,7 +22,7 @@
 QROWS = 256
 KROWS = 280
 TILE = 512
-BLOCK_Q = 1024
+BLOCK_Q = 2048
 VROWS = 128
 MIB = 2**20
 
@@ -69,61 +69,66 @@
     return places, at
 
 
-def pack_kernel(place_ref, q_hbm, k_hbm, v_hbm, *refs):
-    outs, (q_buf, k_buf, v_buf, sems) = refs[:RING], refs[RING:]
+def pack_kernel(shifts, place_ref, q_hbm, k_hbm, v_hbm, *refs):
+    outs, (q_buf, k_buf, v_buf, sems) = refs[: len(shifts)], refs[len(shifts) :]
     places, _ = layout()
-    order = (1, 3, 2, 0)
-    copies = {}
-    for d in order:
+    copies = []
+    for i, d in enumerate(shifts):
         group = lax.rem(place_ref[0] + d, RING)
         lanes = pl.ds(pl.multiple_of(group * (RING * PAIR), RING * PAIR), RING * PAIR)
-        copies[d] = [
-            pltpu.make_async_copy(source.at[:, lanes], target.at[d], sems.at[d, n])
-            for n, (source, target) in enumerate(((q_hbm, q_buf), (k_hbm, k_buf), (v_hbm, v_buf)))
-        ]
-        for copy in copies[d]:
+        copies.append(
+            [
+                pltpu.make_async_copy(source.at[:, lanes], target.at[i], sems.at[i, n])
+                for n, (source, target) in enumerate(((q_hbm, q_buf), (k_hbm, k_buf), (v_hbm, v_buf)))
+            ]
+        )
+        for copy in copies[i]:
             copy.start()
-    for d in order:
-        for copy in copies[d]:
+    for i in range(len(shifts)):
+        for copy in copies[i]:
             copy.wait()
-        out = outs[d]
+        out = outs[i]
         for e in range(RING):
             pair = lax.rem(place_ref[1] + e, RING)
             lanes = pl.ds(pl.multiple_of(pair * PAIR, PAIR), PAIR)
-            out[e, 0:QROWS] = head_norm(q_buf[d, :, lanes])
-            keys = head_norm(k_buf[d, :, lanes])
+            out[e, 0:QROWS] = head_norm(q_buf[i, :, lanes])
+            keys = head_norm(k_buf[i, :, lanes])
             for (k0, k1), (kp, vp) in zip(KEY_CUTS, places):
                 out[e, kp : kp + k1 - k0] = keys[k0:k1]
-                out[e, vp : vp + k1 - k0] = v_buf[d, k0:k1, lanes]
+                out[e, vp : vp + k1 - k0] = v_buf[i, k0:k1, lanes]
                 gap = padded(k1 - k0) - (k1 - k0)
                 if gap:
                     out[e, vp - gap : vp] = jnp.zeros((gap, PAIR), jnp.bfloat16)
                     out[e, vp + k1 - k0 : vp + k1 - k0 + gap] = jnp.zeros((gap, PAIR), jnp.bfloat16)
 
 
-def pack(place, queries, keys, values):
+def pack(place, queries, keys, values, shifts):
     _, rows = layout()
     vmem = pl.BlockSpec(memory_space=pltpu.VMEM)
     wide = RING * PAIR
+    count = len(shifts)
     return pl.pallas_call(
-        pack_kernel,
+        functools.partial(pack_kernel, shifts),
         in_specs=[pl.BlockSpec(memory_space=pltpu.SMEM)] + [pl.BlockSpec(memory_space=pltpu.HBM)] * 3,
-        out_specs=[vmem] * RING,
-        out_shape=[jax.ShapeDtypeStruct((RING, rows, PAIR), jnp.bfloat16)] * RING,
+        out_specs=[vmem] * count,
+        out_shape=[jax.ShapeDtypeStruct((RING, rows, PAIR), jnp.bfloat16)] * count,
         scratch_shapes=[
-            pltpu.VMEM((RING, QROWS, wide), jnp.bfloat16),
-            pltpu.VMEM((RING, KROWS, wide), jnp.bfloat16),
-            pltpu.VMEM((RING, KROWS, wide), jnp.bfloat16),
-            pltpu.SemaphoreType.DMA((RING, 3)),
+            pltpu.VMEM((count, QROWS, wide), jnp.bfloat16),
+            pltpu.VMEM((count, KROWS, wide), jnp.bfloat16),
+            pltpu.VMEM((count, KROWS, wide), jnp.bfloat16),
+            pltpu.SemaphoreType.DMA((count, 3)),
         ],
         compiler_params=pltpu.CompilerParams(vmem_limit_bytes=59 * MIB),
-        cost_estimate=pl.CostEstimate(flops=2 * 2 * rows * HD * PAIR, bytes_accessed=4 * rows * HD, transcendentals=0),
+        cost_estimate=pl.CostEstimate(
+            flops=count * rows * HD * PAIR, bytes_accessed=count * rows * HD, transcendentals=0
+        ),
         name="pack",
     )(place, queries, keys, values)
 
 
-def first_hop(parts):
-    return [parts[0]] + [send(parts[d], True, d) for d in range(1, RING)]
+def first_hop(place, queries, keys, values):
+    up, down, across, own = pack(place, queries, keys, values, (1, 3, 2, 0))
+    return [own, send(up, True, 1), send(across, True, 2), send(down, True, 3)]
 
 
 def second_hop(landed, start, stop):
@@ -240,27 +245,27 @@
 
 
 def project_kernel(place_ref, level_ref, got_ref, hidden_ref, w_proj_ref, w_final_ref, base_ref, slope_ref, *refs):
-    velocity_ref, drift_ref, later_ref, joined, gated = refs
+    velocity_ref, drift_ref, joined = refs
     for j in range(RING * RING):
         hi, lo = divmod(j, RING)
         pair = hi * place_ref[2] + lo * place_ref[3]
         joined[:, pl.ds(pl.multiple_of(pair * PAIR, PAIR), PAIR)] = got_ref[j]
     squares = jnp.zeros((QROWS, 1), jnp.float32)
+    product = jnp.zeros((LAT, QROWS), jnp.float32)
     for start, size in cuts_of(D, 512):
         cols = slice(start, start + size)
         projected = jnp.dot(joined[...], w_proj_ref[:, cols], preferred_element_type=jnp.float32)
         gate = base_ref[:, cols] + level_ref[0] * slope_ref[:, cols]
         value = hidden_ref[:, cols].astype(jnp.float32) + gate * projected
-        gated[:, cols] = value
+        product = product + lax.dot_general(
+            w_final_ref[:, cols], value.astype(jnp.bfloat16), NT, preferred_element_type=jnp.float32
+        )
         squares = squares + jnp.sum(value * value, axis=1, keepdims=True)
-    normed = (gated[...] * lax.rsqrt(squares * (1.0 / D) + 1e-06)).astype(jnp.bfloat16)
-    velocity = lax.dot_general(w_final_ref[...], normed, NT, preferred_element_type=jnp.float32)
+    along = jnp.broadcast_to(squares, (QROWS, PAIR)).T[0:1]
+    velocity = product * lax.rsqrt(along * (1.0 / D) + 1e-06)
     velocity_ref[...] = velocity
     drift = velocity * level_ref[1]
     drift_ref[...] = drift
-    low = drift.astype(jnp.bfloat16)
-    for k in range(SLOTS):
-        later_ref[k] = jnp.where(place_ref[4] < k, low, jnp.zeros_like(low))
 
 
 def project(place, level, got, hidden, w_proj, w_final, base, slope):
@@ -269,13 +274,12 @@
     return pl.pallas_call(
         project_kernel,
         in_specs=[smem, smem] + [vmem] * 6,
-        out_specs=[vmem] * 3,
+        out_specs=[vmem] * 2,
         out_shape=[
             jax.ShapeDtypeStruct((LAT, QROWS), jnp.float32),
             jax.ShapeDtypeStruct((LAT, QROWS), jnp.float32),
-            jax.ShapeDtypeStruct((SLOTS, LAT, QROWS), jnp.bfloat16),
         ],
-        scratch_shapes=[pltpu.VMEM((QROWS, HD), jnp.bfloat16), pltpu.VMEM((QROWS, D), jnp.float32)],
+        scratch_shapes=[pltpu.VMEM((QROWS, HD), jnp.bfloat16)],
         compiler_params=pltpu.CompilerParams(vmem_limit_bytes=16 * MIB),
         cost_estimate=pl.CostEstimate(flops=2 * QROWS * HD * D, bytes_accessed=12 * MIB, transcendentals=0),
         name="project",
@@ -303,7 +307,7 @@
 
     places, end = layout()
     starts = [0] + [kp for kp, _ in places[1:]] + [end]
-    landed = first_hop(pack(place, queries[0], keys[0], values[0]))
+    landed = first_hop(place, queries[0], keys[0], values[0])
     received = [second_hop(landed, start, stop) for start, stop in zip(starts, starts[1:])]
     acc = None
     for number, ((k0, k1), (kp, vp)) in enumerate(zip(KEY_CUTS, places)):
@@ -311,13 +315,18 @@
         last = number == len(KEY_CUTS) - 1
         got = attend(place, received[0], received[number], acc, k1 - k0, kp - start, vp - start, last)
         acc = None if last else got[0]
-    got, *operands = lax.optimization_barrier(
-        (got[0], level, hidden[0], w_proj, w_final.T, gate_base[None], gate_slope[None])
+    ahead = (lax.broadcasted_iota(jnp.int32, (SLOTS // 2, LAT, QROWS), 0) > slot // 2).astype(jnp.float32)
+    from_other = jnp.broadcast_to(jnp.where(even, 0.0, 1.0), (LAT, QROWS))
+    got, ahead, from_other, *operands = lax.optimization_barrier(
+        (got[0], ahead, from_other, level, hidden[0], w_proj, w_final.T, gate_base[None], gate_slope[None])
     )
     got = lax.all_to_all(got, "seq", 0, 0, tiled=True)
-    velocity, drift, later = project(place, operands[0], got, *operands[1:])
-    earlier = lax.all_to_all(later, "tm", 0, 0, tiled=True).astype(jnp.float32)
-    latents = start_latent.T + drift + jnp.sum(earlier, axis=0)
+    velocity, drift = project(place, operands[0], got, *operands[1:])
+    other = lax.ppermute(drift, "tm", [(i, i ^ 1) for i in range(SLOTS)])
+    later = (ahead * (drift + other)[None]).astype(jnp.bfloat16)
+    groups = [[core + 2 * chip for chip in range(SLOTS // 2)] for core in range(2)]
+    earlier = lax.all_to_all(later, "tm", 0, 0, axis_index_groups=groups, tiled=True).astype(jnp.float32)
+    latents = start_latent.T + drift + from_other * other + jnp.sum(earlier, axis=0)
     return (velocity.T[None], latents.T[None])
 
 

time: 122 us -> 120 us (0.984)
  Pallas kernels: 44.5 us -> 43 us
  blocking collectives: 30.9 us -> 29.4 us
  waiting for transfers between devices: 23.6 us -> 24.9 us
    all_to_all x1, blocking collectives: 11.8 us -> 10.2 us  [per_device(): lax.all_to_all(later, 'tm', 0, 0, axis_index_groups=groups, tiled=True)]
    ppermute x0 -> x1, waiting for transfers between devices: none -> 1.25 us  [per_device(): other = lax.ppermute(drift, 'tm', [(i, i ^ 1) for i in range(SLOTS)])]
  transfers between devices with their start and end apart: 9 -> 10, of which waited for: 4 -> 5; matrix products, arithmetic and copies ran while one was open for 3% -> 3% of each run, Pallas kernels for 10% -> 9%
where the time goes in v5:
time: 120 us; the launch traced here: 119 us
  Pallas kernels  43 us (36%)
  blocking collectives  29.4 us (24%)
  waiting for transfers between devices  24.9 us (21%)
  starting transfers between devices  15 us (12%)
  local copies, waits for them, and re-layouts  3.71 us (3%)
  between operations  2.37 us (2%)
  other arithmetic  1.24 us (1%)
    pallas_call x2, Pallas kernels, attend(): pl.pallas_call(functools.partial(attend_kernel, nk, kp, vp, first, last),...  32.5 us
    ppermute x9, waiting for transfers between devices, send(): return lax.ppermute(value, BOTH, ring_perm(first, shift % RING))  23.6 us
    all_to_all x1, blocking collectives, per_device(): got = lax.all_to_all(got, 'seq', 0, 0, tiled=True)  19.1 us
    ppermute x9, starting transfers between devices, send(): return lax.ppermute(value, BOTH, ring_perm(first, shift % RING))  14.9 us
    all_to_all x1, blocking collectives, per_device(): lax.all_to_all(later, 'tm', 0, 0, axis_index_groups=groups, tiled=True)  10.2 us
    pallas_call x1, Pallas kernels, pack(): pl.pallas_call(functools.partial(pack_kernel, shifts), in_specs=[pl.Block...  5.47 us
    pallas_call x1, Pallas kernels, project(): pl.pallas_call(project_kernel, in_specs=[smem, smem] + [vmem] * 6, out_sp...  5.02 us
  transfers between devices with their start and end apart: 10, of which 5 were waited for; matrix products, arithmetic and copies ran while one was open for 3% of the time, Pallas kernels for 9%

profile of v5, /device:TPU:0, one launch (start us, length us, event | category | flops | bytes accessed | tf_op | source)
XLA Modules:
  0.0 119.5 jit_solution(5724652972767412518)
XLA Ops:
  0.7 0.6 stack.56.place_ref
  1.3 5.5 %pack.1 = (bf16[4,832,128]{2,1,0:T(8,128)(2,1)}, bf16[4,832,128]{2,1,0:T(8,128)(2,1)}, bf16[4,832,128]{2,1,0:T(8,128)(2,1)}, bf16[4,832,128]{2,1,0:T(8,128)(2,1)}) custom-call(s32[5]{0:T(128)} %stack.56.place_ref, bf16[256,2048]{1,0:T(8,128)(2,1)} %bitcast.31, bf16[280,2048]{1,0:T(8,128)(2,1)} %bitcast.29, bf16[280,2048]{1,0:T(8,128)(2,1)} %bitcast.30), custom_call_target="tpu_custom_call" | custom-call | flops 872415232 | bytes 6815744 | tf_op jit(solution)/shard_map/pack/pallas_call | solution.py:110
  6.8 2.9 %collective-permute-start.2 = (bf16[4,832,128]{2,1,0:T(8,128)(2,1)}, bf16[4,832,128]{2,1,0:T(8,128)(2,1)S(1)}, u32[]{:S(2)}, u32[]{:S(2)}) collective-permute-start(bf16[4,832,128]{2,1,0:T(8,128)(2,1)} %get-tuple-element.20), channel_id=1, source_target_pairs={{0,12},{1,13},{2,14},{3,15},{4,0},{5,1},{6,2},{7,3},{8,4},{9,5},{1... | collective-permute-start | bytes 2555912 | tf_op jit(solution)/shard_map/ppermute | solution.py:44
  9.7 0.8 collective-permute-start.1
  10.5 0.9 collective-permute-start
  11.4 1.1 fusion.3
  12.4 0.0 copy-done.6
  12.5 0.6 fusion.11
  14.5 0.1 pad_maximum_fusion.8.level_ref
  14.6 1.1 fusion.7
  15.7 13.7 %collective-permute-done.2 = bf16[4,832,128]{2,1,0:T(8,128)(2,1)S(1)} collective-permute-done((bf16[4,832,128]{2,1,0:T(8,128)(2,1)}, bf16[4,832,128]{2,1,0:T(8,128)(2,1)S(1)}, u32[]{:S(2)}, u32[]{:S(2)}) %collective-permute-start.2) | collective-permute-done | bytes 852000 | tf_op jit(solution)/shard_map/ppermute | solution.py:44
  29.4 0.0 collective-permute-done.1
  29.4 3.8 %collective-permute-done = bf16[4,832,128]{2,1,0:T(8,128)(2,1)S(1)} collective-permute-done((bf16[4,832,128]{2,1,0:T(8,128)(2,1)}, bf16[4,832,128]{2,1,0:T(8,128)(2,1)S(1)}, u32[]{:S(2)}, u32[]{:S(2)}) %collective-permute-start) | collective-permute-done | bytes 852000 | tf_op jit(solution)/shard_map/ppermute | solution.py:44
  33.2 0.1 pad_maximum_fusion.1
  33.3 2.0 %collective-permute-start.3 = (bf16[4,448,128]{2,1,0:T(8,128)(2,1)S(1)}, bf16[4,448,128]{2,1,0:T(8,128)(2,1)S(1)}, u32[]{:S(2)}, u32[]{:S(2)}) collective-permute-start(bf16[4,448,128]{2,1,0:T(8,128)(2,1)S(1)} %pad_maximum_fusion.1), channel_id=1, source_target_pairs={{0,1},{1,2},{2,3},{3,0},{4,5},{5,6},{6,7},{7,4},{8,9},{9,10},{10,1... | collective-permute-start | bytes 1376264 | tf_op jit(solution)/shard_map/ppermute | solution.py:44
  35.3 0.1 pad_maximum_fusion.2
  35.3 3.7 %collective-permute-start.4 = (bf16[4,448,128]{2,1,0:T(8,128)(2,1)S(1)}, bf16[4,448,128]{2,1,0:T(8,128)(2,1)S(1)}, u32[]{:S(2)}, u32[]{:S(2)}) collective-permute-start(bf16[4,448,128]{2,1,0:T(8,128)(2,1)S(1)} %pad_maximum_fusion.2), channel_id=1, source_target_pairs={{0,2},{1,3},{2,0},{3,1},{4,6},{5,7},{6,4},{7,5},{8,10},{9,11},{10,... | collective-permute-start | bytes 1376264 | tf_op jit(solution)/shard_map/ppermute | solution.py:44
  39.0 0.1 pad_maximum_fusion.3
  39.1 1.1 collective-permute-start.5
  40.2 0.1 pad_maximum_fusion.5
  40.3 1.1 collective-permute-start.6
  41.4 0.1 pad_maximum_fusion.6
  41.5 0.5 collective-permute-start.7
  42.0 0.1 pad_maximum_fusion.4.refs_4_
  42.0 0.1 pad_maximum_fusion.7
  42.1 0.1 pad_maximum_fusion.refs_0_
  42.2 1.7 %collective-permute-done.3.refs_1_ = bf16[4,448,128]{2,1,0:T(8,128)(2,1)S(1)} collective-permute-done((bf16[4,448,128]{2,1,0:T(8,128)(2,1)S(1)}, bf16[4,448,128]{2,1,0:T(8,128)(2,1)S(1)}, u32[]{:S(2)}, u32[]{:S(2)}) %collective-permute-start.3) | collective-permute-done | bytes 458784 | tf_op jit(solution)/shard_map/ppermute | solution.py:44
  43.9 2.0 %collective-permute-start.8 = (bf16[4,384,128]{2,1,0:T(8,128)(2,1)S(1)}, bf16[4,384,128]{2,1,0:T(8,128)(2,1)S(1)}, u32[]{:S(2)}, u32[]{:S(2)}) collective-permute-start(bf16[4,384,128]{2,1,0:T(8,128)(2,1)S(1)} %pad_maximum_fusion.7), channel_id=1, source_target_pairs={{0,3},{1,0},{2,1},{3,2},{4,7},{5,4},{6,5},{7,6},{8,11},{9,8},{10,9... | collective-permute-start | bytes 1179656 | tf_op jit(solution)/shard_map/ppermute | solution.py:44
  45.9 4.5 %collective-permute-done.4.refs_2_ = bf16[4,448,128]{2,1,0:T(8,128)(2,1)S(1)} collective-permute-done((bf16[4,448,128]{2,1,0:T(8,128)(2,1)S(1)}, bf16[4,448,128]{2,1,0:T(8,128)(2,1)S(1)}, u32[]{:S(2)}, u32[]{:S(2)}) %collective-permute-start.4) | collective-permute-done | bytes 458784 | tf_op jit(solution)/shard_map/ppermute | solution.py:44
  50.4 0.0 collective-permute-done.5.refs_3_
  50.4 0.0 copy-done.2
  50.4 0.0 slice-start.1
  50.4 11.2 %attend.2.refs_8_ = f32[2,72,4096]{2,1,0:T(8,128)S(1)} custom-call(s32[5]{0:T(128)S(1)} %copy-done.2, bf16[4,448,128]{2,1,0:T(8,128)(2,1)S(1)} %pad_maximum_fusion.refs_0_, bf16[4,448,128]{2,1,0:T(8,128)(2,1)S(1)} %collective-permute-done.3.refs_1_, bf16[4,448,128]{2,1,0:T(8,128)(2,1)S(1)} %collective-permute-done.4.refs_2_, ...), custom_call_target="tpu_custom_call" | custom-call | flops 12884901888 | bytes 2097152 | tf_op jit(solution)/shard_map/attend/pallas_call | solution.py:228
  61.5 0.0 slice-start.2
  61.6 0.0 collective-permute-done.6.refs_5_
  61.6 0.0 collective-permute-done.7.refs_6_
  61.6 0.0 collective-permute-done.8.refs_7_
  61.6 21.3 %attend.3 = bf16[16,256,128]{2,1,0:T(8,128)(2,1)S(1)} custom-call(s32[5]{0:T(128)S(1)} %copy-done.2, bf16[4,448,128]{2,1,0:T(8,128)(2,1)S(1)} %pad_maximum_fusion.refs_0_, bf16[4,448,128]{2,1,0:T(8,128)(2,1)S(1)} %collective-permute-done.3.refs_1_, bf16[4,448,128]{2,1,0:T(8,128)(2,1)S(1)} %collective-permute-done.4.refs_2_, ...), custom_call_target="tpu_custom_call" | custom-call | flops 24696061952 | bytes 2097152 | tf_op jit(solution)/shard_map/attend/pallas_call | solution.py:228
  82.9 0.0 copy-start
  82.9 0.0 copy-start.1
  83.0 0.1 iota.7
  83.1 19.1 %all_to_all.10.got_ref = bf16[16,256,128]{2,1,0:T(8,128)(2,1)S(1)} all-to-all(bf16[16,256,128]{2,1,0:T(8,128)(2,1)S(1)} %attend.3), channel_id=1, replica_groups=mesh['tm'=8,'seq'=16] {'seq'}, dimensions={0} | all-to-all | bytes 2097152 | tf_op jit(solution)/shard_map/all_to_all | solution.py:323
  102.2 0.0 copy-start.3
  102.3 5.0 %project.1 = (f32[64,256]{1,0:T(8,128)}, f32[64,256]{1,0:T(8,128)S(1)}) custom-call(s32[5]{0:T(128)S(1)} %copy-done.2, f32[2]{0:T(128)S(1)} %pad_maximum_fusion.8.level_ref, bf16[16,256,128]{2,1,0:T(8,128)(2,1)S(1)} %all_to_all.10.got_ref, bf16[256,2432]{1,0:T(8,128)(2,1)S(1)} %bitcast.27, bf16[2048,2432]{1,0:T(8,128)(2,1)S(1)} %bitcast.26, ...), custom_call_target="tpu_custom_call" | custom-call | flops 2550136832 | bytes 12582912 | tf_op jit(solution)/shard_map/project/pallas_call | solution.py:274
  107.3 0.0 collective-permute-start.9
  107.3 1.3 %collective-permute-done.9 = f32[64,256]{1,0:T(8,128)S(1)} collective-permute-done((f32[64,256]{1,0:T(8,128)S(1)}, f32[64,256]{1,0:T(8,128)S(1)}, u32[]{:S(2)}, u32[]{:S(2)}) %collective-permute-start.9) | collective-permute-done | bytes 65568 | tf_op jit(solution)/shard_map/ppermute | solution.py:325
  108.6 10.2 %all_to_all.11 = bf16[4,64,256]{2,1,0:T(8,128)(2,1)S(1)} all-to-all(bf16[4,64,256]{2,1,0:T(8,128)(2,1)S(1)} %multiply_convert_fusion), channel_id=1, replica_groups={{0,32,64,96},{16,48,80,112},{1,33,65,97},{17,49,81,113},{2,34,66,98},{1..., dimensions={0} | all-to-all | bytes 262144 | tf_op jit(solution)/shard_map/all_to_all | solution.py:328
  118.8 0.7 fusion.2
  (27 shorter events, 0.3 us)
Async XLA Ops:
  1.3 11.2 %copy-start.6 = (s32[9]{0:T(128)S(1)}, s32[9]{0:T(128)}, u32[]{:S(2)}) copy-start(s32[9]{0:T(128)} %param.19) | copy-start | bytes 112
  1.3 13.1 %copy-start.4 = (f32[2432]{0:T(1024)S(1)}, f32[2432]{0:T(1024)}, u32[]{:S(2)}) copy-start(f32[2432]{0:T(1024)} %param.16) | copy-start | bytes 29188
  1.3 13.1 %copy-start.5 = (f32[2432]{0:T(1024)S(1)}, f32[2432]{0:T(1024)}, u32[]{:S(2)}) copy-start(f32[2432]{0:T(1024)} %param.17) | copy-start | bytes 29188
  6.8 22.6 %collective-permute-start.2 = (bf16[4,832,128]{2,1,0:T(8,128)(2,1)}, bf16[4,832,128]{2,1,0:T(8,128)(2,1)S(1)}, u32[]{:S(2)}, u32[]{:S(2)}) collective-permute-start(bf16[4,832,128]{2,1,0:T(8,128)(2,1)} %get-tuple-element.20), channel_id=1, source_target_pairs={{0,12},{1,13},{2,14},{3,15},{4,0},{5,1},{6,2},{7,3},{8,4},{9,5},{1... | collective-permute-start | bytes 2555912 | tf_op jit(solution)/shard_map/ppermute | solution.py:44
  9.7 19.7 %collective-permute-start.1 = (bf16[4,832,128]{2,1,0:T(8,128)(2,1)}, bf16[4,832,128]{2,1,0:T(8,128)(2,1)S(1)}, u32[]{:S(2)}, u32[]{:S(2)}) collective-permute-start(bf16[4,832,128]{2,1,0:T(8,128)(2,1)} %get-tuple-element.19), channel_id=1, source_target_pairs={{0,8},{1,9},{2,10},{3,11},{4,12},{5,13},{6,14},{7,15},{8,0},{9,1},... | collective-permute-start | bytes 2555912 | tf_op jit(solution)/shard_map/ppermute | solution.py:44
  10.5 22.7 %collective-permute-start = (bf16[4,832,128]{2,1,0:T(8,128)(2,1)}, bf16[4,832,128]{2,1,0:T(8,128)(2,1)S(1)}, u32[]{:S(2)}, u32[]{:S(2)}) collective-permute-start(bf16[4,832,128]{2,1,0:T(8,128)(2,1)} %get-tuple-element.18), channel_id=1, source_target_pairs={{0,4},{1,5},{2,6},{3,7},{4,8},{5,9},{6,10},{7,11},{8,12},{9,13},{1... | collective-permute-start | bytes 2555912 | tf_op jit(solution)/shard_map/ppermute | solution.py:44
  33.3 10.6 %collective-permute-start.3 = (bf16[4,448,128]{2,1,0:T(8,128)(2,1)S(1)}, bf16[4,448,128]{2,1,0:T(8,128)(2,1)S(1)}, u32[]{:S(2)}, u32[]{:S(2)}) collective-permute-start(bf16[4,448,128]{2,1,0:T(8,128)(2,1)S(1)} %pad_maximum_fusion.1), channel_id=1, source_target_pairs={{0,1},{1,2},{2,3},{3,0},{4,5},{5,6},{6,7},{7,4},{8,9},{9,10},{10,1... | collective-permute-start | bytes 1376264 | tf_op jit(solution)/shard_map/ppermute | solution.py:44
  35.3 15.0 %collective-permute-start.4 = (bf16[4,448,128]{2,1,0:T(8,128)(2,1)S(1)}, bf16[4,448,128]{2,1,0:T(8,128)(2,1)S(1)}, u32[]{:S(2)}, u32[]{:S(2)}) collective-permute-start(bf16[4,448,128]{2,1,0:T(8,128)(2,1)S(1)} %pad_maximum_fusion.2), channel_id=1, source_target_pairs={{0,2},{1,3},{2,0},{3,1},{4,6},{5,7},{6,4},{7,5},{8,10},{9,11},{10,... | collective-permute-start | bytes 1376264 | tf_op jit(solution)/shard_map/ppermute | solution.py:44
  39.1 11.3 %collective-permute-start.5 = (bf16[4,448,128]{2,1,0:T(8,128)(2,1)S(1)}, bf16[4,448,128]{2,1,0:T(8,128)(2,1)S(1)}, u32[]{:S(2)}, u32[]{:S(2)}) collective-permute-start(bf16[4,448,128]{2,1,0:T(8,128)(2,1)S(1)} %pad_maximum_fusion.3), channel_id=1, source_target_pairs={{0,3},{1,0},{2,1},{3,2},{4,7},{5,4},{6,5},{7,6},{8,11},{9,8},{10,9... | collective-permute-start | bytes 1376264 | tf_op jit(solution)/shard_map/ppermute | solution.py:44
  40.3 21.3 %collective-permute-start.6 = (bf16[4,384,128]{2,1,0:T(8,128)(2,1)S(1)}, bf16[4,384,128]{2,1,0:T(8,128)(2,1)S(1)}, u32[]{:S(2)}, u32[]{:S(2)}) collective-permute-start(bf16[4,384,128]{2,1,0:T(8,128)(2,1)S(1)} %pad_maximum_fusion.5), channel_id=1, source_target_pairs={{0,1},{1,2},{2,3},{3,0},{4,5},{5,6},{6,7},{7,4},{8,9},{9,10},{10,1... | collective-permute-start | bytes 1179656 | tf_op jit(solution)/shard_map/ppermute | solution.py:44
  41.5 20.1 %collective-permute-start.7 = (bf16[4,384,128]{2,1,0:T(8,128)(2,1)S(1)}, bf16[4,384,128]{2,1,0:T(8,128)(2,1)S(1)}, u32[]{:S(2)}, u32[]{:S(2)}) collective-permute-start(bf16[4,384,128]{2,1,0:T(8,128)(2,1)S(1)} %pad_maximum_fusion.6), channel_id=1, source_target_pairs={{0,2},{1,3},{2,0},{3,1},{4,6},{5,7},{6,4},{7,5},{8,10},{9,11},{10,... | collective-permute-start | bytes 1179656 | tf_op jit(solution)/shard_map/ppermute | solution.py:44
  42.0 8.4 %copy-start.2 = (s32[5]{0:T(128)S(1)}, s32[5]{0:T(128)}, u32[]{:S(2)}) copy-start(s32[5]{0:T(128)} %stack.56.place_ref) | copy-start | bytes 64
  43.9 17.7 %collective-permute-start.8 = (bf16[4,384,128]{2,1,0:T(8,128)(2,1)S(1)}, bf16[4,384,128]{2,1,0:T(8,128)(2,1)S(1)}, u32[]{:S(2)}, u32[]{:S(2)}) collective-permute-start(bf16[4,384,128]{2,1,0:T(8,128)(2,1)S(1)} %pad_maximum_fusion.7), channel_id=1, source_target_pairs={{0,3},{1,0},{2,1},{3,2},{4,7},{5,4},{6,5},{7,6},{8,11},{9,8},{10,9... | collective-permute-start | bytes 1179656 | tf_op jit(solution)/shard_map/ppermute | solution.py:44
  50.4 51.8 %slice-start = ((s8[9961472]{0:T(1024)(128)(4,1)}), s8[4194304]{0:T(1024)(128)(4,1)S(1)}, s32[]{:S(2)}) async-start(s8[9961472]{0:T(1024)(128)(4,1)} %bitcast.25), calls=%async_computation.2 | async-start | bytes 8388608
  50.4 51.8 %slice-start.1 = ((s8[9961472]{0:T(1024)(128)(4,1)}), s8[4194304]{0:T(1024)(128)(4,1)S(1)}, s32[]{:S(2)}) async-start(s8[9961472]{0:T(1024)(128)(4,1)} %bitcast.25), calls=%async_computation.3 | async-start | bytes 8388608
  61.5 40.7 %slice-start.2 = ((s8[9961472]{0:T(1024)(128)(4,1)}), s8[1572864]{0:T(1024)(128)(4,1)S(1)}, s32[]{:S(2)}) async-start(s8[9961472]{0:T(1024)(128)(4,1)} %bitcast.25), calls=%async_computation.4 | async-start | bytes 3145728
  82.9 19.3 %copy-start = (bf16[1,256,2432]{2,1,0:T(8,128)(2,1)S(1)}, bf16[1,256,2432]{2,1,0:T(8,128)(2,1)}, u32[]{:S(2)}) copy-start(bf16[1,256,2432]{2,1,0:T(8,128)(2,1)} %param.13) | copy-start | bytes 3735556
  82.9 19.3 %copy-start.1 = (bf16[2432,64]{0,1:T(8,128)(2,1)S(1)}, bf16[2432,64]{0,1:T(8,128)(2,1)}, u32[]{:S(2)}) copy-start(bf16[2432,64]{0,1:T(8,128)(2,1)} %param.15) | copy-start | bytes 933892
  102.2 16.6 %copy-start.3 = (f32[256,64]{0,1:T(8,128)S(1)}, f32[256,64]{0,1:T(8,128)}, u32[]{:S(2)}) copy-start(f32[256,64]{0,1:T(8,128)} %param.18) | copy-start | bytes 196612
  107.3 1.3 %collective-permute-start.9 = (f32[64,256]{1,0:T(8,128)S(1)}, f32[64,256]{1,0:T(8,128)S(1)}, u32[]{:S(2)}, u32[]{:S(2)}) collective-permute-start(f32[64,256]{1,0:T(8,128)S(1)} %get-tuple-element.29), channel_id=1, source_target_pairs={{0,16},{16,0},{32,48},{48,32},{64,80},{80,64},{96,112},{112,96},{1... | collective-permute-start | bytes 196616 | tf_op jit(solution)/shard_map/ppermute | solution.py:325
